TPU v7x, 128 devices: a whole 4x4x4 slice. The times are simulated.
128 devices in a mesh: row: 8 (over z, core), col: 16 (over x, y).
Axes of the slice: x: 4, y: 4, z: 4, core: 2. Of those that a mesh axis runs over, the one named last changes fastest.
Arguments:
- node_codes: bfloat16 [262144, 768], P(('row', 'col')), may hold values from -127 to 127
- node_scales: bfloat16 [262144], P(('row', 'col')), may hold values from 0.0049743652 to 0.049804688
- target_rows: int32 [131072], P(('row', 'col')), may hold values from 0 to 2047
- owners: int32 [16384, 1], P(('row', 'col')), may hold values from 0 to 127; in each aligned block of 128 rows (0 to 127, 128 to 255, ...) at most 2 rows name the same one
- local_blocks: int32 [16384], P(('row', 'col')), may hold values from 0 to 63
- neighbours: int32 [131072, 10], P(('row', 'col')), may hold values from 0 to 4095
- weight_self: bfloat16 [768, 1024], replicated, may hold values from -0.21875 to 0.21875
- weight_neigh: bfloat16 [768, 1024], replicated, may hold values from -0.21875 to 0.21875
- bias: float32 [1024], replicated, may hold values from -3 to 3
- cotangent: bfloat16 [131072, 1024], P(('row', 'col')), may hold values from -0.016479492 to 0.016479492
Outputs:
- hidden: bfloat16 [131072, 1024], P(('row', 'col'))
- grad_self: float32 [768, 1024], replicated
- grad_neigh: float32 [768, 1024], replicated
- grad_bias: float32 [1024], replicated
Inputs may be any that keep to these rules, and one draw needn't show every extreme that they name: `owners`: among the 128 requests of one device, at most 2 name the same owner, and some device's requests name one owner exactly 2 times.
All inputs are finite; a program needn't handle non-finite values.
Results may differ from a plain program's by a relative error of at most 0.013.
Values may be sent and summed in bfloat16 or wider, within the bound.
No kernel may reach another device: no remote copies, remote signals or barrier semaphores. Data moves between devices by JAX's collectives and lax.ppermute only.
A program may use at most 128 MiB of HBM per device.

v0:
```python
import jax
import jax.numpy as jnp
from jax import lax
from jax.sharding import PartitionSpec as P

BR = 32
K = 10
CAP = 2


def gelu_value(pre):
    inner = 0.7978845608 * (pre + 0.044715 * pre * pre * pre)
    return 0.5 * pre * (1.0 + jnp.tanh(inner))


def gelu_slope(pre):
    inner = 0.7978845608 * (pre + 0.044715 * pre * pre * pre)
    tangent = jnp.tanh(inner)
    return 0.5 * (1.0 + tangent) + 0.5 * pre * (1.0 - tangent * tangent) * 0.7978845608 * (
        1.0 + 3.0 * 0.044715 * pre * pre
    )


def select_rows(indices, count, source):
    columns = jnp.arange(count, dtype=jnp.int32)
    picker = (indices[:, None] == columns[None, :]).astype(jnp.bfloat16)
    return jnp.dot(picker, source, preferred_element_type=jnp.float32).astype(jnp.bfloat16)


def local(
    node_codes,
    node_scales,
    target_rows,
    owners,
    local_blocks,
    neighbours,
    weight_self,
    weight_neigh,
    bias,
    cotangent,
):
    row_count = lax.axis_size("row")
    col_count = lax.axis_size("col")
    devices = row_count * col_count
    width = node_codes.shape[1]
    owned_nodes = node_codes.shape[0]
    block_count = owned_nodes // BR
    first_owner = owners[:, 0]
    requests = first_owner.shape[0]
    order = jnp.arange(requests, dtype=jnp.int32)
    earlier = (first_owner[:, None] == first_owner[None, :]) & (order[None, :] < order[:, None])
    ranking = jnp.sum(earlier.astype(jnp.int32), axis=1)
    slots = first_owner * CAP + ranking
    table = jnp.zeros((devices * CAP,), jnp.int32).at[slots].set(local_blocks)
    asked = lax.all_to_all(table, ("row", "col"), split_axis=0, concat_axis=0, tiled=True)
    code_blocks = node_codes.reshape(block_count, BR * width)
    scale_blocks = node_scales.reshape(block_count, BR)
    send_codes = select_rows(asked, block_count, code_blocks).reshape(devices * CAP, BR, width)
    send_scales = select_rows(asked, block_count, scale_blocks)
    got_codes, got_scales = (
        lax.all_to_all(send_codes, ("row", "col"), split_axis=0, concat_axis=0, tiled=True),
        lax.all_to_all(send_scales, ("row", "col"), split_axis=0, concat_axis=0, tiled=True),
    )
    slot_count = devices * CAP
    pool_codes = select_rows(slots, slot_count, got_codes.reshape(slot_count, BR * width)).reshape(
        -1, width
    )
    pool_scales = select_rows(slots, slot_count, got_scales).reshape(-1)
    pool_value = pool_codes.astype(jnp.float32) * pool_scales.astype(jnp.float32)[:, None]
    value_high = pool_value.astype(jnp.bfloat16)
    value_low = (pool_value - value_high.astype(jnp.float32)).astype(jnp.bfloat16)
    self_codes = select_rows(target_rows, owned_nodes, node_codes)
    self_scales = select_rows(target_rows, owned_nodes, node_scales[:, None])
    x_self = (self_codes.astype(jnp.float32) * self_scales.astype(jnp.float32)).astype(jnp.bfloat16)
    pool_rows = pool_value.shape[0]
    column_ids = jnp.arange(pool_rows, dtype=jnp.int32)
    tally = jnp.zeros((target_rows.shape[0], pool_rows), jnp.float32)
    for step in range(K):
        tally = tally + (neighbours[:, step][:, None] == column_ids[None, :]).astype(jnp.float32)
    tally_half = tally.astype(jnp.bfloat16)
    total = jnp.dot(tally_half, value_high, preferred_element_type=jnp.float32) + jnp.dot(
        tally_half, value_low, preferred_element_type=jnp.float32
    )
    neigh_mean = (total / K).astype(jnp.bfloat16)
    pre = (
        jnp.dot(x_self, weight_self, preferred_element_type=jnp.float32)
        + jnp.dot(neigh_mean, weight_neigh, preferred_element_type=jnp.float32)
        + bias
    )
    hidden = gelu_value(pre).astype(jnp.bfloat16)
    delta = (cotangent.astype(jnp.float32) * gelu_slope(pre)).astype(jnp.bfloat16)
    term_self = lax.dot_general(
        x_self, delta, (((0,), (0,)), ((), ())), preferred_element_type=jnp.float32
    )
    term_neigh = lax.dot_general(
        neigh_mean, delta, (((0,), (0,)), ((), ())), preferred_element_type=jnp.float32
    )
    term_bias = jnp.sum(delta.astype(jnp.float32), axis=0)
    grad_self, grad_neigh, grad_bias = lax.psum((term_self, term_neigh, term_bias), ("row", "col"))
    return (hidden, grad_self, grad_neigh, grad_bias)


def solution(mesh):
    placed = (
        P(("row", "col"), None),
        P(("row", "col")),
        P(("row", "col")),
        P(("row", "col"), None),
        P(("row", "col")),
        P(("row", "col"), None),
        P(),
        P(),
        P(),
        P(("row", "col"), None),
    )
    return jax.shard_map(
        local,
        mesh=mesh,
        in_specs=placed,
        out_specs=(P(("row", "col"), None), P(), P(), P()),
        check_vma=False,
    )
```

profile of v0, /device:TPU:1, one launch (start us, length us, event | category | flops | bytes accessed | tf_op | source)
XLA Modules:
  0.0 517.6 jit_solution(15410714516528327008)
XLA Ops:
  10.7 11.5 %all-to-all-start = ((s32[128,2,1]{1,2,0:T(1,128)}), s32[128,2,1]{1,2,0:T(1,128)S(1)}, u32[]{:S(2)}, u32[]{:S(2)}) async-start(s32[128,2,1]{1,2,0:T(1,128)} %bitcast.15), calls=%async_computation | async-start | bytes 131072 | tf_op jit(solution)/shard_map/all_to_all | solution.py:55
  22.2 4.8 reshape.48
  27.1 4.6 all-to-all-done
  34.2 5.2 all-to-all-start.2
  39.3 5.6 %convolution_convert_fusion = bf16[256,24576]{1,0:T(8,128)(2,1)S(1)} fusion(bf16[64,24576]{1,0:T(8,128)(2,1)} %reshape.48, s32[256]{0:T(256)S(1)} %eq.280), kind=kOutput, calls=%fused_computation.1 | convolution fusion | flops 811614208 | bytes 15729664 | tf_op jit(solution)/shard_map/dot_general | solution.py:27
  44.9 6.9 %copy.22 = bf16[32,8,32,768]{3,2,1,0:T(8,128)(2,1)} copy(bf16[32,8,32,768]{3,1,2,0:T(8,128)(2,1)S(1)} %bitcast.48) | data formatting | bytes 25165824
  51.9 10.2 %all-to-all-start.1 = ((bf16[256,32,768]{2,1,0:T(8,128)(2,1)}), bf16[256,32,768]{2,1,0:T(8,128)(2,1)}, u32[]{:S(2)}, u32[]{:S(2)}) async-start(bf16[256,32,768]{2,1,0:T(8,128)(2,1)} %bitcast.47), calls=%async_computation.1 | async-start | bytes 25165824 | tf_op jit(solution)/shard_map/all_to_all | solution.py:61
  64.0 5.7 %multiply_convert_fusion.4 = bf16[1024,768]{1,0:T(8,128)(2,1)S(1)} fusion(f32[1024]{0:T(1024)S(1)} %convert_convert_fusion, bf16[2048,768]{1,0:T(8,128)(2,1)} %param.10, s32[1024]{0:T(1024)S(1)} %copy-done.7), kind=kOutput, calls=%fused_computation.39 | convolution fusion | flops 3226468352 | bytes 4726784 | tf_op jit(solution)/shard_map/dot_general | solution.py:27
  69.7 3.8 fusion.29
  73.9 159.0 %all-to-all-done.1 = bf16[256,32,768]{2,1,0:T(8,128)(2,1)} async-done(((bf16[256,32,768]{2,1,0:T(8,128)(2,1)}), bf16[256,32,768]{2,1,0:T(8,128)(2,1)}, u32[]{:S(2)}, u32[]{:S(2)}) %all-to-all-start.1) | async-done | bytes 12582944 | tf_op jit(solution)/shard_map/all_to_all | solution.py:61
  232.9 12.2 %copy.23 = bf16[32,8,32,768]{3,1,2,0:T(8,128)(2,1)S(1)} copy(bf16[32,8,32,768]{3,2,1,0:T(8,128)(2,1)} %bitcast.20) | data formatting | bytes 25165824
  245.1 6.4 %fusion = f32[128,24576]{1,0:T(8,128)} fusion(bf16[256,24576]{1,0:T(8,128)(2,1)S(1)} %bitcast.46, s32[128]{0:T(128)S(1)} %get-tuple-element.19), kind=kOutput, calls=%fused_computation.3 | convolution fusion | flops 1616936960 | bytes 25166336 | tf_op jit(solution)/shard_map/dot_general | solution.py:27
  251.5 11.8 %reshape.52 = f32[4096,768]{1,0:T(8,128)} reshape(f32[128,24576]{1,0:T(8,128)} %fusion) | data formatting | bytes 25165824 | tf_op jit(solution)/shard_map/convert_element_type | solution.py:69
  263.3 6.7 %multiply_convert_fusion.8 = bf16[4096,768]{1,0:T(8,128)(2,1)S(1)} fusion(f32[4096,768]{1,0:T(8,128)} %reshape.52, f32[4096]{0:T(1024)S(1)} %reshape.53), kind=kLoop, calls=%fused_computation.16.clone.1.clone.2 | loop fusion | flops 6291456 | bytes 18890752 | tf_op jit(solution)/shard_map/dot_general | solution.py:81
  271.6 2.1 subtract_convert_fusion.7
  273.7 26.2 %fusion.1 = f32[1024,768]{1,0:T(8,128)S(1)} fusion(s32[1024]{0:T(1024)S(1)} %bitcast.66, s32[1024]{0:T(1024)S(1)} %bitcast.68, s32[1024]{0:T(1024)S(1)} %bitcast.52, s32[1024]{0:T(1024)S(1)} %bitcast.54, s32[1024]{0:T(1024)S(1)} %bitcast.56, s32[1024]{0:T(1024)S(1)} %bitcast.58, s32[1024]{0:T(1024)S(1)} %bitcast.60, s32[1024]{0:T(1024)S(1)} %bitcast.62, ...), kind=kOutput, calls=%fused_computation.17 | convolution fusion | flops 6568280064 | bytes 9478144 | tf_op jit(solution)/shard_map/dot_general | solution.py:81
  299.9 26.6 %multiply_convert_fusion.3 = bf16[1024,768]{1,0:T(8,128)(2,1)S(1)} fusion(f32[1024,768]{1,0:T(8,128)S(1)} %fusion.1, s32[1024]{0:T(1024)S(1)} %bitcast.67, s32[1024]{0:T(1024)S(1)} %bitcast.69, s32[1024]{0:T(1024)S(1)} %bitcast.53, s32[1024]{0:T(1024)S(1)} %bitcast.55, s32[1024]{0:T(1024)S(1)} %bitcast.57, s32[1024]{0:T(1024)S(1)} %bitcast.59, ...), kind=kOutput, calls=%fused_computation.38 | convolution fusion | flops 6570639360 | bytes 11051008 | tf_op jit(solution)/shard_map/dot_general | solution.py:81
  326.6 6.1 %convert_reduce_fusion = (f32[1024]{0:T(1024)S(1)}, bf16[1024,1024]{1,0:T(8,128)(2,1)S(1)}, bf16[1024,1024]{1,0:T(8,128)(2,1)}) fusion(bf16[1024,1024]{1,0:T(8,128)(2,1)S(1)} %copy-done.5, f32[1024]{0:T(1024)S(1)} %copy-done.8, f32[1024,1024]{1,0:T(8,128)S(1)} %copy-done.9, bf16[1024,768]{1,0:T(8,128)(2,1)S(1)} %multiply_convert_fusion.3, ...), kind=kOutput, calls=%fused_computation.33 | convolution fusion | flops 1637874688 | bytes 13639680 | tf_op jit(solution)/shard_map/dot_general | solution.py:87
  332.6 3.5 fusion.31
  336.1 3.5 fusion.30
  339.7 72.4 %psum.23 = f32[1024]{0:T(1024)} all-reduce(f32[1024]{0:T(1024)S(1)} %get-tuple-element.6), channel_id=1, replica_groups=mesh['row'=8,'col'=16] {'row','col'}, use_global_device_ids=true, to_apply=%region_5.0 | all-reduce | flops 1024 | bytes 8192 | tf_op jit(solution)/shard_map/psum | solution.py:99
  412.1 92.7 %all-reduce.3.cloned.1.call-done = (f32[768,1024]{1,0:T(8,128)}, f32[768,1024]{1,0:T(8,128)}) async-done(((f32[768,1024]{1,0:T(8,128)}, f32[768,1024]{1,0:T(8,128)}), (f32[768,1024]{1,0:T(8,128)}, f32[768,1024]{1,0:T(8,128)})) %all-reduce.3.cloned.1.call-update) | async-done | bytes 6291472 | tf_op jit(solution)/shard_map/psum | solution.py:99
  504.8 4.1 copy.26
  508.9 1.7 copy.27
  (40 shorter events, 9.9 us)
Async XLA Ops:
  7.2 319.4 %copy-start = (bf16[768,1024]{1,0:T(8,128)(2,1)S(1)}, bf16[768,1024]{1,0:T(8,128)(2,1)}, u32[]{:S(2)}) copy-start(bf16[768,1024]{1,0:T(8,128)(2,1)} %param.17) | copy-start | bytes 4718596
  7.2 19.8 %copy-start.4 = (bf16[2048]{0:T(1024)(128)(2,1)S(1)}, bf16[2048]{0:T(1024)(128)(2,1)}, u32[]{:S(2)}) copy-start(bf16[2048]{0:T(1024)(128)(2,1)} %param.11) | copy-start | bytes 12292
  10.7 21.0 %all-to-all-start = ((s32[128,2,1]{1,2,0:T(1,128)}), s32[128,2,1]{1,2,0:T(1,128)S(1)}, u32[]{:S(2)}, u32[]{:S(2)}) async-start(s32[128,2,1]{1,2,0:T(1,128)} %bitcast.15), calls=%async_computation | async-start | bytes 131072 | tf_op jit(solution)/shard_map/all_to_all | solution.py:55
  34.2 17.7 %all-to-all-start.2 = ((bf16[128,2,32]{2,1,0:T(2,128)(2,1)}), bf16[128,2,32]{2,1,0:T(2,128)(2,1)S(1)}, u32[]{:S(2)}, u32[]{:S(2)}) async-start(bf16[128,2,32]{2,1,0:T(2,128)(2,1)} %bitcast.16), calls=%async_computation.2 | async-start | bytes 131072 | tf_op jit(solution)/shard_map/all_to_all | solution.py:62
  51.8 10.4 %copy-start.7 = (s32[1024]{0:T(1024)S(1)}, s32[1024]{0:T(1024)}, u32[]{:S(2)}) copy-start(s32[1024]{0:T(1024)} %param.12) | copy-start | bytes 12292
  51.9 12.1 %copy-start.3 = (s32[1024,10]{0,1:T(8,128)S(1)}, s32[1024,10]{0,1:T(8,128)}, u32[]{:S(2)}) copy-start(s32[1024,10]{0,1:T(8,128)} %param.15) | copy-start | bytes 122884
  51.9 181.1 %all-to-all-start.1 = ((bf16[256,32,768]{2,1,0:T(8,128)(2,1)}), bf16[256,32,768]{2,1,0:T(8,128)(2,1)}, u32[]{:S(2)}, u32[]{:S(2)}) async-start(bf16[256,32,768]{2,1,0:T(8,128)(2,1)} %bitcast.47), calls=%async_computation.1 | async-start | bytes 25165824 | tf_op jit(solution)/shard_map/all_to_all | solution.py:61
  62.0 442.7 %all-reduce.3.cloned.1.call-start = ((), (), s32[]{:S(2)}) async-start(), calls=%async_computation.3 | async-start | bytes 12582912 | tf_op jit(solution)/shard_map/psum | solution.py:99
  63.9 5.8 %copy-start.6 = (bf16[768,1024]{1,0:T(8,128)(2,1)S(1)}, bf16[768,1024]{1,0:T(8,128)(2,1)}, u32[]{:S(2)}) copy-start(bf16[768,1024]{1,0:T(8,128)(2,1)} %param.16) | copy-start | bytes 4718596
  263.3 8.3 %copy-start.1 = (f32[4096,768]{1,0:T(8,128)S(1)}, f32[4096,768]{1,0:T(8,128)}, u32[]{:S(2)}) copy-start(f32[4096,768]{1,0:T(8,128)} %reshape.52) | copy-start | bytes 37748740
  299.9 26.6 %copy-start.5 = (bf16[1024,1024]{1,0:T(8,128)(2,1)S(1)}, bf16[1024,1024]{1,0:T(8,128)(2,1)}, u32[]{:S(2)}) copy-start(bf16[1024,1024]{1,0:T(8,128)(2,1)} %param.19) | copy-start | bytes 6291460
  299.9 26.6 %copy-start.8 = (f32[1024]{0:T(1024)S(1)}, f32[1024]{0:T(1024)}, u32[]{:S(2)}) copy-start(f32[1024]{0:T(1024)} %param.18) | copy-start | bytes 12292
  299.9 26.6 %copy-start.9 = (f32[1024,1024]{1,0:T(8,128)S(1)}, f32[1024,1024]{1,0:T(8,128)}, u32[]{:S(2)}) copy-start(f32[1024,1024]{1,0:T(8,128)} %fusion.29) | copy-start | bytes 12582916
  504.8 4.1 copy-start.2
Sparse Core Ops, SparseCore 0:
  339.8 164.9 all-reduce.2
where the time goes:
time: 523 us; the launch traced here: 518 us
  waiting for transfers between devices  256 us (49%)
  matrix products  89.4 us (17%)
  blocking collectives  72.4 us (14%)
  local copies, waits for them, and re-layouts  46.7 us (9%)
  starting transfers between devices  27 us (5%)
  between operations  14.5 us (3%)
  other arithmetic  11.3 us (2%)
    all_to_all x1, waiting for transfers between devices, local(): lax.all_to_all(send_codes, ('row', 'col'), split_axis=0, concat_axis=0, t...  159 us
    psum x1, waiting for transfers between devices, local(): lax.psum((term_self, term_neigh, term_bias), ('row', 'col'))  92.7 us
    psum x1, blocking collectives, local(): lax.psum((term_self, term_neigh, term_bias), ('row', 'col'))  72.4 us
    dot_general x1, matrix products, local(): jnp.dot(tally_half, value_low, preferred_element_type=jnp.float32)  26.6 us
    unnamed x25, local copies, waits for them, and re-layouts  26.5 us
    dot_general x1, matrix products, local(): jnp.dot(tally_half, value_high, preferred_element_type=jnp.float32)  26.2 us
    dot_general x6, matrix products, select_rows(): jnp.dot(picker, source, preferred_element_type=jnp.float32)  19.8 us
    convert_element_type x1, local copies, waits for them, and re-layouts, local(): pool_codes.astype(jnp.float32) * pool_scales.astype(jnp.float32)[:, None]  11.8 us
  transfers between devices with their start and end apart: 4, of which 3 were waited for; matrix products, arithmetic and copies ran while one was open for 6% of the time, Pallas kernels for 0%

commit v1 on v0

v1 whole, which is shorter than its diff:
```python
import jax
import jax.numpy as jnp
from jax import lax
from jax.sharding import Mesh, PartitionSpec as P

BR = 32
K = 10
CAP = 2


def gelu_value(pre):
    inner = 0.7978845608 * (pre + 0.044715 * pre * pre * pre)
    return 0.5 * pre * (1.0 + jnp.tanh(inner))


def gelu_slope(pre):
    inner = 0.7978845608 * (pre + 0.044715 * pre * pre * pre)
    tangent = jnp.tanh(inner)
    return 0.5 * (1.0 + tangent) + 0.5 * pre * (1.0 - tangent * tangent) * 0.7978845608 * (
        1.0 + 3.0 * 0.044715 * pre * pre
    )


def select_rows(indices, count, source):
    columns = jnp.arange(count, dtype=jnp.int32)
    picker = (indices[:, None] == columns[None, :]).astype(jnp.bfloat16)
    return jnp.dot(picker, source, preferred_element_type=jnp.float32).astype(jnp.bfloat16)


ALL = ("z", "core", "x", "y")
CHIPS = ("z", "x", "y")
SWAP = [(0, 1), (1, 0)]


def exchange(array, axes):
    return lax.all_to_all(array, axes, split_axis=0, concat_axis=0, tiled=True)


def pack(term, bias_term):
    rows = term.reshape(8, 96, 8, 128).transpose(0, 2, 1, 3)
    tail = jnp.zeros((8, 8, 16, 128), jnp.float32).at[:, :, 0, :].set(bias_term.reshape(8, 128))
    return jnp.concatenate([rows, tail], axis=2).astype(jnp.bfloat16).reshape(64, 112, 128)


def unpack(chunks):
    rows = chunks.reshape(8, 8, 112, 128)
    grad = rows[:, :, :96, :].transpose(0, 2, 1, 3).reshape(768, 1024).astype(jnp.float32)
    return grad, rows[0, :, 96, :].reshape(1024).astype(jnp.float32)


def sum_over_devices(term_self, term_neigh, term_bias):
    first = lax.axis_index("core") == 0
    packed_self, packed_neigh = pack(term_self, term_bias), pack(term_neigh, term_bias)
    kept = jnp.where(first, packed_self, packed_neigh)
    given = jnp.where(first, packed_neigh, packed_self)
    received = lax.ppermute(given, "core", SWAP)
    chip = (kept.astype(jnp.float32) + received.astype(jnp.float32)).astype(jnp.bfloat16)
    parts = exchange(chip, CHIPS)
    mine = jnp.sum(parts.astype(jnp.float32), axis=0).astype(jnp.bfloat16)
    full = exchange(jnp.broadcast_to(mine[None], (64, 112, 128)), CHIPS)
    theirs = lax.ppermute(full, "core", SWAP)
    grad_self, grad_bias = unpack(jnp.where(first, full, theirs))
    grad_neigh, _ = unpack(jnp.where(first, theirs, full))
    return grad_self, grad_neigh, grad_bias


def local(
    node_codes,
    node_scales,
    target_rows,
    owners,
    local_blocks,
    neighbours,
    weight_self,
    weight_neigh,
    bias,
    cotangent,
):
    devices = lax.axis_size("z") * lax.axis_size("core") * lax.axis_size("x") * lax.axis_size("y")
    width = node_codes.shape[1]
    owned_nodes = node_codes.shape[0]
    block_count = owned_nodes // BR
    first_owner = owners[:, 0]
    requests = first_owner.shape[0]
    order = jnp.arange(requests, dtype=jnp.int32)
    earlier = (first_owner[:, None] == first_owner[None, :]) & (order[None, :] < order[:, None])
    ranking = jnp.sum(earlier.astype(jnp.int32), axis=1)
    slots = first_owner * CAP + ranking
    table = jnp.zeros((devices * CAP,), jnp.int32).at[slots].set(local_blocks)
    asked = exchange(table, ALL)
    values = (
        node_codes.astype(jnp.float32) * node_scales.astype(jnp.float32)[:, None]
    ).astype(jnp.bfloat16)
    blocks = values.reshape(block_count, BR * width)
    send = select_rows(asked, block_count, blocks).reshape(devices * CAP, BR, width)
    got = exchange(send, ALL)
    slot_count = devices * CAP
    pool = select_rows(slots, slot_count, got.reshape(slot_count, BR * width)).reshape(-1, width)
    x_self = select_rows(target_rows, owned_nodes, values)
    pool_rows = pool.shape[0]
    column_ids = jnp.arange(pool_rows, dtype=jnp.int32)
    tally = jnp.zeros((target_rows.shape[0], pool_rows), jnp.float32)
    for step in range(K):
        tally = tally + (neighbours[:, step][:, None] == column_ids[None, :]).astype(jnp.float32)
    tally_half = tally.astype(jnp.bfloat16)
    total = jnp.dot(tally_half, pool, preferred_element_type=jnp.float32)
    neigh_mean = (total / K).astype(jnp.bfloat16)
    pre = (
        jnp.dot(x_self, weight_self, preferred_element_type=jnp.float32)
        + jnp.dot(neigh_mean, weight_neigh, preferred_element_type=jnp.float32)
        + bias
    )
    hidden = gelu_value(pre).astype(jnp.bfloat16)
    delta = (cotangent.astype(jnp.float32) * gelu_slope(pre)).astype(jnp.bfloat16)
    term_self = lax.dot_general(
        x_self, delta, (((0,), (0,)), ((), ())), preferred_element_type=jnp.float32
    )
    term_neigh = lax.dot_general(
        neigh_mean, delta, (((0,), (0,)), ((), ())), preferred_element_type=jnp.float32
    )
    term_bias = jnp.sum(delta.astype(jnp.float32), axis=0)
    grad_self, grad_neigh, grad_bias = sum_over_devices(
        term_self, term_neigh, term_bias
    )
    return (hidden, grad_self, grad_neigh, grad_bias)


def solution(mesh):
    fine = Mesh(mesh.devices.reshape(4, 2, 4, 4), ALL)
    placed = (
        P(ALL, None),
        P(ALL),
        P(ALL),
        P(ALL, None),
        P(ALL),
        P(ALL, None),
        P(),
        P(),
        P(),
        P(ALL, None),
    )
    return jax.shard_map(
        local,
        mesh=fine,
        in_specs=placed,
        out_specs=(P(ALL, None), P(), P(), P()),
        check_vma=False,
    )
```

time: 523 us -> 379 us (0.72)
  waiting for transfers between devices: 256 us -> 166 us
  matrix products: 89.4 us -> 58.3 us
  between operations: 14.5 us -> 1.12 us
  blocking collectives: 72.4 us -> 65.1 us
    psum x1 -> x0, waiting for transfers between devices: 92.7 us -> none  [local(): lax.psum((term_self, term_neigh, term_bias), ('row', 'col'))]
    psum x1 -> x0, blocking collectives: 72.4 us -> none  [local(): lax.psum((term_self, term_neigh, term_bias), ('row', 'col'))]
    all_to_all x0 -> x2, blocking collectives: none -> 65.1 us  [exchange(): return lax.all_to_all(array, axes, split_axis=0, concat_axis=0, tiled=True)]
    dot_general x2 -> x1, matrix products: 52.8 us -> 29.2 us  [local(): total = jnp.dot(tally_half, pool, preferred_element_type=jnp.float32)]
    reshape x2 -> x4, local copies, waits for them, and re-layouts: 4.89 us -> 14.5 us  [the longest x1 9.09 us: local(): select_rows(slots, slot_count, got.reshape(slot_count, BR * width))]
    dot_general x2 -> x0, other arithmetic: 8.82 us -> none  [the longest x1 6.74 us: local(): jnp.dot(tally_half, value_high, preferred_element_type=jnp.float32)]
    convert_element_type x1 -> x6, other arithmetic: 0.01 us -> 6.89 us  [the longest x1 4.13 us: local(): values = (node_codes.astype(jnp.float32) * node_scales.astype(jnp.float32...]
    ppermute x0 -> x2, waiting for transfers between devices: none -> 6.82 us  [the longest x1 3.41 us: sum_over_devices(): received = lax.ppermute(given, 'core', SWAP)]
  transfers between devices with their start and end apart: 4 -> 4, of which waited for: 3 -> 3; matrix products, arithmetic and copies ran while one was open for 6% -> 5% of each run, Pallas kernels for 0% -> 0%
where the time goes in v1:
time: 379 us; the launch traced here: 374 us
  waiting for transfers between devices  166 us (44%)
  blocking collectives  65.1 us (17%)
  matrix products  58.3 us (15%)
  local copies, waits for them, and re-layouts  45.2 us (12%)
  starting transfers between devices  28.5 us (8%)
  other arithmetic  10.2 us (3%)
    all_to_all x2, waiting for transfers between devices, exchange(): return lax.all_to_all(array, axes, split_axis=0, concat_axis=0, tiled=True)  159 us
    all_to_all x2, blocking collectives, exchange(): return lax.all_to_all(array, axes, split_axis=0, concat_axis=0, tiled=True)  65.1 us
    dot_general x1, matrix products, local(): total = jnp.dot(tally_half, pool, preferred_element_type=jnp.float32)  29.2 us
    all_to_all x2, starting transfers between devices, exchange(): return lax.all_to_all(array, axes, split_axis=0, concat_axis=0, tiled=True)  22.4 us
    unnamed x18, local copies, waits for them, and re-layouts  20 us
    dot_general x3, matrix products, select_rows(): jnp.dot(picker, source, preferred_element_type=jnp.float32)  15.8 us
    reshape x1, local copies, waits for them, and re-layouts, local(): select_rows(slots, slot_count, got.reshape(slot_count, BR * width))  9.09 us
    convert_element_type x3, local copies, waits for them, and re-layouts, unpack(): rows[:, :, :96, :].transpose(0, 2, 1, 3).reshape(768, 1024)  7.81 us
  transfers between devices with their start and end apart: 4, of which 3 were waited for; matrix products, arithmetic and copies ran while one was open for 5% of the time, Pallas kernels for 0%

profile of v1, /device:TPU:1, one launch (start us, length us, event | category | flops | bytes accessed | tf_op | source)
XLA Modules:
  0.0 374.0 jit_solution(15647682663048102318)
XLA Ops:
  4.2 11.5 %all-to-all-start = ((s32[128,2,1]{1,2,0:T(1,128)}), s32[128,2,1]{1,2,0:T(1,128)S(1)}, u32[]{:S(2)}, u32[]{:S(2)}) async-start(s32[128,2,1]{1,2,0:T(1,128)} %bitcast.14), calls=%async_computation | async-start | bytes 131072 | tf_op jit(solution)/shard_map/all_to_all | solution.py:36
  16.4 4.1 %multiply_convert_fusion = bf16[2048,768]{1,0:T(8,128)(2,1)} fusion(bf16[2048,768]{1,0:T(8,128)(2,1)} %param.14, f32[2048]{0:T(1024)S(1)} %convert_element_type.112), kind=kLoop, calls=%fused_computation.29 | loop fusion | flops 4718592 | bytes 6299648 | tf_op jit(solution)/shard_map/convert_element_type | solution.py:93
  20.5 4.8 %reshape.117 = bf16[64,24576]{1,0:T(8,128)(2,1)} reshape(bf16[2048,768]{1,0:T(8,128)(2,1)} %multiply_convert_fusion) | data formatting | bytes 6291456 | tf_op jit(solution)/shard_map/reshape | solution.py:94
  26.8 5.6 %convolution_convert_fusion = bf16[256,24576]{1,0:T(8,128)(2,1)S(1)} fusion(bf16[64,24576]{1,0:T(8,128)(2,1)} %reshape.117, s32[256]{0:T(256)S(1)} %eq.262), kind=kOutput, calls=%fused_computation.1 | convolution fusion | flops 811614208 | bytes 15729664 | tf_op jit(solution)/shard_map/dot_general | solution.py:27
  32.4 6.9 %copy.30 = bf16[32,8,32,768]{3,2,1,0:T(8,128)(2,1)} copy(bf16[32,8,32,768]{3,1,2,0:T(8,128)(2,1)S(1)} %bitcast.72) | data formatting | bytes 25165824
  39.3 10.9 %all-to-all-start.1 = ((bf16[256,32,768]{2,1,0:T(8,128)(2,1)}), bf16[256,32,768]{2,1,0:T(8,128)(2,1)}, u32[]{:S(2)}, u32[]{:S(2)}) async-start(bf16[256,32,768]{2,1,0:T(8,128)(2,1)} %bitcast.70), calls=%async_computation.1 | async-start | bytes 25165824 | tf_op jit(solution)/shard_map/all_to_all | solution.py:36
  50.2 5.7 %fusion.20 = bf16[1024,768]{1,0:T(8,128)(2,1)S(1)} fusion(bf16[2048,768]{1,0:T(8,128)(2,1)} %multiply_convert_fusion, s32[1024]{0:T(1024)S(1)} %copy-done.4), kind=kOutput, calls=%fused_computation.52 | convolution fusion | flops 3224109056 | bytes 4722688 | tf_op jit(solution)/shard_map/dot_general | solution.py:27
  56.0 3.7 %fusion.32 = f32[1024,1024]{1,0:T(8,128)} fusion(bf16[1024,768]{1,0:T(8,128)(2,1)S(1)} %fusion.20, bf16[768,1024]{1,0:T(8,128)(2,1)S(1)} %copy-done.3), kind=kOutput, calls=%fused_computation.73 | convolution fusion | flops 1610612736 | bytes 7340032 | tf_op jit(solution)/shard_map/dot_general | solution.py:109
  59.7 158.7 %all-to-all-done.1 = bf16[256,32,768]{2,1,0:T(8,128)(2,1)} async-done(((bf16[256,32,768]{2,1,0:T(8,128)(2,1)}), bf16[256,32,768]{2,1,0:T(8,128)(2,1)}, u32[]{:S(2)}, u32[]{:S(2)}) %all-to-all-start.1) | async-done | bytes 12582944 | tf_op jit(solution)/shard_map/all_to_all | solution.py:36
  218.4 12.2 %copy.31 = bf16[32,8,32,768]{3,1,2,0:T(8,128)(2,1)S(1)} copy(bf16[32,8,32,768]{3,2,1,0:T(8,128)(2,1)} %bitcast.30) | data formatting | bytes 25165824
  230.6 4.5 %convolution_convert_fusion.1 = bf16[128,24576]{1,0:T(8,128)(2,1)} fusion(bf16[256,24576]{1,0:T(8,128)(2,1)S(1)} %bitcast.71, s32[128]{0:T(128)S(1)} %get-tuple-element.39), kind=kOutput, calls=%fused_computation.2 | convolution fusion | flops 1613791232 | bytes 18874880 | tf_op jit(solution)/shard_map/dot_general | solution.py:27
  235.1 9.1 %reshape.120 = bf16[4096,768]{1,0:T(8,128)(2,1)} reshape(bf16[128,24576]{1,0:T(8,128)(2,1)} %convolution_convert_fusion.1) | data formatting | bytes 12582912 | tf_op jit(solution)/shard_map/reshape | solution.py:98
  244.3 29.2 %multiply_convert_fusion.2 = bf16[1024,768]{1,0:T(8,128)(2,1)S(1)} fusion(bf16[4096,768]{1,0:T(8,128)(2,1)} %reshape.120, s32[1024]{0:T(1024)S(1)} %bitcast.94, s32[1024]{0:T(1024)S(1)} %bitcast.95, s32[1024]{0:T(1024)S(1)} %bitcast.87, s32[1024]{0:T(1024)S(1)} %bitcast.88, s32[1024]{0:T(1024)S(1)} %bitcast.89, s32[1024]{0:T(1024)S(1)} %bitcast.90, ...), kind=kOutput, calls=%fused_computation.46 | convolution fusion | flops 6569852928 | bytes 7905280 | tf_op jit(solution)/shard_map/dot_general | solution.py:106
  273.5 5.9 %convert_reduce_fusion = (bf16[1024]{0:T(1024)(128)(2,1)S(1)}, bf16[1024,1024]{1,0:T(8,128)(2,1)S(1)}, bf16[1024,1024]{1,0:T(8,128)(2,1)}) fusion(bf16[1024,1024]{1,0:T(8,128)(2,1)S(1)} %copy-done.2, f32[1024]{0:T(1024)S(1)} %copy-done.5, f32[1024,1024]{1,0:T(8,128)S(1)} %copy-done.6, bf16[1024,768]{1,0:T(8,128)(2,1)S(1)} %multiply_convert_fusion.2, ...), kind=kOutput, calls=%fused_computation.37 | convolution fusion | flops 1637874688 | bytes 13637632 | tf_op jit(solution)/shard_map/dot_general | solution.py:110
  279.4 1.8 fusion.22
  281.2 1.8 fusion.21
  285.1 2.4 collective-permute-start
  287.5 3.4 collective-permute-done
  291.6 35.1 %all_to_all.24 = bf16[64,112,128]{2,1,0:T(8,128)(2,1)S(1)} all-to-all(bf16[64,112,128]{2,1,0:T(8,128)(2,1)S(1)} %add_convert_fusion.2), channel_id=1, replica_groups=mesh['z'=4,'core'=2,'x'=4,'y'=4] {'z','x','y'}, dimensions={0} | all-to-all | bytes 3670016 | tf_op jit(solution)/shard_map/all_to_all | solution.py:36
  327.2 30.0 %all_to_all.25 = bf16[64,112,128]{2,1,0:T(8,128)(2,1)S(1)} all-to-all(bf16[64,112,128]{2,1,0:T(8,128)(2,1)S(1)} %broadcast_in_dim.5), channel_id=1, replica_groups=mesh['z'=4,'core'=2,'x'=4,'y'=4] {'z','x','y'}, dimensions={0} | all-to-all | bytes 3670016 | tf_op jit(solution)/shard_map/all_to_all | solution.py:36
  357.2 3.7 collective-permute-start.1
  361.0 3.4 collective-permute-done.1
  367.8 1.8 copy.29
  369.6 4.2 %copy_bitcast_fusion = (f32[768,1024]{1,0:T(8,128)}, f32[768,1024]{1,0:T(8,128)}) fusion(f32[96,8,8,128]{3,2,1,0:T(8,128)S(1)} %bitcast.78, f32[96,8,8,128]{3,2,1,0:T(8,128)S(1)} %bitcast.77), kind=kLoop, calls=%fused_computation.42 | loop fusion | bytes 12582912 | tf_op jit(solution)/shard_map/convert_element_type | solution.py:47
  (39 shorter events, 12.3 us)
Async XLA Ops:
  0.6 272.8 %copy-start = (bf16[768,1024]{1,0:T(8,128)(2,1)S(1)}, bf16[768,1024]{1,0:T(8,128)(2,1)}, u32[]{:S(2)}) copy-start(bf16[768,1024]{1,0:T(8,128)(2,1)} %param.21) | copy-start | bytes 4718596
  4.2 21.1 %all-to-all-start = ((s32[128,2,1]{1,2,0:T(1,128)}), s32[128,2,1]{1,2,0:T(1,128)S(1)}, u32[]{:S(2)}, u32[]{:S(2)}) async-start(s32[128,2,1]{1,2,0:T(1,128)} %bitcast.14), calls=%async_computation | async-start | bytes 131072 | tf_op jit(solution)/shard_map/all_to_all | solution.py:36
  39.3 10.9 %copy-start.1 = (s32[1024,10]{0,1:T(8,128)S(1)}, s32[1024,10]{0,1:T(8,128)}, u32[]{:S(2)}) copy-start(s32[1024,10]{0,1:T(8,128)} %param.19) | copy-start | bytes 122884
  39.3 10.9 %copy-start.4 = (s32[1024]{0:T(1024)S(1)}, s32[1024]{0:T(1024)}, u32[]{:S(2)}) copy-start(s32[1024]{0:T(1024)} %param.16) | copy-start | bytes 12292
  39.3 179.1 %all-to-all-start.1 = ((bf16[256,32,768]{2,1,0:T(8,128)(2,1)}), bf16[256,32,768]{2,1,0:T(8,128)(2,1)}, u32[]{:S(2)}, u32[]{:S(2)}) async-start(bf16[256,32,768]{2,1,0:T(8,128)(2,1)} %bitcast.70), calls=%async_computation.1 | async-start | bytes 25165824 | tf_op jit(solution)/shard_map/all_to_all | solution.py:36
  50.2 5.7 %copy-start.3 = (bf16[768,1024]{1,0:T(8,128)(2,1)S(1)}, bf16[768,1024]{1,0:T(8,128)(2,1)}, u32[]{:S(2)}) copy-start(bf16[768,1024]{1,0:T(8,128)(2,1)} %param.20) | copy-start | bytes 4718596
  244.2 29.2 %copy-start.2 = (bf16[1024,1024]{1,0:T(8,128)(2,1)S(1)}, bf16[1024,1024]{1,0:T(8,128)(2,1)}, u32[]{:S(2)}) copy-start(bf16[1024,1024]{1,0:T(8,128)(2,1)} %param.23) | copy-start | bytes 6291460
  244.2 29.2 %copy-start.5 = (f32[1024]{0:T(1024)S(1)}, f32[1024]{0:T(1024)}, u32[]{:S(2)}) copy-start(f32[1024]{0:T(1024)} %param.22) | copy-start | bytes 12292
  244.2 29.2 %copy-start.6 = (f32[1024,1024]{1,0:T(8,128)S(1)}, f32[1024,1024]{1,0:T(8,128)}, u32[]{:S(2)}) copy-start(f32[1024,1024]{1,0:T(8,128)} %fusion.32) | copy-start | bytes 12582916
  285.1 5.8 %collective-permute-start = (bf16[64,112,128]{2,1,0:T(8,128)(2,1)S(1)}, bf16[64,112,128]{2,1,0:T(8,128)(2,1)S(1)}, u32[]{:S(2)}, u32[]{:S(2)}) collective-permute-start(bf16[64,112,128]{2,1,0:T(8,128)(2,1)S(1)} %broadcast_select_fusion.2), channel_id=1, source_target_pairs={{0,16},{16,0},{1,17},{17,1},{2,18},{18,2},{3,19},{19,3},{4,20},{20... | collective-permute-start | bytes 5505032 | tf_op jit(solution)/shard_map/ppermute | solution.py:56
  357.2 7.1 %collective-permute-start.1 = (bf16[64,112,128]{2,1,0:T(8,128)(2,1)S(1)}, bf16[64,112,128]{2,1,0:T(8,128)(2,1)S(1)}, u32[]{:S(2)}, u32[]{:S(2)}) collective-permute-start(bf16[64,112,128]{2,1,0:T(8,128)(2,1)S(1)} %all_to_all.25), channel_id=1, source_target_pairs={{0,16},{16,0},{1,17},{17,1},{2,18},{18,2},{3,19},{19,3},{4,20},{20... | collective-permute-start | bytes 5505032 | tf_op jit(solution)/shard_map/ppermute | solution.py:61

commit v2 on v1

v2 whole, which is shorter than its diff:
```python
import jax
import jax.numpy as jnp
from jax import lax
from jax.experimental import pallas as pl
from jax.experimental.pallas import tpu as pltpu
from jax.sharding import Mesh, PartitionSpec as P

F = 768
H = 1024
BR = 32
K = 10
NODE_DEV = 2048
TGT = 1024
NB_DEV = 64
R_DEV = 128
CHIP_COUNT = 64
DEVICES = 128
HALF = F // 2
RQ = R_DEV // 2
ALL = ("z", "core", "x", "y")
CHIPS = ("z", "x", "y")
SWAP = [(0, 1), (1, 0)]
HB = 256
RB = 96
RBP = 112


def exchange(array, axes):
    return lax.all_to_all(array, axes, split_axis=0, concat_axis=0, tiled=True)


def select_rows(indices, count, source):
    columns = jnp.arange(count, dtype=jnp.int32)
    picker = (indices[:, None] == columns[None, :]).astype(jnp.bfloat16)
    return jnp.dot(picker, source, preferred_element_type=jnp.float32).astype(jnp.bfloat16)


def stripe_kernel(codes_ref, scales_ref, values_ref, stripes_ref, wide):
    wide[...] = codes_ref[...].astype(jnp.float32) * scales_ref[...]
    values_ref[...] = wide[...].astype(jnp.bfloat16)
    for row in range(BR):
        stripes_ref[row, 0] = wide[pl.ds(row, NB_DEV, stride=BR), :].astype(jnp.bfloat16)


def make_stripes(codes, scales):
    return pl.pallas_call(
        stripe_kernel,
        grid=(6,),
        in_specs=[
            pl.BlockSpec((NODE_DEV, 128), lambda k: (0, k)),
            pl.BlockSpec((NODE_DEV, 1), lambda k: (0, 0)),
        ],
        out_specs=[
            pl.BlockSpec((NODE_DEV, 128), lambda k: (0, k)),
            pl.BlockSpec((BR, 1, NB_DEV, 128), lambda k: (0, k // 3, 0, k % 3)),
        ],
        out_shape=[
            jax.ShapeDtypeStruct((NODE_DEV, F), jnp.bfloat16),
            jax.ShapeDtypeStruct((BR, 2, NB_DEV, HALF), jnp.bfloat16),
        ],
        scratch_shapes=[pltpu.VMEM((NODE_DEV, 128), jnp.float32)],
        compiler_params=pltpu.CompilerParams(vmem_limit_bytes=32 << 20),
        name="make_stripes",
    )(codes, scales)


GROUP = 8
TABLE = CHIP_COUNT * NB_DEV


def gather_kernel(wanted_ref, own_ref, sister_ref, out_ref, t0, t1, t2, g0, g1, g2):
    tables, picked = (t0, t1, t2), (g0, g1, g2)

    @pl.when(pl.program_id(0) == 0)
    def _():
        for k in range(3):
            for part, source in enumerate((own_ref, sister_ref)):
                tables[k][pl.ds(part * TABLE, TABLE), :] = source[
                    :, k * 128 : (k + 1) * 128
                ].astype(jnp.float32)

    first = pl.program_id(0) * GROUP

    def one(step, carry):
        for j in range(RQ):
            at = wanted_ref[first + step, j]
            for k in range(3):
                picked[k][pl.ds(j, 1), :] = tables[k][pl.ds(at, 1), :]
        for k in range(3):
            out_ref[step, :, k * 128 : (k + 1) * 128] = picked[k][...].astype(jnp.bfloat16)
        return carry

    lax.fori_loop(0, GROUP, one, 0)


def gather(wanted, own, sister):
    return pl.pallas_call(
        gather_kernel,
        grid_spec=pltpu.PrefetchScalarGridSpec(
            num_scalar_prefetch=1,
            grid=(DEVICES // GROUP,),
            in_specs=[
                pl.BlockSpec((TABLE, HALF), lambda i, w: (0, 0), pipeline_mode=pl.Buffered(1)),
                pl.BlockSpec((TABLE, HALF), lambda i, w: (0, 0), pipeline_mode=pl.Buffered(1)),
            ],
            out_specs=pl.BlockSpec((GROUP, RQ, HALF), lambda i, w: (i, 0, 0)),
            scratch_shapes=[pltpu.VMEM((2 * TABLE, 128), jnp.float32)] * 3
            + [pltpu.VMEM((RQ, 128), jnp.float32)] * 3,
        ),
        out_shape=jax.ShapeDtypeStruct((DEVICES, RQ, HALF), jnp.bfloat16),
        compiler_params=pltpu.CompilerParams(vmem_limit_bytes=40 << 20),
        name="gather_rows",
    )(wanted, own, sister)


MEAN_STEPS = 8
COLS = 2 * BR * R_DEV // 2 // MEAN_STEPS


def layer_kernel(
    core_ref, got_ref, tally_ref, pre_ref, x_t_ref, weight_ref, cot_ref,
    hidden_ref, kept_ref, given_ref, acc, mean, mean_t,
):
    step = pl.program_id(0)

    @pl.when(step < MEAN_STEPS)
    def _():
        counts = tally_ref[...]
        for half in range(2):
            rows = jnp.concatenate(
                [got_ref[2 * e + half] for e in range(8)], axis=0
            )
            part = jnp.dot(counts, rows, preferred_element_type=jnp.float32)

            @pl.when(step == 0)
            def _():
                acc[half] = part

            @pl.when(step > 0)
            def _():
                acc[half] += part

    @pl.when(step == MEAN_STEPS - 1)
    def _():
        for half in range(2):
            value = (acc[half] / K).astype(jnp.bfloat16)
            mean[:, half * HALF : (half + 1) * HALF] = value
            mean_t[half * HALF : (half + 1) * HALF, :] = value.T

    @pl.when(step >= MEAN_STEPS)
    def _():
        pre = pre_ref[...] + jnp.dot(
            mean[...], weight_ref[...], preferred_element_type=jnp.float32
        )
        square = pre * pre
        tangent = jnp.tanh(0.7978845608 * (pre + 0.044715 * pre * square))
        rest = 1.0 + tangent
        hidden_ref[...] = (0.5 * pre * rest).astype(jnp.bfloat16)
        slope = 0.5 * rest + 0.5 * pre * (1.0 - tangent * tangent) * 0.7978845608 * (
            1.0 + 3.0 * 0.044715 * square
        )
        wide = cot_ref[...].astype(jnp.float32) * slope
        delta = wide.astype(jnp.bfloat16)
        bias_term = jnp.sum(delta.astype(jnp.float32), axis=0, keepdims=True)
        first = core_ref[0] == 0
        grad_self = jnp.dot(x_t_ref[...], delta, preferred_element_type=jnp.float32)
        grad_neigh = jnp.dot(mean_t[...], delta, preferred_element_type=jnp.float32)
        tail = jnp.broadcast_to(bias_term, (RBP - RB, HB)).astype(jnp.bfloat16)
        for ref, value in (
            (kept_ref, jnp.where(first, grad_self, grad_neigh)),
            (given_ref, jnp.where(first, grad_neigh, grad_self)),
        ):
            value = value.astype(jnp.bfloat16)
            for c in range(HB // 128):
                lanes = slice(c * 128, (c + 1) * 128)
                for r in range(8):
                    ref[r, c, :RB, :] = value[r * RB : (r + 1) * RB, lanes]
                    ref[r, c, RB:, :] = tail[:, lanes]


def layer(core, got, tally, pre_self, x_t, weight_neigh, cotangent):
    last = MEAN_STEPS - 1
    early = lambda i, w: jnp.minimum(i, last)
    late = lambda i, w: jnp.maximum(i - MEAN_STEPS, 0)
    term = pl.BlockSpec((8, HB // 128, RBP, 128), lambda i, w: (0, late(i, w), 0, 0))
    return pl.pallas_call(
        layer_kernel,
        grid_spec=pltpu.PrefetchScalarGridSpec(
            num_scalar_prefetch=1,
            grid=(MEAN_STEPS + H // HB,),
            in_specs=[
                pl.BlockSpec((16, RQ, HALF), lambda i, w: (early(i, w), 0, 0)),
                pl.BlockSpec((TGT, COLS), lambda i, w: (0, early(i, w))),
                pl.BlockSpec((TGT, HB), lambda i, w: (0, late(i, w))),
                pl.BlockSpec((F, TGT), lambda i, w: (0, 0)),
                pl.BlockSpec((F, HB), lambda i, w: (0, late(i, w))),
                pl.BlockSpec((TGT, HB), lambda i, w: (0, late(i, w))),
            ],
            out_specs=[pl.BlockSpec((TGT, HB), lambda i, w: (0, late(i, w))), term, term],
            scratch_shapes=[
                pltpu.VMEM((2, TGT, HALF), jnp.float32),
                pltpu.VMEM((TGT, F), jnp.bfloat16),
                pltpu.VMEM((F, TGT), jnp.bfloat16),
            ],
        ),
        out_shape=[
            jax.ShapeDtypeStruct((TGT, H), jnp.bfloat16),
            jax.ShapeDtypeStruct((8, 8, RBP, 128), jnp.bfloat16),
            jax.ShapeDtypeStruct((8, 8, RBP, 128), jnp.bfloat16),
        ],
        compiler_params=pltpu.CompilerParams(vmem_limit_bytes=56 << 20),
        name="layer",
    )(core, got, tally, pre_self, x_t, weight_neigh, cotangent)


def unpack(chunks):
    rows = chunks.reshape(8, 8, RBP, 128)
    grad = rows[:, :, :RB, :].transpose(0, 2, 1, 3).reshape(F, H).astype(jnp.float32)
    return grad, rows[0, :, RB, :].reshape(H).astype(jnp.float32)


def sum_over_devices(kept, given, first):
    kept = kept.reshape(CHIP_COUNT, RBP, 128)
    received = lax.ppermute(given.reshape(CHIP_COUNT, RBP, 128), "core", SWAP)
    chip = (kept.astype(jnp.float32) + received.astype(jnp.float32)).astype(jnp.bfloat16)
    parts = exchange(chip, CHIPS)
    mine = jnp.sum(parts.astype(jnp.float32), axis=0).astype(jnp.bfloat16)
    full = exchange(jnp.broadcast_to(mine[None], (CHIP_COUNT, RBP, 128)), CHIPS)
    theirs = lax.ppermute(full, "core", SWAP)
    grad_self, grad_bias = unpack(jnp.where(first, full, theirs))
    grad_neigh, _ = unpack(jnp.where(first, theirs, full))
    return grad_self, grad_neigh, grad_bias


def local(
    node_codes, node_scales, target_rows, owners, local_blocks, neighbours,
    weight_self, weight_neigh, bias, cotangent,
):
    core = lax.axis_index("core")
    owner = owners[:, 0]
    owner_core = (owner // 16) % 2
    owner_chip = (owner // 32) * 16 + owner % 16
    serving = (jnp.arange(R_DEV, dtype=jnp.int32) // RQ) % 2
    place = (owner_core != serving).astype(jnp.int32) * TABLE + owner_chip * NB_DEV + local_blocks
    asked = jnp.broadcast_to(place.reshape(1, 2, 1, RQ), (4, 2, 16, RQ)).reshape(DEVICES, RQ)
    wanted = exchange(asked, ALL)

    values, stripes = make_stripes(node_codes, node_scales.astype(jnp.float32)[:, None])
    own = exchange(stripes.reshape(CHIP_COUNT, NB_DEV, HALF), CHIPS)
    own = own.reshape(TABLE, HALF)
    sister = lax.ppermute(own, "core", SWAP)
    got = exchange(gather(wanted, own, sister), ALL)

    x_self = select_rows(target_rows, NODE_DEV, values)
    pre_self = jnp.dot(x_self, weight_self, preferred_element_type=jnp.float32) + bias
    block, row = neighbours // BR, neighbours % BR
    column = (row // 8) * 1024 + (block // RQ) * 512 + (row % 8) * RQ + block % RQ
    ids = jnp.arange(R_DEV * BR, dtype=jnp.int32)
    tally = jnp.zeros((TGT, R_DEV * BR), jnp.float32)
    for step in range(K):
        tally = tally + (column[:, step][:, None] == ids[None, :]).astype(jnp.float32)

    hidden, kept, given = layer(
        core.reshape(1).astype(jnp.int32), got, tally.astype(jnp.bfloat16), pre_self, x_self.T,
        weight_neigh, cotangent,
    )
    return (hidden,) + sum_over_devices(kept, given, core == 0)


def solution(mesh):
    fine = Mesh(mesh.devices.reshape(4, 2, 4, 4), ALL)
    placed = (
        P(ALL, None),
        P(ALL),
        P(ALL),
        P(ALL, None),
        P(ALL),
        P(ALL, None),
        P(),
        P(),
        P(),
        P(ALL, None),
    )
    return jax.shard_map(
        local,
        mesh=fine,
        in_specs=placed,
        out_specs=(P(ALL, None), P(), P(), P()),
        check_vma=False,
    )
```

time: 379 us -> 296 us (0.78); the launches traced: 374 us -> 295 us
  waiting for transfers between devices: 166 us -> 47.3 us
  blocking collectives: 65.1 us -> 126 us
  Pallas kernels: 0 us -> 54 us
  matrix products: 58.3 us -> 9.54 us
  local copies, waits for them, and re-layouts: 45.2 us -> 13.1 us
  other arithmetic: 10.2 us -> 32.4 us
  starting transfers between devices: 28.5 us -> 11.8 us
    all_to_all x2 -> x1, waiting for transfers between devices: 159 us -> 39.8 us  [exchange(): return lax.all_to_all(array, axes, split_axis=0, concat_axis=0, tiled=True)]
    all_to_all x2 -> x4, blocking collectives: 65.1 us -> 126 us  [exchange(): return lax.all_to_all(array, axes, split_axis=0, concat_axis=0, tiled=True)]
    pallas_call x0 -> x3, Pallas kernels: none -> 54 us  [the longest x1 26.7 us: layer(): pl.pallas_call(layer_kernel, grid_spec=pltpu.PrefetchScalarGridSpec(num_s...]
    dot_general x5 -> x1, matrix products: 42.5 us -> 3.83 us  [local(): jnp.dot(x_self, weight_self, preferred_element_type=jnp.float32) + bias]
    convert_element_type x5 -> x4, other arithmetic: 6.21 us -> 27.4 us  [the longest x1 26 us: local(): tally.astype(jnp.bfloat16)]
    all_to_all x2 -> x1, starting transfers between devices: 22.4 us -> 5.67 us  [exchange(): return lax.all_to_all(array, axes, split_axis=0, concat_axis=0, tiled=True)]
    unnamed x18 -> x22, local copies, waits for them, and re-layouts: 20 us -> 4.51 us
    reshape x4 -> x0, local copies, waits for them, and re-layouts: 14.5 us -> none  [the longest x1 9.09 us: local(): select_rows(slots, slot_count, got.reshape(slot_count, BR * width))]
  transfers between devices with their start and end apart: 4 -> 4, of which waited for: 3 -> 3; matrix products, arithmetic and copies ran while one was open for 5% -> 12% of each run, Pallas kernels for 0% -> 0%
where the time goes in v2:
time: 296 us; the launch traced here: 295 us
  blocking collectives  126 us (43%)
  Pallas kernels  54 us (18%)
  waiting for transfers between devices  47.3 us (16%)
  other arithmetic  32.4 us (11%)
  local copies, waits for them, and re-layouts  13.1 us (4%)
  starting transfers between devices  11.8 us (4%)
  matrix products  9.54 us (3%)
    all_to_all x4, blocking collectives, exchange(): return lax.all_to_all(array, axes, split_axis=0, concat_axis=0, tiled=True)  126 us
    all_to_all x1, waiting for transfers between devices, exchange(): return lax.all_to_all(array, axes, split_axis=0, concat_axis=0, tiled=True)  39.8 us
    pallas_call x1, Pallas kernels, layer(): pl.pallas_call(layer_kernel, grid_spec=pltpu.PrefetchScalarGridSpec(num_s...  26.7 us
    convert_element_type x1, other arithmetic, local(): tally.astype(jnp.bfloat16)  26 us
    pallas_call x1, Pallas kernels, gather(): pl.pallas_call(gather_kernel, grid_spec=pltpu.PrefetchScalarGridSpec(num_...  20.4 us
    convert_element_type x3, local copies, waits for them, and re-layouts, unpack(): rows[:, :, :RB, :].transpose(0, 2, 1, 3).reshape(F, H).astype(jnp.float32)  7.84 us
    pallas_call x1, Pallas kernels, make_stripes(): pl.pallas_call(stripe_kernel, grid=(6,), in_specs=[pl.BlockSpec((NODE_DEV...  6.88 us
  transfers between devices with their start and end apart: 4, of which 3 were waited for; matrix products, arithmetic and copies ran while one was open for 12% of the time, Pallas kernels for 0%

profile of v2, /device:TPU:1, one launch (start us, length us, event | category | flops | bytes accessed | tf_op | source)
XLA Modules:
  0.0 295.2 jit_solution(17198667708189497834)
XLA Ops:
  0.6 0.8 broadcast_in_dim.15
  1.8 1.9 copy-done.3
  3.7 6.9 %make_stripes.1 = (bf16[2048,768]{1,0:T(8,128)(2,1)S(1)}, bf16[32,2,64,384]{3,2,1,0:T(8,128)(2,1)S(1)}) custom-call(bf16[2048,768]{1,0:T(8,128)(2,1)S(1)} %copy-done.3, f32[2048,1]{1,0:T(8,128)S(1)} %copy.21.scales_ref), custom_call_target="tpu_custom_call" | custom-call | tf_op jit(solution)/shard_map/make_stripes/pallas_call | solution.py:46
  10.6 51.6 %all_to_all.31 = bf16[64,64,384]{2,1,0:T(8,128)(2,1)} all-to-all(bf16[64,64,384]{2,1,0:T(8,128)(2,1)S(1)} %bitcast.55), channel_id=1, replica_groups=mesh['z'=4,'core'=2,'x'=4,'y'=4] {'z','x','y'}, dimensions={0} | all-to-all | bytes 6291456 | tf_op jit(solution)/shard_map/all_to_all | solution.py:29
  62.3 2.5 collective-permute-start
  64.9 13.2 %all_to_all.32 = s32[128,1,64]{2,1,0:T(1,128)S(1)} all-to-all(s32[128,1,64]{2,1,0:T(1,128)S(1)} %bitcast.63), channel_id=1, replica_groups=mesh['z'=4,'core'=2,'x'=4,'y'=4] {'z','core','x','y'}, dimensions={0} | all-to-all | bytes 65536 | tf_op jit(solution)/shard_map/all_to_all | solution.py:29
  78.1 20.4 %gather_rows.1 = bf16[128,64,384]{2,1,0:T(8,128)(2,1)S(1)} custom-call(s32[128,64]{1,0:T(8,128)S(1)} %bitcast.56, bf16[4096,384]{1,0:T(8,128)(2,1)} %bitcast.6.own_ref, bf16[4096,384]{1,0:T(8,128)(2,1)} %collective-permute-done.sister_ref), custom_call_target="tpu_custom_call" | custom-call | tf_op jit(solution)/shard_map/gather_rows/pallas_call | solution.py:97
  98.6 2.6 copy-done.2
  101.1 5.7 %all-to-all-start.2 = ((bf16[128,64,384]{2,1,0:T(8,128)(2,1)}), bf16[128,64,384]{2,1,0:T(8,128)(2,1)}, u32[]{:S(2)}, u32[]{:S(2)}) async-start(bf16[128,64,384]{2,1,0:T(8,128)(2,1)} %copy-done.2), calls=%async_computation.2 | async-start | bytes 12582912 | tf_op jit(solution)/shard_map/all_to_all | solution.py:29
  107.1 5.7 %fusion.3 = bf16[1024,768]{0,1:T(8,128)(2,1)S(1)} fusion(bf16[2048,768]{1,0:T(8,128)(2,1)} %copy-done.4, s32[1024]{0:T(1024)S(1)} %copy-done.7), kind=kOutput, calls=%fused_computation.23 | convolution fusion | flops 3224109056 | bytes 4722688 | tf_op jit(solution)/shard_map/dot_general | solution.py:35
  112.8 3.8 %broadcast_add_fusion.pre_ref = f32[1024,1024]{1,0:T(8,128)} fusion(f32[1024]{0:T(1024)S(1)} %copy-done.8, bf16[1024,768]{0,1:T(8,128)(2,1)S(1)} %fusion.3, bf16[768,1024]{1,0:T(8,128)(2,1)S(1)} %copy-done), kind=kOutput, calls=%fused_computation.20 | convolution fusion | flops 1611661312 | bytes 7344128 | tf_op jit(solution)/shard_map/dot_general | solution.py:255
  116.7 26.0 %add_convert_fusion.tally_ref = bf16[1024,4096]{1,0:T(8,128)(2,1)} fusion(s32[1024]{0:T(1024)S(1)} %bitcast.66, s32[1024]{0:T(1024)S(1)} %bitcast.67, s32[1024]{0:T(1024)S(1)} %bitcast.68, s32[1024]{0:T(1024)S(1)} %bitcast.69, s32[1024]{0:T(1024)S(1)} %bitcast.70, s32[1024]{0:T(1024)S(1)} %bitcast.71, s32[1024]{0:T(1024)S(1)} %bitcast.72, ...), kind=kLoop, calls=%fused_computation | loop fusion | flops 125829120 | bytes 8429568 | tf_op jit(solution)/shard_map/convert_element_type | solution.py:264
  142.7 39.8 %all-to-all-done.2.got_ref = bf16[128,64,384]{2,1,0:T(8,128)(2,1)} async-done(((bf16[128,64,384]{2,1,0:T(8,128)(2,1)}), bf16[128,64,384]{2,1,0:T(8,128)(2,1)}, u32[]{:S(2)}, u32[]{:S(2)}) %all-to-all-start.2) | async-done | bytes 6291488 | tf_op jit(solution)/shard_map/all_to_all | solution.py:29
  182.5 26.7 %layer.1 = (bf16[1024,1024]{1,0:T(8,128)(2,1)}, bf16[8,8,112,128]{3,2,1,0:T(8,128)(2,1)}, bf16[8,8,112,128]{3,2,1,0:T(8,128)(2,1)}) custom-call(s32[1]{0:T(128)} %bitcast.core_ref, bf16[128,64,384]{2,1,0:T(8,128)(2,1)} %all-to-all-done.2.got_ref, bf16[1024,4096]{1,0:T(8,128)(2,1)} %add_convert_fusion.tally_ref, f32[1024,1024]{1,0:T(8,128)} %broadcast_add_fusion.pre_ref, ...), custom_call_target="tpu_custom_call" | custom-call | tf_op jit(solution)/shard_map/layer/pallas_call | solution.py:186
  209.3 3.9 %collective-permute-done.1 = bf16[64,112,128]{2,1,0:T(8,128)(2,1)S(1)} collective-permute-done((bf16[64,112,128]{2,1,0:T(8,128)(2,1)}, bf16[64,112,128]{2,1,0:T(8,128)(2,1)S(1)}, u32[]{:S(2)}, u32[]{:S(2)}) %collective-permute-start.1) | collective-permute-done | bytes 1835040 | tf_op jit(solution)/shard_map/ppermute | solution.py:224
  213.2 2.0 fusion.2
  215.2 31.4 %all_to_all.33 = bf16[64,112,128]{2,1,0:T(8,128)(2,1)S(1)} all-to-all(bf16[64,112,128]{2,1,0:T(8,128)(2,1)S(1)} %fusion.2), channel_id=1, replica_groups=mesh['z'=4,'core'=2,'x'=4,'y'=4] {'z','x','y'}, dimensions={0} | all-to-all | bytes 3670016 | tf_op jit(solution)/shard_map/all_to_all | solution.py:29
  247.0 30.0 %all_to_all.34 = bf16[64,112,128]{2,1,0:T(8,128)(2,1)S(1)} all-to-all(bf16[64,112,128]{2,1,0:T(8,128)(2,1)S(1)} %broadcast_in_dim.14), channel_id=1, replica_groups=mesh['z'=4,'core'=2,'x'=4,'y'=4] {'z','x','y'}, dimensions={0} | all-to-all | bytes 3670016 | tf_op jit(solution)/shard_map/all_to_all | solution.py:29
  277.1 3.6 %collective-permute-start.2 = (bf16[64,112,128]{2,1,0:T(8,128)(2,1)S(1)}, bf16[64,112,128]{2,1,0:T(8,128)(2,1)}, u32[]{:S(2)}, u32[]{:S(2)}) collective-permute-start(bf16[64,112,128]{2,1,0:T(8,128)(2,1)S(1)} %all_to_all.34), channel_id=1, source_target_pairs={{0,16},{16,0},{1,17},{17,1},{2,18},{18,2},{3,19},{19,3},{4,20},{20... | collective-permute-start | bytes 5505032 | tf_op jit(solution)/shard_map/ppermute | solution.py:229
  280.7 3.5 %collective-permute-done.2 = bf16[64,112,128]{2,1,0:T(8,128)(2,1)} collective-permute-done((bf16[64,112,128]{2,1,0:T(8,128)(2,1)S(1)}, bf16[64,112,128]{2,1,0:T(8,128)(2,1)}, u32[]{:S(2)}, u32[]{:S(2)}) %collective-permute-start.2) | collective-permute-done | bytes 1835040 | tf_op jit(solution)/shard_map/ppermute | solution.py:229
  284.2 1.7 broadcast_select_fusion
  287.0 1.8 copy.23
  289.2 1.8 copy.24
  291.0 4.3 %copy_bitcast_fusion = (f32[768,1024]{1,0:T(8,128)}, f32[768,1024]{1,0:T(8,128)}) fusion(f32[96,8,8,128]{3,2,1,0:T(8,128)S(1)} %bitcast.58, f32[96,8,8,128]{3,2,1,0:T(8,128)S(1)} %bitcast.57), kind=kLoop, calls=%fused_computation.16 | loop fusion | bytes 12582912 | tf_op jit(solution)/shard_map/convert_element_type | solution.py:218
  (33 shorter events, 2.7 us)
Async XLA Ops:
  0.6 112.2 %copy-start = (bf16[768,1024]{1,0:T(8,128)(2,1)S(1)}, bf16[768,1024]{1,0:T(8,128)(2,1)}, u32[]{:S(2)}) copy-start(bf16[768,1024]{1,0:T(8,128)(2,1)} %param.16) | copy-start | bytes 4718596
  1.8 1.9 copy-start.3
  10.6 51.7 %copy-start.4 = (bf16[2048,768]{1,0:T(8,128)(2,1)}, bf16[2048,768]{1,0:T(8,128)(2,1)S(1)}, u32[]{:S(2)}) copy-start(bf16[2048,768]{1,0:T(8,128)(2,1)S(1)} %get-tuple-element.10) | copy-start | bytes 9437188
  10.6 54.2 %copy-start.9 = (s32[128]{0:T(128)S(1)}, s32[128]{0:T(128)}, u32[]{:S(2)}) copy-start(s32[128]{0:T(128)} %param.14) | copy-start | bytes 1540
  10.6 54.2 %copy-start.10 = (s32[128,1]{0,1:T(1,128)S(1)}, s32[128,1]{0,1:T(1,128)}, u32[]{:S(2)}) copy-start(s32[128,1]{0,1:T(1,128)} %param.13) | copy-start | bytes 1540
  62.3 15.8 %collective-permute-start = (bf16[4096,384]{1,0:T(8,128)(2,1)}, bf16[4096,384]{1,0:T(8,128)(2,1)}, u32[]{:S(2)}, u32[]{:S(2)}) collective-permute-start(bf16[4096,384]{1,0:T(8,128)(2,1)} %bitcast.6.own_ref), channel_id=1, source_target_pairs={{0,16},{16,0},{1,17},{17,1},{2,18},{18,2},{3,19},{19,3},{4,20},{20... | collective-permute-start | bytes 9437192 | tf_op jit(solution)/shard_map/ppermute | solution.py:251
  98.6 2.6 copy-start.2
  101.1 5.7 %copy-start.6 = (s32[1024,10]{0,1:T(8,128)S(1)}, s32[1024,10]{0,1:T(8,128)}, u32[]{:S(2)}) copy-start(s32[1024,10]{0,1:T(8,128)} %param.15) | copy-start | bytes 122884
  101.1 5.9 %copy-start.7 = (s32[1024]{0:T(1024)S(1)}, s32[1024]{0:T(1024)}, u32[]{:S(2)}) copy-start(s32[1024]{0:T(1024)} %param.12) | copy-start | bytes 12292
  101.1 81.3 %all-to-all-start.2 = ((bf16[128,64,384]{2,1,0:T(8,128)(2,1)}), bf16[128,64,384]{2,1,0:T(8,128)(2,1)}, u32[]{:S(2)}, u32[]{:S(2)}) async-start(bf16[128,64,384]{2,1,0:T(8,128)(2,1)} %copy-done.2), calls=%async_computation.2 | async-start | bytes 12582912 | tf_op jit(solution)/shard_map/all_to_all | solution.py:29
  107.1 5.7 %copy-start.8 = (f32[1024]{0:T(1024)S(1)}, f32[1024]{0:T(1024)}, u32[]{:S(2)}) copy-start(f32[1024]{0:T(1024)} %param.18) | copy-start | bytes 12292
  112.8 3.8 %copy-start.5 = (bf16[1024,768]{0,1:T(8,128)(2,1)}, bf16[1024,768]{0,1:T(8,128)(2,1)S(1)}, u32[]{:S(2)}) copy-start(bf16[1024,768]{0,1:T(8,128)(2,1)S(1)} %fusion.3) | copy-start | bytes 4718596
  209.2 4.0 %collective-permute-start.1 = (bf16[64,112,128]{2,1,0:T(8,128)(2,1)}, bf16[64,112,128]{2,1,0:T(8,128)(2,1)S(1)}, u32[]{:S(2)}, u32[]{:S(2)}) collective-permute-start(bf16[64,112,128]{2,1,0:T(8,128)(2,1)} %bitcast.76), channel_id=1, source_target_pairs={{0,16},{16,0},{1,17},{17,1},{2,18},{18,2},{3,19},{19,3},{4,20},{20... | collective-permute-start | bytes 5505032 | tf_op jit(solution)/shard_map/ppermute | solution.py:224
  277.1 7.1 %collective-permute-start.2 = (bf16[64,112,128]{2,1,0:T(8,128)(2,1)S(1)}, bf16[64,112,128]{2,1,0:T(8,128)(2,1)}, u32[]{:S(2)}, u32[]{:S(2)}) collective-permute-start(bf16[64,112,128]{2,1,0:T(8,128)(2,1)S(1)} %all_to_all.34), channel_id=1, source_target_pairs={{0,16},{16,0},{1,17},{17,1},{2,18},{18,2},{3,19},{19,3},{4,20},{20... | collective-permute-start | bytes 5505032 | tf_op jit(solution)/shard_map/ppermute | solution.py:229
  291.0 4.3 %copy-start.1 = (bf16[768,1024]{1,0:T(8,128)(2,1)S(1)}, bf16[768,1024]{1,0:T(8,128)(2,1)}, u32[]{:S(2)}) copy-start(bf16[768,1024]{1,0:T(8,128)(2,1)} %param.16) | copy-start | bytes 4718596

commit v3 on v2

--- a/solution.py
+++ b/solution.py
@@ -59,38 +59,40 @@
             jax.ShapeDtypeStruct((BR, 2, NB_DEV, HALF), jnp.bfloat16),
         ],
         scratch_shapes=[pltpu.VMEM((NODE_DEV, 128), jnp.float32)],
-        compiler_params=pltpu.CompilerParams(vmem_limit_bytes=32 << 20),
+        compiler_params=pltpu.CompilerParams(vmem_limit_bytes=60 << 20),
         name="make_stripes",
     )(codes, scales)
 
 
-GROUP = 8
+GROUP = 16
 TABLE = CHIP_COUNT * NB_DEV
-
-
-def gather_kernel(wanted_ref, own_ref, sister_ref, out_ref, t0, t1, t2, g0, g1, g2):
-    tables, picked = (t0, t1, t2), (g0, g1, g2)
-
+SLOT = 4
+
+
+def gather_kernel(wanted_ref, own_ref, sister_ref, out_ref, table, picked):
     @pl.when(pl.program_id(0) == 0)
     def _():
-        for k in range(3):
-            for part, source in enumerate((own_ref, sister_ref)):
-                tables[k][pl.ds(part * TABLE, TABLE), :] = source[
+        for part, source in enumerate((own_ref, sister_ref)):
+            for k in range(3):
+                table[pl.ds(part * TABLE * SLOT + k, TABLE, stride=SLOT), :] = source[
                     :, k * 128 : (k + 1) * 128
                 ].astype(jnp.float32)
 
     first = pl.program_id(0) * GROUP
 
-    def one(step, carry):
-        for j in range(RQ):
-            at = wanted_ref[first + step, j]
+    def pair(step, carry):
+        for u in range(2):
+            base = u * RQ * SLOT
+            for j in range(RQ):
+                at = pl.multiple_of(wanted_ref[first + 2 * step + u, j], SLOT)
+                picked[pl.ds(base + j * SLOT, SLOT), :] = table[pl.ds(at, SLOT), :]
             for k in range(3):
-                picked[k][pl.ds(j, 1), :] = tables[k][pl.ds(at, 1), :]
-        for k in range(3):
-            out_ref[step, :, k * 128 : (k + 1) * 128] = picked[k][...].astype(jnp.bfloat16)
+                out_ref[2 * step + u, :, k * 128 : (k + 1) * 128] = picked[
+                    pl.ds(base + k, RQ, stride=SLOT), :
+                ].astype(jnp.bfloat16)
         return carry
 
-    lax.fori_loop(0, GROUP, one, 0)
+    lax.fori_loop(0, GROUP // 2, pair, 0)
 
 
 def gather(wanted, own, sister):
@@ -104,11 +106,13 @@
                 pl.BlockSpec((TABLE, HALF), lambda i, w: (0, 0), pipeline_mode=pl.Buffered(1)),
             ],
             out_specs=pl.BlockSpec((GROUP, RQ, HALF), lambda i, w: (i, 0, 0)),
-            scratch_shapes=[pltpu.VMEM((2 * TABLE, 128), jnp.float32)] * 3
-            + [pltpu.VMEM((RQ, 128), jnp.float32)] * 3,
+            scratch_shapes=[
+                pltpu.VMEM((2 * TABLE * SLOT, 128), jnp.float32),
+                pltpu.VMEM((2 * RQ * SLOT, 128), jnp.float32),
+            ],
         ),
         out_shape=jax.ShapeDtypeStruct((DEVICES, RQ, HALF), jnp.bfloat16),
-        compiler_params=pltpu.CompilerParams(vmem_limit_bytes=40 << 20),
+        compiler_params=pltpu.CompilerParams(vmem_limit_bytes=60 << 20),
         name="gather_rows",
     )(wanted, own, sister)
 
@@ -125,27 +129,28 @@
 
     @pl.when(step < MEAN_STEPS)
     def _():
-        counts = tally_ref[...]
-        for half in range(2):
-            rows = jnp.concatenate(
-                [got_ref[2 * e + half] for e in range(8)], axis=0
-            )
-            part = jnp.dot(counts, rows, preferred_element_type=jnp.float32)
-
-            @pl.when(step == 0)
-            def _():
-                acc[half] = part
-
-            @pl.when(step > 0)
-            def _():
-                acc[half] += part
+        rows = jnp.concatenate(
+            [
+                jnp.concatenate([got_ref[2 * e + half] for e in range(8)], axis=0)
+                for half in range(2)
+            ],
+            axis=1,
+        )
+        part = jnp.dot(tally_ref[...], rows, preferred_element_type=jnp.float32)
+
+        @pl.when(step == 0)
+        def _():
+            acc[...] = part
+
+        @pl.when(step > 0)
+        def _():
+            acc[...] += part
 
     @pl.when(step == MEAN_STEPS - 1)
     def _():
-        for half in range(2):
-            value = (acc[half] / K).astype(jnp.bfloat16)
-            mean[:, half * HALF : (half + 1) * HALF] = value
-            mean_t[half * HALF : (half + 1) * HALF, :] = value.T
+        value = (acc[...] / K).astype(jnp.bfloat16)
+        mean[...] = value
+        mean_t[...] = value.T
 
     @pl.when(step >= MEAN_STEPS)
     def _():
@@ -198,7 +203,7 @@
             ],
             out_specs=[pl.BlockSpec((TGT, HB), lambda i, w: (0, late(i, w))), term, term],
             scratch_shapes=[
-                pltpu.VMEM((2, TGT, HALF), jnp.float32),
+                pltpu.VMEM((TGT, F), jnp.float32),
                 pltpu.VMEM((TGT, F), jnp.bfloat16),
                 pltpu.VMEM((F, TGT), jnp.bfloat16),
             ],
@@ -213,13 +218,42 @@
     )(core, got, tally, pre_self, x_t, weight_neigh, cotangent)
 
 
-def unpack(chunks):
-    rows = chunks.reshape(8, 8, RBP, 128)
-    grad = rows[:, :, :RB, :].transpose(0, 2, 1, 3).reshape(F, H).astype(jnp.float32)
-    return grad, rows[0, :, RB, :].reshape(H).astype(jnp.float32)
-
-
-def sum_over_devices(kept, given, first):
+def unpack_kernel(core_ref, full_ref, theirs_ref, self_ref, neigh_ref, bias_ref):
+    first = core_ref[0] == 0
+    for c in range(8):
+        lanes = slice(c * 128, (c + 1) * 128)
+        a = full_ref[0, c].astype(jnp.float32)
+        b = theirs_ref[0, c].astype(jnp.float32)
+        self_ref[:, lanes] = jnp.where(first, a[:RB], b[:RB])
+        neigh_ref[:, lanes] = jnp.where(first, b[:RB], a[:RB])
+        bias_ref[:, lanes] = a[RB : RB + 1]
+
+
+def unpack(core, full, theirs):
+    chunks = pl.BlockSpec((1, 8, RBP, 128), lambda i, w: (i, 0, 0, 0))
+    return pl.pallas_call(
+        unpack_kernel,
+        grid_spec=pltpu.PrefetchScalarGridSpec(
+            num_scalar_prefetch=1,
+            grid=(8,),
+            in_specs=[chunks, chunks],
+            out_specs=[
+                pl.BlockSpec((RB, H), lambda i, w: (i, 0)),
+                pl.BlockSpec((RB, H), lambda i, w: (i, 0)),
+                pl.BlockSpec((1, H), lambda i, w: (0, 0)),
+            ],
+        ),
+        out_shape=[
+            jax.ShapeDtypeStruct((F, H), jnp.float32),
+            jax.ShapeDtypeStruct((F, H), jnp.float32),
+            jax.ShapeDtypeStruct((1, H), jnp.float32),
+        ],
+        compiler_params=pltpu.CompilerParams(vmem_limit_bytes=60 << 20),
+        name="unpack",
+    )(core, full.reshape(8, 8, RBP, 128), theirs.reshape(8, 8, RBP, 128))
+
+
+def sum_over_devices(kept, given, core):
     kept = kept.reshape(CHIP_COUNT, RBP, 128)
     received = lax.ppermute(given.reshape(CHIP_COUNT, RBP, 128), "core", SWAP)
     chip = (kept.astype(jnp.float32) + received.astype(jnp.float32)).astype(jnp.bfloat16)
@@ -227,9 +261,8 @@
     mine = jnp.sum(parts.astype(jnp.float32), axis=0).astype(jnp.bfloat16)
     full = exchange(jnp.broadcast_to(mine[None], (CHIP_COUNT, RBP, 128)), CHIPS)
     theirs = lax.ppermute(full, "core", SWAP)
-    grad_self, grad_bias = unpack(jnp.where(first, full, theirs))
-    grad_neigh, _ = unpack(jnp.where(first, theirs, full))
-    return grad_self, grad_neigh, grad_bias
+    grad_self, grad_neigh, grad_bias = unpack(core, full, theirs)
+    return grad_self, grad_neigh, grad_bias.reshape(H)
 
 
 def local(
@@ -242,6 +275,7 @@
     owner_chip = (owner // 32) * 16 + owner % 16
     serving = (jnp.arange(R_DEV, dtype=jnp.int32) // RQ) % 2
     place = (owner_core != serving).astype(jnp.int32) * TABLE + owner_chip * NB_DEV + local_blocks
+    place = place * SLOT
     asked = jnp.broadcast_to(place.reshape(1, 2, 1, RQ), (4, 2, 16, RQ)).reshape(DEVICES, RQ)
     wanted = exchange(asked, ALL)
 
@@ -260,11 +294,11 @@
     for step in range(K):
         tally = tally + (column[:, step][:, None] == ids[None, :]).astype(jnp.float32)
 
+    which = core.reshape(1).astype(jnp.int32)
     hidden, kept, given = layer(
-        core.reshape(1).astype(jnp.int32), got, tally.astype(jnp.bfloat16), pre_self, x_self.T,
-        weight_neigh, cotangent,
+        which, got, tally.astype(jnp.bfloat16), pre_self, x_self.T, weight_neigh, cotangent
     )
-    return (hidden,) + sum_over_devices(kept, given, core == 0)
+    return (hidden,) + sum_over_devices(kept, given, which)
 
 
 def solution(mesh):

time: 296 us -> 285 us (0.963)
  local copies, waits for them, and re-layouts: 13.1 us -> 2.99 us
  other arithmetic: 32.4 us -> 29.3 us
    convert_element_type x3 -> x0, local copies, waits for them, and re-layouts: 7.84 us -> none  [unpack(): rows[:, :, :RB, :].transpose(0, 2, 1, 3).reshape(F, H).astype(jnp.float32)]
    pallas_call x0 -> x1, Pallas kernels: none -> 7.16 us  [unpack(): pl.pallas_call(unpack_kernel, grid_spec=pltpu.PrefetchScalarGridSpec(num_...]
    pallas_call x1, Pallas kernels: 20.4 us -> 16.3 us  [gather(): pl.pallas_call(gather_kernel, grid_spec=pltpu.PrefetchScalarGridSpec(num_...]
    pallas_call x1, Pallas kernels: 26.7 us -> 23.4 us  [layer(): pl.pallas_call(layer_kernel, grid_spec=pltpu.PrefetchScalarGridSpec(num_s...]
    unnamed x22 -> x20, local copies, waits for them, and re-layouts: 4.51 us -> 1.28 us
  transfers between devices with their start and end apart: 4 -> 4, of which waited for: 3 -> 3; matrix products, arithmetic and copies ran while one was open for 12% -> 13% of each run, Pallas kernels for 0% -> 0%
where the time goes in v3:
time: 285 us; the launch traced here: 284 us
  blocking collectives  127 us (45%)
  Pallas kernels  55.5 us (19%)
  waiting for transfers between devices  47.2 us (17%)
  other arithmetic  29.3 us (10%)
  starting transfers between devices  12 us (4%)
  matrix products  9.55 us (3%)
  local copies, waits for them, and re-layouts  2.99 us (1%)
    all_to_all x4, blocking collectives, exchange(): return lax.all_to_all(array, axes, split_axis=0, concat_axis=0, tiled=True)  127 us
    all_to_all x1, waiting for transfers between devices, exchange(): return lax.all_to_all(array, axes, split_axis=0, concat_axis=0, tiled=True)  39.8 us
    convert_element_type x1, other arithmetic, local(): tally.astype(jnp.bfloat16)  26 us
    pallas_call x1, Pallas kernels, layer(): pl.pallas_call(layer_kernel, grid_spec=pltpu.PrefetchScalarGridSpec(num_s...  23.4 us
    pallas_call x1, Pallas kernels, gather(): pl.pallas_call(gather_kernel, grid_spec=pltpu.PrefetchScalarGridSpec(num_...  16.3 us
    pallas_call x1, Pallas kernels, make_stripes(): pl.pallas_call(stripe_kernel, grid=(6,), in_specs=[pl.BlockSpec((NODE_DEV...  8.67 us
    pallas_call x1, Pallas kernels, unpack(): pl.pallas_call(unpack_kernel, grid_spec=pltpu.PrefetchScalarGridSpec(num_...  7.16 us
    all_to_all x1, starting transfers between devices, exchange(): return lax.all_to_all(array, axes, split_axis=0, concat_axis=0, tiled=True)  5.88 us
  transfers between devices with their start and end apart: 4, of which 3 were waited for; matrix products, arithmetic and copies ran while one was open for 13% of the time, Pallas kernels for 0%

profile of v3, /device:TPU:1, one launch (start us, length us, event | category | flops | bytes accessed | tf_op | source)
XLA Modules:
  0.0 284.0 jit_solution(17291134532536185924)
XLA Ops:
  0.6 0.8 broadcast_in_dim.15
  1.5 1.3 copy.17.scales_ref
  2.8 8.7 %make_stripes.1 = (bf16[2048,768]{1,0:T(8,128)(2,1)}, bf16[32,2,64,384]{3,2,1,0:T(8,128)(2,1)}) custom-call(bf16[2048,768]{1,0:T(8,128)(2,1)} %codes_ref.1, f32[2048,1]{1,0:T(8,128)} %copy.17.scales_ref), custom_call_target="tpu_custom_call" | custom-call | tf_op jit(solution)/shard_map/make_stripes/pallas_call | solution.py:46
  11.5 51.8 %all_to_all.31 = bf16[64,64,384]{2,1,0:T(8,128)(2,1)} all-to-all(bf16[64,64,384]{2,1,0:T(8,128)(2,1)} %bitcast.46), channel_id=1, replica_groups=mesh['z'=4,'core'=2,'x'=4,'y'=4] {'z','x','y'}, dimensions={0} | all-to-all | bytes 6291456 | tf_op jit(solution)/shard_map/all_to_all | solution.py:29
  63.3 2.5 collective-permute-start
  65.9 13.4 %all_to_all.32 = s32[128,1,64]{2,1,0:T(1,128)} all-to-all(s32[128,1,64]{2,1,0:T(1,128)S(1)} %bitcast.50), channel_id=1, replica_groups=mesh['z'=4,'core'=2,'x'=4,'y'=4] {'z','core','x','y'}, dimensions={0} | all-to-all | bytes 65536 | tf_op jit(solution)/shard_map/all_to_all | solution.py:29
  79.4 16.3 %gather_rows.1 = bf16[128,64,384]{2,1,0:T(8,128)(2,1)} custom-call(s32[128,64]{1,0:T(8,128)} %bitcast.49, bf16[4096,384]{1,0:T(8,128)(2,1)} %bitcast.6.own_ref, bf16[4096,384]{1,0:T(8,128)(2,1)} %collective-permute-done.sister_ref), custom_call_target="tpu_custom_call" | custom-call | tf_op jit(solution)/shard_map/gather_rows/pallas_call | solution.py:99
  95.6 5.9 %all-to-all-start.2 = ((bf16[128,64,384]{2,1,0:T(8,128)(2,1)}), bf16[128,64,384]{2,1,0:T(8,128)(2,1)}, u32[]{:S(2)}, u32[]{:S(2)}) async-start(bf16[128,64,384]{2,1,0:T(8,128)(2,1)} %gather_rows.1), calls=%async_computation.2 | async-start | bytes 12582912 | tf_op jit(solution)/shard_map/all_to_all | solution.py:29
  101.5 0.2 fusion.7
  101.8 5.7 %fusion.3 = bf16[1024,768]{0,1:T(8,128)(2,1)S(1)} fusion(bf16[2048,768]{1,0:T(8,128)(2,1)} %get-tuple-element.13, s32[1024]{0:T(1024)S(1)} %copy-done.6), kind=kOutput, calls=%fused_computation.17 | convolution fusion | flops 3224109056 | bytes 4722688 | tf_op jit(solution)/shard_map/dot_general | solution.py:35
  107.5 3.8 %broadcast_add_fusion.pre_ref = f32[1024,1024]{1,0:T(8,128)} fusion(f32[1024]{0:T(1024)S(1)} %copy-done.7, bf16[1024,768]{0,1:T(8,128)(2,1)S(1)} %fusion.3, bf16[768,1024]{1,0:T(8,128)(2,1)S(1)} %copy-done), kind=kOutput, calls=%fused_computation.16 | convolution fusion | flops 1611661312 | bytes 7344128 | tf_op jit(solution)/shard_map/dot_general | solution.py:289
  111.4 26.0 %add_convert_fusion.tally_ref = bf16[1024,4096]{1,0:T(8,128)(2,1)} fusion(s32[1024]{0:T(1024)S(1)} %bitcast.53, s32[1024]{0:T(1024)S(1)} %bitcast.54, s32[1024]{0:T(1024)S(1)} %bitcast.55, s32[1024]{0:T(1024)S(1)} %bitcast.56, s32[1024]{0:T(1024)S(1)} %bitcast.57, s32[1024]{0:T(1024)S(1)} %bitcast.58, s32[1024]{0:T(1024)S(1)} %bitcast.59, ...), kind=kLoop, calls=%fused_computation | loop fusion | flops 125829120 | bytes 8429568 | tf_op jit(solution)/shard_map/convert_element_type | solution.py:299
  137.4 39.8 %all-to-all-done.2.got_ref = bf16[128,64,384]{2,1,0:T(8,128)(2,1)} async-done(((bf16[128,64,384]{2,1,0:T(8,128)(2,1)}), bf16[128,64,384]{2,1,0:T(8,128)(2,1)}, u32[]{:S(2)}, u32[]{:S(2)}) %all-to-all-start.2) | async-done | bytes 6291488 | tf_op jit(solution)/shard_map/all_to_all | solution.py:29
  177.2 23.4 %layer.1 = (bf16[1024,1024]{1,0:T(8,128)(2,1)}, bf16[8,8,112,128]{3,2,1,0:T(8,128)(2,1)}, bf16[8,8,112,128]{3,2,1,0:T(8,128)(2,1)}) custom-call(s32[1]{0:T(128)} %bitcast.core_ref, bf16[128,64,384]{2,1,0:T(8,128)(2,1)} %all-to-all-done.2.got_ref, bf16[1024,4096]{1,0:T(8,128)(2,1)} %add_convert_fusion.tally_ref, f32[1024,1024]{1,0:T(8,128)} %broadcast_add_fusion.pre_ref, ...), custom_call_target="tpu_custom_call" | custom-call | tf_op jit(solution)/shard_map/layer/pallas_call | solution.py:191
  200.7 3.9 %collective-permute-done.1 = bf16[64,112,128]{2,1,0:T(8,128)(2,1)S(1)} collective-permute-done((bf16[64,112,128]{2,1,0:T(8,128)(2,1)}, bf16[64,112,128]{2,1,0:T(8,128)(2,1)S(1)}, u32[]{:S(2)}, u32[]{:S(2)}) %collective-permute-start.1) | collective-permute-done | bytes 1835040 | tf_op jit(solution)/shard_map/ppermute | solution.py:258
  204.6 2.0 fusion.2
  206.6 31.4 %all_to_all.33 = bf16[64,112,128]{2,1,0:T(8,128)(2,1)S(1)} all-to-all(bf16[64,112,128]{2,1,0:T(8,128)(2,1)S(1)} %fusion.2), channel_id=1, replica_groups=mesh['z'=4,'core'=2,'x'=4,'y'=4] {'z','x','y'}, dimensions={0} | all-to-all | bytes 3670016 | tf_op jit(solution)/shard_map/all_to_all | solution.py:29
  237.9 0.3 reduce_sum.12
  238.2 0.2 broadcast_in_dim.14
  238.4 30.0 %all_to_all.34 = bf16[64,112,128]{2,1,0:T(8,128)(2,1)S(1)} all-to-all(bf16[64,112,128]{2,1,0:T(8,128)(2,1)S(1)} %broadcast_in_dim.14), channel_id=1, replica_groups=mesh['z'=4,'core'=2,'x'=4,'y'=4] {'z','x','y'}, dimensions={0} | all-to-all | bytes 3670016 | tf_op jit(solution)/shard_map/all_to_all | solution.py:29
  268.5 3.6 %collective-permute-start.2 = (bf16[64,112,128]{2,1,0:T(8,128)(2,1)S(1)}, bf16[64,112,128]{2,1,0:T(8,128)(2,1)S(1)}, u32[]{:S(2)}, u32[]{:S(2)}) collective-permute-start(bf16[64,112,128]{2,1,0:T(8,128)(2,1)S(1)} %all_to_all.34), channel_id=1, source_target_pairs={{0,16},{16,0},{1,17},{17,1},{2,18},{18,2},{3,19},{19,3},{4,20},{20... | collective-permute-start | bytes 5505032 | tf_op jit(solution)/shard_map/ppermute | solution.py:263
  272.1 3.4 %collective-permute-done.2 = bf16[64,112,128]{2,1,0:T(8,128)(2,1)S(1)} collective-permute-done((bf16[64,112,128]{2,1,0:T(8,128)(2,1)S(1)}, bf16[64,112,128]{2,1,0:T(8,128)(2,1)S(1)}, u32[]{:S(2)}, u32[]{:S(2)}) %collective-permute-start.2) | collective-permute-done | bytes 1835040 | tf_op jit(solution)/shard_map/ppermute | solution.py:263
  275.5 1.2 copy-done.3
  276.7 7.2 %unpack.1 = (f32[768,1024]{1,0:T(8,128)}, f32[768,1024]{1,0:T(8,128)}, f32[1,1024]{1,0:T(1,128)}) custom-call(s32[1]{0:T(128)} %bitcast.core_ref, bf16[8,8,112,128]{3,2,1,0:T(8,128)(2,1)} %bitcast.45, bf16[8,8,112,128]{3,2,1,0:T(8,128)(2,1)} %bitcast.47), custom_call_target="tpu_custom_call" | custom-call | tf_op jit(solution)/shard_map/unpack/pallas_call | solution.py:234
  (25 shorter events, 0.3 us)
Async XLA Ops:
  0.6 106.9 %copy-start = (bf16[768,1024]{1,0:T(8,128)(2,1)S(1)}, bf16[768,1024]{1,0:T(8,128)(2,1)}, u32[]{:S(2)}) copy-start(bf16[768,1024]{1,0:T(8,128)(2,1)} %param.16) | copy-start | bytes 4718596
  11.5 54.3 %copy-start.8 = (s32[128]{0:T(128)S(1)}, s32[128]{0:T(128)}, u32[]{:S(2)}) copy-start(s32[128]{0:T(128)} %param.14) | copy-start | bytes 1540
  11.5 54.3 %copy-start.9 = (s32[128,1]{0,1:T(1,128)S(1)}, s32[128,1]{0,1:T(1,128)}, u32[]{:S(2)}) copy-start(s32[128,1]{0,1:T(1,128)} %param.13) | copy-start | bytes 1540
  63.3 16.1 %collective-permute-start = (bf16[4096,384]{1,0:T(8,128)(2,1)}, bf16[4096,384]{1,0:T(8,128)(2,1)}, u32[]{:S(2)}, u32[]{:S(2)}) collective-permute-start(bf16[4096,384]{1,0:T(8,128)(2,1)} %bitcast.6.own_ref), channel_id=1, source_target_pairs={{0,16},{16,0},{1,17},{17,1},{2,18},{18,2},{3,19},{19,3},{4,20},{20... | collective-permute-start | bytes 9437192 | tf_op jit(solution)/shard_map/ppermute | solution.py:285
  95.6 5.9 %copy-start.5 = (s32[1024,10]{0,1:T(8,128)S(1)}, s32[1024,10]{0,1:T(8,128)}, u32[]{:S(2)}) copy-start(s32[1024,10]{0,1:T(8,128)} %param.15) | copy-start | bytes 122884
  95.6 6.1 %copy-start.6 = (s32[1024]{0:T(1024)S(1)}, s32[1024]{0:T(1024)}, u32[]{:S(2)}) copy-start(s32[1024]{0:T(1024)} %param.12) | copy-start | bytes 12292
  95.6 81.6 %all-to-all-start.2 = ((bf16[128,64,384]{2,1,0:T(8,128)(2,1)}), bf16[128,64,384]{2,1,0:T(8,128)(2,1)}, u32[]{:S(2)}, u32[]{:S(2)}) async-start(bf16[128,64,384]{2,1,0:T(8,128)(2,1)} %gather_rows.1), calls=%async_computation.2 | async-start | bytes 12582912 | tf_op jit(solution)/shard_map/all_to_all | solution.py:29
  101.8 5.7 %copy-start.7 = (f32[1024]{0:T(1024)S(1)}, f32[1024]{0:T(1024)}, u32[]{:S(2)}) copy-start(f32[1024]{0:T(1024)} %param.18) | copy-start | bytes 12292
  107.5 3.8 %copy-start.4 = (bf16[1024,768]{0,1:T(8,128)(2,1)}, bf16[1024,768]{0,1:T(8,128)(2,1)S(1)}, u32[]{:S(2)}) copy-start(bf16[1024,768]{0,1:T(8,128)(2,1)S(1)} %fusion.3) | copy-start | bytes 4718596
  200.6 4.0 %collective-permute-start.1 = (bf16[64,112,128]{2,1,0:T(8,128)(2,1)}, bf16[64,112,128]{2,1,0:T(8,128)(2,1)S(1)}, u32[]{:S(2)}, u32[]{:S(2)}) collective-permute-start(bf16[64,112,128]{2,1,0:T(8,128)(2,1)} %bitcast.62), channel_id=1, source_target_pairs={{0,16},{16,0},{1,17},{17,1},{2,18},{18,2},{3,19},{19,3},{4,20},{20... | collective-permute-start | bytes 5505032 | tf_op jit(solution)/shard_map/ppermute | solution.py:258
  237.9 46.0 %copy-start.1 = (bf16[768,1024]{1,0:T(8,128)(2,1)S(1)}, bf16[768,1024]{1,0:T(8,128)(2,1)}, u32[]{:S(2)}) copy-start(bf16[768,1024]{1,0:T(8,128)(2,1)} %param.16) | copy-start | bytes 4718596
  268.5 8.2 %copy-start.2 = (bf16[64,112,128]{2,1,0:T(8,128)(2,1)}, bf16[64,112,128]{2,1,0:T(8,128)(2,1)S(1)}, u32[]{:S(2)}) copy-start(bf16[64,112,128]{2,1,0:T(8,128)(2,1)S(1)} %all_to_all.34) | copy-start | bytes 5505028
  268.5 7.0 %collective-permute-start.2 = (bf16[64,112,128]{2,1,0:T(8,128)(2,1)S(1)}, bf16[64,112,128]{2,1,0:T(8,128)(2,1)S(1)}, u32[]{:S(2)}, u32[]{:S(2)}) collective-permute-start(bf16[64,112,128]{2,1,0:T(8,128)(2,1)S(1)} %all_to_all.34), channel_id=1, source_target_pairs={{0,16},{16,0},{1,17},{17,1},{2,18},{18,2},{3,19},{19,3},{4,20},{20... | collective-permute-start | bytes 5505032 | tf_op jit(solution)/shard_map/ppermute | solution.py:263
  275.5 1.2 copy-start.3

commit v4 on v3

--- a/solution.py
+++ b/solution.py
@@ -35,9 +35,24 @@
     return jnp.dot(picker, source, preferred_element_type=jnp.float32).astype(jnp.bfloat16)
 
 
-def stripe_kernel(codes_ref, scales_ref, values_ref, stripes_ref, wide):
-    wide[...] = codes_ref[...].astype(jnp.float32) * scales_ref[...]
-    values_ref[...] = wide[...].astype(jnp.bfloat16)
+def stripe_copy(codes_ref, codes, sem, k):
+    lanes = pl.ds(pl.multiple_of(k * 128, 128), 128)
+    return pltpu.make_async_copy(codes_ref.at[:, lanes], codes.at[k], sem.at[k])
+
+
+def stripe_kernel(codes_ref, scales_ref, stripes_ref, codes, scales, wide, sem):
+    k = pl.program_id(0)
+
+    @pl.when(k == 0)
+    def _():
+        for n in range(6):
+            stripe_copy(codes_ref, codes, sem, n).start()
+        columns = scales_ref[...].T
+        for c in range(NODE_DEV // 128):
+            scales[c * 128 : (c + 1) * 128, :] = jnp.broadcast_to(columns[:, c : c + 1], (128, 128))
+
+    stripe_copy(codes_ref, codes, sem, k).wait()
+    wide[...] = codes[k].astype(jnp.float32) * scales[...]
     for row in range(BR):
         stripes_ref[row, 0] = wide[pl.ds(row, NB_DEV, stride=BR), :].astype(jnp.bfloat16)
 
@@ -47,21 +62,20 @@
         stripe_kernel,
         grid=(6,),
         in_specs=[
-            pl.BlockSpec((NODE_DEV, 128), lambda k: (0, k)),
-            pl.BlockSpec((NODE_DEV, 1), lambda k: (0, 0)),
+            pl.BlockSpec(memory_space=pltpu.HBM),
+            pl.BlockSpec((NODE_DEV // 128, 128), lambda k: (0, 0)),
         ],
-        out_specs=[
-            pl.BlockSpec((NODE_DEV, 128), lambda k: (0, k)),
-            pl.BlockSpec((BR, 1, NB_DEV, 128), lambda k: (0, k // 3, 0, k % 3)),
+        out_specs=pl.BlockSpec((BR, 1, NB_DEV, 128), lambda k: (0, k // 3, 0, k % 3)),
+        out_shape=jax.ShapeDtypeStruct((BR, 2, NB_DEV, HALF), jnp.bfloat16),
+        scratch_shapes=[
+            pltpu.VMEM((6, NODE_DEV, 128), jnp.bfloat16),
+            pltpu.VMEM((NODE_DEV, 128), jnp.float32),
+            pltpu.VMEM((NODE_DEV, 128), jnp.float32),
+            pltpu.SemaphoreType.DMA((6,)),
         ],
-        out_shape=[
-            jax.ShapeDtypeStruct((NODE_DEV, F), jnp.bfloat16),
-            jax.ShapeDtypeStruct((BR, 2, NB_DEV, HALF), jnp.bfloat16),
-        ],
-        scratch_shapes=[pltpu.VMEM((NODE_DEV, 128), jnp.float32)],
-        compiler_params=pltpu.CompilerParams(vmem_limit_bytes=60 << 20),
+        compiler_params=pltpu.CompilerParams(vmem_limit_bytes=12 << 20),
         name="make_stripes",
-    )(codes, scales)
+    )(codes, scales.reshape(NODE_DEV // 128, 128))
 
 
 GROUP = 16
@@ -111,13 +125,13 @@
                 pltpu.VMEM((2 * RQ * SLOT, 128), jnp.float32),
             ],
         ),
-        out_shape=jax.ShapeDtypeStruct((DEVICES, RQ, HALF), jnp.bfloat16),
-        compiler_params=pltpu.CompilerParams(vmem_limit_bytes=60 << 20),
+        out_shape=pltpu.HBM((DEVICES, RQ, HALF), jnp.bfloat16),
+        compiler_params=pltpu.CompilerParams(vmem_limit_bytes=27 << 20),
         name="gather_rows",
     )(wanted, own, sister)
 
 
-MEAN_STEPS = 8
+MEAN_STEPS = 4
 COLS = 2 * BR * R_DEV // 2 // MEAN_STEPS
 
 
@@ -131,7 +145,7 @@
     def _():
         rows = jnp.concatenate(
             [
-                jnp.concatenate([got_ref[2 * e + half] for e in range(8)], axis=0)
+                jnp.concatenate([got_ref[2 * e + half] for e in range(COLS // RQ)], axis=0)
                 for half in range(2)
             ],
             axis=1,
@@ -194,7 +208,7 @@
             num_scalar_prefetch=1,
             grid=(MEAN_STEPS + H // HB,),
             in_specs=[
-                pl.BlockSpec((16, RQ, HALF), lambda i, w: (early(i, w), 0, 0)),
+                pl.BlockSpec((DEVICES // MEAN_STEPS, RQ, HALF), lambda i, w: (early(i, w), 0, 0)),
                 pl.BlockSpec((TGT, COLS), lambda i, w: (0, early(i, w))),
                 pl.BlockSpec((TGT, HB), lambda i, w: (0, late(i, w))),
                 pl.BlockSpec((F, TGT), lambda i, w: (0, 0)),
@@ -213,33 +227,35 @@
             jax.ShapeDtypeStruct((8, 8, RBP, 128), jnp.bfloat16),
             jax.ShapeDtypeStruct((8, 8, RBP, 128), jnp.bfloat16),
         ],
-        compiler_params=pltpu.CompilerParams(vmem_limit_bytes=56 << 20),
+        compiler_params=pltpu.CompilerParams(vmem_limit_bytes=28 << 20),
         name="layer",
     )(core, got, tally, pre_self, x_t, weight_neigh, cotangent)
 
 
 def unpack_kernel(core_ref, full_ref, theirs_ref, self_ref, neigh_ref, bias_ref):
     first = core_ref[0] == 0
-    for c in range(8):
-        lanes = slice(c * 128, (c + 1) * 128)
-        a = full_ref[0, c].astype(jnp.float32)
-        b = theirs_ref[0, c].astype(jnp.float32)
-        self_ref[:, lanes] = jnp.where(first, a[:RB], b[:RB])
-        neigh_ref[:, lanes] = jnp.where(first, b[:RB], a[:RB])
-        bias_ref[:, lanes] = a[RB : RB + 1]
+    for r in range(2):
+        rows = slice(r * RB, (r + 1) * RB)
+        for c in range(8):
+            lanes = slice(c * 128, (c + 1) * 128)
+            a = full_ref[r, c].astype(jnp.float32)
+            b = theirs_ref[r, c].astype(jnp.float32)
+            self_ref[rows, lanes] = jnp.where(first, a[:RB], b[:RB])
+            neigh_ref[rows, lanes] = jnp.where(first, b[:RB], a[:RB])
+            bias_ref[:, lanes] = a[RB : RB + 1]
 
 
 def unpack(core, full, theirs):
-    chunks = pl.BlockSpec((1, 8, RBP, 128), lambda i, w: (i, 0, 0, 0))
+    chunks = pl.BlockSpec((2, 8, RBP, 128), lambda i, w: (i, 0, 0, 0))
     return pl.pallas_call(
         unpack_kernel,
         grid_spec=pltpu.PrefetchScalarGridSpec(
             num_scalar_prefetch=1,
-            grid=(8,),
+            grid=(4,),
             in_specs=[chunks, chunks],
             out_specs=[
-                pl.BlockSpec((RB, H), lambda i, w: (i, 0)),
-                pl.BlockSpec((RB, H), lambda i, w: (i, 0)),
+                pl.BlockSpec((2 * RB, H), lambda i, w: (i, 0)),
+                pl.BlockSpec((2 * RB, H), lambda i, w: (i, 0)),
                 pl.BlockSpec((1, H), lambda i, w: (0, 0)),
             ],
         ),
@@ -248,7 +264,7 @@
             jax.ShapeDtypeStruct((F, H), jnp.float32),
             jax.ShapeDtypeStruct((1, H), jnp.float32),
         ],
-        compiler_params=pltpu.CompilerParams(vmem_limit_bytes=60 << 20),
+        compiler_params=pltpu.CompilerParams(vmem_limit_bytes=12 << 20),
         name="unpack",
     )(core, full.reshape(8, 8, RBP, 128), theirs.reshape(8, 8, RBP, 128))
 
@@ -279,13 +295,15 @@
     asked = jnp.broadcast_to(place.reshape(1, 2, 1, RQ), (4, 2, 16, RQ)).reshape(DEVICES, RQ)
     wanted = exchange(asked, ALL)
 
-    values, stripes = make_stripes(node_codes, node_scales.astype(jnp.float32)[:, None])
+    stripes = make_stripes(node_codes, node_scales.astype(jnp.float32))
     own = exchange(stripes.reshape(CHIP_COUNT, NB_DEV, HALF), CHIPS)
     own = own.reshape(TABLE, HALF)
     sister = lax.ppermute(own, "core", SWAP)
     got = exchange(gather(wanted, own, sister), ALL)
 
-    x_self = select_rows(target_rows, NODE_DEV, values)
+    self_codes = select_rows(target_rows, NODE_DEV, node_codes)
+    self_scales = select_rows(target_rows, NODE_DEV, node_scales[:, None])
+    x_self = (self_codes.astype(jnp.float32) * self_scales.astype(jnp.float32)).astype(jnp.bfloat16)
     pre_self = jnp.dot(x_self, weight_self, preferred_element_type=jnp.float32) + bias
     block, row = neighbours // BR, neighbours % BR
     column = (row // 8) * 1024 + (block // RQ) * 512 + (row % 8) * RQ + block % RQ

time: 285 us -> 276 us (0.968)
  Pallas kernels: 55.5 us -> 46.2 us
  local copies, waits for them, and re-layouts: 2.99 us -> 6.1 us
    unnamed x20 -> x29, local copies, waits for them, and re-layouts: 1.28 us -> 5.73 us
    pallas_call x1, Pallas kernels: 7.16 us -> 3.15 us  [unpack(): pl.pallas_call(unpack_kernel, grid_spec=pltpu.PrefetchScalarGridSpec(num_...]
    dot_general x1 -> x2, matrix products: 5.71 us -> 7.37 us  [select_rows(): jnp.dot(picker, source, preferred_element_type=jnp.float32)]
  transfers between devices with their start and end apart: 4 -> 4, of which waited for: 3 -> 3; matrix products, arithmetic and copies ran while one was open for 13% -> 14% of each run, Pallas kernels for 0% -> 0%
where the time goes in v4:
time: 276 us; the launch traced here: 275 us
  blocking collectives  126 us (46%)
  Pallas kernels  46.2 us (17%)
  waiting for transfers between devices  45.2 us (16%)
  other arithmetic  27.9 us (10%)
  starting transfers between devices  11.8 us (4%)
  matrix products  11.2 us (4%)
  local copies, waits for them, and re-layouts  6.1 us (2%)
    all_to_all x4, blocking collectives, exchange(): return lax.all_to_all(array, axes, split_axis=0, concat_axis=0, tiled=True)  126 us
    all_to_all x1, waiting for transfers between devices, exchange(): return lax.all_to_all(array, axes, split_axis=0, concat_axis=0, tiled=True)  38.1 us
    convert_element_type x1, other arithmetic, local(): tally.astype(jnp.bfloat16)  26 us
    pallas_call x1, Pallas kernels, layer(): pl.pallas_call(layer_kernel, grid_spec=pltpu.PrefetchScalarGridSpec(num_s...  20.6 us
    pallas_call x1, Pallas kernels, gather(): pl.pallas_call(gather_kernel, grid_spec=pltpu.PrefetchScalarGridSpec(num_...  16.1 us
    dot_general x2, matrix products, select_rows(): jnp.dot(picker, source, preferred_element_type=jnp.float32)  7.37 us
    pallas_call x1, Pallas kernels, make_stripes(): pl.pallas_call(stripe_kernel, grid=(6,), in_specs=[pl.BlockSpec(memory_sp...  6.28 us
    unnamed x29, local copies, waits for them, and re-layouts  5.73 us
  transfers between devices with their start and end apart: 4, of which 3 were waited for; matrix products, arithmetic and copies ran while one was open for 14% of the time, Pallas kernels for 0%

profile of v4, /device:TPU:1, one launch (start us, length us, event | category | flops | bytes accessed | tf_op | source)
XLA Modules:
  0.0 275.4 jit_solution(12754936188193438563)
XLA Ops:
  0.6 0.8 bitcast_convert_fusion.scales_ref
  1.5 1.9 copy-done.3
  3.3 6.3 %make_stripes.1 = bf16[32,2,64,384]{3,2,1,0:T(8,128)(2,1)S(1)} custom-call(bf16[2048,768]{1,0:T(8,128)(2,1)S(1)} %copy-done.3, f32[16,128]{1,0:T(8,128)S(1)} %bitcast_convert_fusion.scales_ref), custom_call_target="tpu_custom_call" | custom-call | tf_op jit(solution)/shard_map/make_stripes/pallas_call | solution.py:61
  9.7 51.5 %all_to_all.31 = bf16[64,64,384]{2,1,0:T(8,128)(2,1)} all-to-all(bf16[64,64,384]{2,1,0:T(8,128)(2,1)S(1)} %bitcast.49), channel_id=1, replica_groups=mesh['z'=4,'core'=2,'x'=4,'y'=4] {'z','x','y'}, dimensions={0} | all-to-all | bytes 6291456 | tf_op jit(solution)/shard_map/all_to_all | solution.py:29
  61.2 2.5 collective-permute-start
  63.8 13.2 %all_to_all.32 = s32[128,1,64]{2,1,0:T(1,128)S(1)} all-to-all(s32[128,1,64]{2,1,0:T(1,128)S(1)} %bitcast.55), channel_id=1, replica_groups=mesh['z'=4,'core'=2,'x'=4,'y'=4] {'z','core','x','y'}, dimensions={0} | all-to-all | bytes 65536 | tf_op jit(solution)/shard_map/all_to_all | solution.py:29
  77.0 16.1 %gather_rows.1 = bf16[128,64,384]{2,1,0:T(8,128)(2,1)} custom-call(s32[128,64]{1,0:T(8,128)S(1)} %bitcast.53, bf16[4096,384]{1,0:T(8,128)(2,1)} %bitcast.6.own_ref, bf16[4096,384]{1,0:T(8,128)(2,1)} %collective-permute-done.sister_ref), custom_call_target="tpu_custom_call" | custom-call | tf_op jit(solution)/shard_map/gather_rows/pallas_call | solution.py:113
  93.1 5.7 %all-to-all-start.2 = ((bf16[128,64,384]{2,1,0:T(8,128)(2,1)}), bf16[128,64,384]{2,1,0:T(8,128)(2,1)}, u32[]{:S(2)}, u32[]{:S(2)}) async-start(bf16[128,64,384]{2,1,0:T(8,128)(2,1)} %gather_rows.1), calls=%async_computation.2 | async-start | bytes 12582912 | tf_op jit(solution)/shard_map/all_to_all | solution.py:29
  98.8 1.6 fusion
  100.7 5.7 %multiply_convert_fusion = bf16[1024,768]{0,1:T(8,128)(2,1)S(1)} fusion(f32[1024]{0:T(1024)S(1)} %convert_convert_fusion, bf16[2048,768]{1,0:T(8,128)(2,1)} %codes_ref.1, s32[1024]{0:T(1024)S(1)} %copy-done.10), kind=kOutput, calls=%fused_computation.18 | convolution fusion | flops 3226468352 | bytes 4726784 | tf_op jit(solution)/shard_map/dot_general | solution.py:35
  106.5 3.8 %broadcast_add_fusion.pre_ref = f32[1024,1024]{1,0:T(8,128)} fusion(f32[1024]{0:T(1024)S(1)} %copy-done.11, bf16[1024,768]{0,1:T(8,128)(2,1)S(1)} %multiply_convert_fusion, bf16[768,1024]{1,0:T(8,128)(2,1)S(1)} %copy-done), kind=kOutput, calls=%fused_computation.19 | convolution fusion | flops 1611661312 | bytes 7344128 | tf_op jit(solution)/shard_map/dot_general | solution.py:307
  110.3 26.0 %add_convert_fusion.tally_ref = bf16[1024,4096]{1,0:T(8,128)(2,1)} fusion(s32[1024]{0:T(1024)S(1)} %bitcast.57, s32[1024]{0:T(1024)S(1)} %bitcast.58, s32[1024]{0:T(1024)S(1)} %bitcast.59, s32[1024]{0:T(1024)S(1)} %bitcast.60, s32[1024]{0:T(1024)S(1)} %bitcast.61, s32[1024]{0:T(1024)S(1)} %bitcast.62, s32[1024]{0:T(1024)S(1)} %bitcast.63, ...), kind=kLoop, calls=%fused_computation | loop fusion | flops 125829120 | bytes 8429568 | tf_op jit(solution)/shard_map/convert_element_type | solution.py:317
  136.4 38.1 %all-to-all-done.2.got_ref = bf16[128,64,384]{2,1,0:T(8,128)(2,1)} async-done(((bf16[128,64,384]{2,1,0:T(8,128)(2,1)}), bf16[128,64,384]{2,1,0:T(8,128)(2,1)}, u32[]{:S(2)}, u32[]{:S(2)}) %all-to-all-start.2) | async-done | bytes 6291488 | tf_op jit(solution)/shard_map/all_to_all | solution.py:29
  174.5 2.2 copy-done.2
  176.7 1.6 copy-done.4
  178.3 20.6 %layer.1 = (bf16[1024,1024]{1,0:T(8,128)(2,1)}, bf16[8,8,112,128]{3,2,1,0:T(8,128)(2,1)S(1)}, bf16[8,8,112,128]{3,2,1,0:T(8,128)(2,1)S(1)}) custom-call(s32[1]{0:T(128)} %bitcast.core_ref, bf16[128,64,384]{2,1,0:T(8,128)(2,1)} %all-to-all-done.2.got_ref, bf16[1024,4096]{1,0:T(8,128)(2,1)} %add_convert_fusion.tally_ref, f32[1024,1024]{1,0:T(8,128)S(1)} %copy-done.2, ...), custom_call_target="tpu_custom_call" | custom-call | tf_op jit(solution)/shard_map/layer/pallas_call | solution.py:205
  199.0 3.7 %collective-permute-done.1 = bf16[64,112,128]{2,1,0:T(8,128)(2,1)S(1)} collective-permute-done((bf16[64,112,128]{2,1,0:T(8,128)(2,1)S(1)}, bf16[64,112,128]{2,1,0:T(8,128)(2,1)S(1)}, u32[]{:S(2)}, u32[]{:S(2)}) %collective-permute-start.1) | collective-permute-done | bytes 1835040 | tf_op jit(solution)/shard_map/ppermute | solution.py:274
  202.7 0.6 fusion.4
  203.3 31.4 %all_to_all.33 = bf16[64,112,128]{2,1,0:T(8,128)(2,1)S(1)} all-to-all(bf16[64,112,128]{2,1,0:T(8,128)(2,1)S(1)} %fusion.4), channel_id=1, replica_groups=mesh['z'=4,'core'=2,'x'=4,'y'=4] {'z','x','y'}, dimensions={0} | all-to-all | bytes 3670016 | tf_op jit(solution)/shard_map/all_to_all | solution.py:29
  234.6 0.3 reduce_sum.12
  235.2 30.0 %all_to_all.34 = bf16[64,112,128]{2,1,0:T(8,128)(2,1)S(1)} all-to-all(bf16[64,112,128]{2,1,0:T(8,128)(2,1)S(1)} %broadcast_in_dim.8), channel_id=1, replica_groups=mesh['z'=4,'core'=2,'x'=4,'y'=4] {'z','x','y'}, dimensions={0} | all-to-all | bytes 3670016 | tf_op jit(solution)/shard_map/all_to_all | solution.py:29
  265.2 3.6 %collective-permute-start.2 = (bf16[64,112,128]{2,1,0:T(8,128)(2,1)S(1)}, bf16[64,112,128]{2,1,0:T(8,128)(2,1)S(1)}, u32[]{:S(2)}, u32[]{:S(2)}) collective-permute-start(bf16[64,112,128]{2,1,0:T(8,128)(2,1)S(1)} %all_to_all.34), channel_id=1, source_target_pairs={{0,16},{16,0},{1,17},{17,1},{2,18},{18,2},{3,19},{19,3},{4,20},{20... | collective-permute-start | bytes 5505032 | tf_op jit(solution)/shard_map/ppermute | solution.py:279
  268.8 3.4 %collective-permute-done.2 = bf16[64,112,128]{2,1,0:T(8,128)(2,1)S(1)} collective-permute-done((bf16[64,112,128]{2,1,0:T(8,128)(2,1)S(1)}, bf16[64,112,128]{2,1,0:T(8,128)(2,1)S(1)}, u32[]{:S(2)}, u32[]{:S(2)}) %collective-permute-start.2) | collective-permute-done | bytes 1835040 | tf_op jit(solution)/shard_map/ppermute | solution.py:279
  272.2 3.2 %unpack.1 = (f32[768,1024]{1,0:T(8,128)}, f32[768,1024]{1,0:T(8,128)}, f32[1,1024]{1,0:T(1,128)}) custom-call(s32[1]{0:T(128)} %bitcast.core_ref, bf16[8,8,112,128]{3,2,1,0:T(8,128)(2,1)S(1)} %bitcast.50, bf16[8,8,112,128]{3,2,1,0:T(8,128)(2,1)S(1)} %bitcast.51), custom_call_target="tpu_custom_call" | custom-call | tf_op jit(solution)/shard_map/unpack/pallas_call | solution.py:250
  (35 shorter events, 0.7 us)
Async XLA Ops:
  0.6 105.9 %copy-start = (bf16[768,1024]{1,0:T(8,128)(2,1)S(1)}, bf16[768,1024]{1,0:T(8,128)(2,1)}, u32[]{:S(2)}) copy-start(bf16[768,1024]{1,0:T(8,128)(2,1)} %param.16) | copy-start | bytes 4718596
  1.5 1.9 copy-start.3
  9.6 54.0 %copy-start.12 = (s32[128]{0:T(128)S(1)}, s32[128]{0:T(128)}, u32[]{:S(2)}) copy-start(s32[128]{0:T(128)} %param.14) | copy-start | bytes 1540
  9.6 54.0 %copy-start.13 = (s32[128,1]{0,1:T(1,128)S(1)}, s32[128,1]{0,1:T(1,128)}, u32[]{:S(2)}) copy-start(s32[128,1]{0,1:T(1,128)} %param.13) | copy-start | bytes 1540
  61.2 15.8 %collective-permute-start = (bf16[4096,384]{1,0:T(8,128)(2,1)}, bf16[4096,384]{1,0:T(8,128)(2,1)}, u32[]{:S(2)}, u32[]{:S(2)}) collective-permute-start(bf16[4096,384]{1,0:T(8,128)(2,1)} %bitcast.6.own_ref), channel_id=1, source_target_pairs={{0,16},{16,0},{1,17},{17,1},{2,18},{18,2},{3,19},{19,3},{4,20},{20... | collective-permute-start | bytes 9437192 | tf_op jit(solution)/shard_map/ppermute | solution.py:301
  93.1 5.7 %copy-start.9 = (bf16[2048]{0:T(1024)(128)(2,1)S(1)}, bf16[2048]{0:T(1024)(128)(2,1)}, u32[]{:S(2)}) copy-start(bf16[2048]{0:T(1024)(128)(2,1)} %param.11) | copy-start | bytes 12292
  93.1 5.7 %copy-start.10 = (s32[1024]{0:T(1024)S(1)}, s32[1024]{0:T(1024)}, u32[]{:S(2)}) copy-start(s32[1024]{0:T(1024)} %param.12) | copy-start | bytes 12292
  93.1 7.4 %copy-start.8 = (s32[1024,10]{0,1:T(8,128)S(1)}, s32[1024,10]{0,1:T(8,128)}, u32[]{:S(2)}) copy-start(s32[1024,10]{0,1:T(8,128)} %param.15) | copy-start | bytes 122884
  93.1 81.3 %all-to-all-start.2 = ((bf16[128,64,384]{2,1,0:T(8,128)(2,1)}), bf16[128,64,384]{2,1,0:T(8,128)(2,1)}, u32[]{:S(2)}, u32[]{:S(2)}) async-start(bf16[128,64,384]{2,1,0:T(8,128)(2,1)} %gather_rows.1), calls=%async_computation.2 | async-start | bytes 12582912 | tf_op jit(solution)/shard_map/all_to_all | solution.py:29
  100.7 5.8 %copy-start.11 = (f32[1024]{0:T(1024)S(1)}, f32[1024]{0:T(1024)}, u32[]{:S(2)}) copy-start(f32[1024]{0:T(1024)} %param.18) | copy-start | bytes 12292
  106.5 3.8 %copy-start.6 = (bf16[1024,768]{0,1:T(8,128)(2,1)}, bf16[1024,768]{0,1:T(8,128)(2,1)S(1)}, u32[]{:S(2)}) copy-start(bf16[1024,768]{0,1:T(8,128)(2,1)S(1)} %multiply_convert_fusion) | copy-start | bytes 4718596
  110.3 64.1 %copy-start.5 = (bf16[768,1024]{1,0:T(8,128)(2,1)S(1)}, bf16[768,1024]{1,0:T(8,128)(2,1)}, u32[]{:S(2)}) copy-start(bf16[768,1024]{1,0:T(8,128)(2,1)} %weight_ref.1) | copy-start | bytes 4718596
  110.3 64.1 %copy-start.7 = (bf16[1024,768]{0,1:T(8,128)(2,1)S(1)}, bf16[1024,768]{0,1:T(8,128)(2,1)}, u32[]{:S(2)}) copy-start(bf16[1024,768]{0,1:T(8,128)(2,1)} %copy-done.6) | copy-start | bytes 4718596
  174.5 2.2 copy-start.2
  176.7 1.6 copy-start.4
  198.9 3.8 %collective-permute-start.1 = (bf16[64,112,128]{2,1,0:T(8,128)(2,1)S(1)}, bf16[64,112,128]{2,1,0:T(8,128)(2,1)S(1)}, u32[]{:S(2)}, u32[]{:S(2)}) collective-permute-start(bf16[64,112,128]{2,1,0:T(8,128)(2,1)S(1)} %bitcast.54), channel_id=1, source_target_pairs={{0,16},{16,0},{1,17},{17,1},{2,18},{18,2},{3,19},{19,3},{4,20},{20... | collective-permute-start | bytes 5505032 | tf_op jit(solution)/shard_map/ppermute | solution.py:274
  234.6 40.7 %copy-start.1 = (bf16[768,1024]{1,0:T(8,128)(2,1)S(1)}, bf16[768,1024]{1,0:T(8,128)(2,1)}, u32[]{:S(2)}) copy-start(bf16[768,1024]{1,0:T(8,128)(2,1)} %param.16) | copy-start | bytes 4718596
  265.2 7.0 %collective-permute-start.2 = (bf16[64,112,128]{2,1,0:T(8,128)(2,1)S(1)}, bf16[64,112,128]{2,1,0:T(8,128)(2,1)S(1)}, u32[]{:S(2)}, u32[]{:S(2)}) collective-permute-start(bf16[64,112,128]{2,1,0:T(8,128)(2,1)S(1)} %all_to_all.34), channel_id=1, source_target_pairs={{0,16},{16,0},{1,17},{17,1},{2,18},{18,2},{3,19},{19,3},{4,20},{20... | collective-permute-start | bytes 5505032 | tf_op jit(solution)/shard_map/ppermute | solution.py:279

commit v5 on v4

--- a/solution.py
+++ b/solution.py
@@ -22,17 +22,11 @@
 SWAP = [(0, 1), (1, 0)]
 HB = 256
 RB = 96
-RBP = 112
+RBP = 104
 
 
 def exchange(array, axes):
     return lax.all_to_all(array, axes, split_axis=0, concat_axis=0, tiled=True)
-
-
-def select_rows(indices, count, source):
-    columns = jnp.arange(count, dtype=jnp.int32)
-    picker = (indices[:, None] == columns[None, :]).astype(jnp.bfloat16)
-    return jnp.dot(picker, source, preferred_element_type=jnp.float32).astype(jnp.bfloat16)
 
 
 def stripe_copy(codes_ref, codes, sem, k):
@@ -62,7 +56,7 @@
         stripe_kernel,
         grid=(6,),
         in_specs=[
-            pl.BlockSpec(memory_space=pltpu.HBM),
+            pl.BlockSpec(memory_space=pl.ANY),
             pl.BlockSpec((NODE_DEV // 128, 128), lambda k: (0, 0)),
         ],
         out_specs=pl.BlockSpec((BR, 1, NB_DEV, 128), lambda k: (0, k // 3, 0, k % 3)),
@@ -73,7 +67,7 @@
             pltpu.VMEM((NODE_DEV, 128), jnp.float32),
             pltpu.SemaphoreType.DMA((6,)),
         ],
-        compiler_params=pltpu.CompilerParams(vmem_limit_bytes=12 << 20),
+        compiler_params=pltpu.CompilerParams(vmem_limit_bytes=60 << 20),
         name="make_stripes",
     )(codes, scales.reshape(NODE_DEV // 128, 128))
 
@@ -129,6 +123,63 @@
         compiler_params=pltpu.CompilerParams(vmem_limit_bytes=27 << 20),
         name="gather_rows",
     )(wanted, own, sister)
+
+
+SIDE = 128
+
+
+def side_kernel(
+    target_ref, column_ref, codes_ref, scales_ref, weight_ref, bias_ref, x_t_ref, pre_ref, tally_ref
+):
+    hit = target_ref[...] == lax.broadcasted_iota(jnp.int32, (SIDE, NODE_DEV), 1)
+    picker = hit.astype(jnp.float32).astype(jnp.bfloat16)
+    own_codes = jnp.dot(picker, codes_ref[...], preferred_element_type=jnp.float32)
+    own_scales = jnp.sum(jnp.where(hit, scales_ref[...], 0.0), axis=1, keepdims=True)
+    x_self = (own_codes * own_scales).astype(jnp.bfloat16)
+    x_t_ref[...] = x_self.T
+    pre_ref[...] = bias_ref[...] + jnp.dot(
+        x_self, weight_ref[...], preferred_element_type=jnp.float32
+    )
+    wide = 256
+
+    def count(c, carry):
+        first = pl.multiple_of(c * wide, wide)
+        ids = lax.broadcasted_iota(jnp.int32, (SIDE, wide), 1) + first
+        total = jnp.zeros((SIDE, wide), jnp.float32)
+        for k in range(K):
+            total = total + jnp.where(column_ref[:, k : k + 1] == ids, 1.0, 0.0)
+        tally_ref[:, pl.ds(first, wide)] = total.astype(jnp.bfloat16)
+        return carry
+
+    lax.fori_loop(0, R_DEV * BR // wide, count, 0)
+
+
+def side(targets, columns, codes, scales, weight, bias):
+    same = lambda i: (0, 0)
+    return pl.pallas_call(
+        side_kernel,
+        grid=(TGT // SIDE,),
+        in_specs=[
+            pl.BlockSpec((SIDE, 1), lambda i: (i, 0)),
+            pl.BlockSpec((SIDE, K), lambda i: (i, 0)),
+            pl.BlockSpec((NODE_DEV, F), same),
+            pl.BlockSpec((1, NODE_DEV), same),
+            pl.BlockSpec((F, H), same),
+            pl.BlockSpec((1, H), same),
+        ],
+        out_specs=[
+            pl.BlockSpec((F, SIDE), lambda i: (0, i)),
+            pl.BlockSpec((SIDE, H), lambda i: (i, 0)),
+            pl.BlockSpec((SIDE, R_DEV * BR), lambda i: (i, 0)),
+        ],
+        out_shape=[
+            jax.ShapeDtypeStruct((F, TGT), jnp.bfloat16),
+            jax.ShapeDtypeStruct((TGT, H), jnp.float32),
+            jax.ShapeDtypeStruct((TGT, R_DEV * BR), jnp.bfloat16),
+        ],
+        compiler_params=pltpu.CompilerParams(vmem_limit_bytes=24 << 20),
+        name="side",
+    )(targets[:, None], columns, codes, scales[None, :], weight, bias[None, :])
 
 
 MEAN_STEPS = 4
@@ -184,17 +235,17 @@
         first = core_ref[0] == 0
         grad_self = jnp.dot(x_t_ref[...], delta, preferred_element_type=jnp.float32)
         grad_neigh = jnp.dot(mean_t[...], delta, preferred_element_type=jnp.float32)
-        tail = jnp.broadcast_to(bias_term, (RBP - RB, HB)).astype(jnp.bfloat16)
+        tail = jnp.broadcast_to(bias_term, (RBP - RB, HB))
         for ref, value in (
             (kept_ref, jnp.where(first, grad_self, grad_neigh)),
             (given_ref, jnp.where(first, grad_neigh, grad_self)),
         ):
-            value = value.astype(jnp.bfloat16)
             for c in range(HB // 128):
                 lanes = slice(c * 128, (c + 1) * 128)
                 for r in range(8):
-                    ref[r, c, :RB, :] = value[r * RB : (r + 1) * RB, lanes]
-                    ref[r, c, RB:, :] = tail[:, lanes]
+                    ref[r, c] = jnp.concatenate(
+                        [value[r * RB : (r + 1) * RB, lanes], tail[:, lanes]], axis=0
+                    ).astype(jnp.bfloat16)
 
 
 def layer(core, got, tally, pre_self, x_t, weight_neigh, cotangent):
@@ -299,22 +350,18 @@
     own = exchange(stripes.reshape(CHIP_COUNT, NB_DEV, HALF), CHIPS)
     own = own.reshape(TABLE, HALF)
     sister = lax.ppermute(own, "core", SWAP)
-    got = exchange(gather(wanted, own, sister), ALL)
-
-    self_codes = select_rows(target_rows, NODE_DEV, node_codes)
-    self_scales = select_rows(target_rows, NODE_DEV, node_scales[:, None])
-    x_self = (self_codes.astype(jnp.float32) * self_scales.astype(jnp.float32)).astype(jnp.bfloat16)
-    pre_self = jnp.dot(x_self, weight_self, preferred_element_type=jnp.float32) + bias
+    send = gather(wanted, own, sister)
+    send, neighbours, target_rows = lax.optimization_barrier((send, neighbours, target_rows))
+    got = exchange(send, ALL)
+
     block, row = neighbours // BR, neighbours % BR
     column = (row // 8) * 1024 + (block // RQ) * 512 + (row % 8) * RQ + block % RQ
-    ids = jnp.arange(R_DEV * BR, dtype=jnp.int32)
-    tally = jnp.zeros((TGT, R_DEV * BR), jnp.float32)
-    for step in range(K):
-        tally = tally + (column[:, step][:, None] == ids[None, :]).astype(jnp.float32)
-
+    x_t, pre_self, tally = side(
+        target_rows, column, node_codes, node_scales.astype(jnp.float32), weight_self, bias
+    )
     which = core.reshape(1).astype(jnp.int32)
     hidden, kept, given = layer(
-        which, got, tally.astype(jnp.bfloat16), pre_self, x_self.T, weight_neigh, cotangent
+        which, got, tally, pre_self, x_t, weight_neigh, cotangent
     )
     return (hidden,) + sum_over_devices(kept, given, which)
 

time: 276 us -> 274 us (level)
  Pallas kernels: 46.2 us -> 88.8 us
  other arithmetic: 27.9 us -> 4.59 us
  waiting for transfers between devices: 45.2 us -> 26.3 us
  local copies, waits for them, and re-layouts: 6.1 us -> 17.8 us
  matrix products: 11.2 us -> 0 us
  blocking collectives: 126 us -> 123 us
    pallas_call x0 -> x1, Pallas kernels: none -> 42.7 us  [side(): pl.pallas_call(side_kernel, grid=(TGT // SIDE,), in_specs=[pl.BlockSpec((...]
    convert_element_type x2 -> x1, other arithmetic: 26 us -> 1.29 us  [local(): stripes = make_stripes(node_codes, node_scales.astype(jnp.float32))]
    all_to_all x1, waiting for transfers between devices: 38.1 us -> 19.6 us  [exchange(): return lax.all_to_all(array, axes, split_axis=0, concat_axis=0, tiled=True)]
    dot_general x3 -> x0, matrix products: 11.2 us -> none  [the longest x2 7.37 us: select_rows(): jnp.dot(picker, source, preferred_element_type=jnp.float32)]
    unnamed x29 -> x30, local copies, waits for them, and re-layouts: 5.73 us -> 15.4 us
  transfers between devices with their start and end apart: 4 -> 4, of which waited for: 3 -> 3; matrix products, arithmetic and copies ran while one was open for 14% -> 2% of each run, Pallas kernels for 0% -> 16%
where the time goes in v5:
time: 274 us
  blocking collectives  123 us (45%)
  Pallas kernels  88.8 us (32%)
  waiting for transfers between devices  26.3 us (10%)
  local copies, waits for them, and re-layouts  17.8 us (6%)
  starting transfers between devices  12 us (4%)
  other arithmetic  4.59 us (2%)
    all_to_all x4, blocking collectives, exchange(): return lax.all_to_all(array, axes, split_axis=0, concat_axis=0, tiled=True)  123 us
    pallas_call x1, Pallas kernels, side(): pl.pallas_call(side_kernel, grid=(TGT // SIDE,), in_specs=[pl.BlockSpec((...  42.7 us
    pallas_call x1, Pallas kernels, layer(): pl.pallas_call(layer_kernel, grid_spec=pltpu.PrefetchScalarGridSpec(num_s...  20.6 us
    all_to_all x1, waiting for transfers between devices, exchange(): return lax.all_to_all(array, axes, split_axis=0, concat_axis=0, tiled=True)  19.6 us
    unnamed x30, local copies, waits for them, and re-layouts  15.4 us
    pallas_call x1, Pallas kernels, gather(): pl.pallas_call(gather_kernel, grid_spec=pltpu.PrefetchScalarGridSpec(num_...  15.2 us
    pallas_call x1, Pallas kernels, make_stripes(): pl.pallas_call(stripe_kernel, grid=(6,), in_specs=[pl.BlockSpec(memory_sp...  7.3 us
    all_to_all x1, starting transfers between devices, exchange(): return lax.all_to_all(array, axes, split_axis=0, concat_axis=0, tiled=True)  5.89 us
  transfers between devices with their start and end apart: 4, of which 3 were waited for; matrix products, arithmetic and copies ran while one was open for 2% of the time, Pallas kernels for 16%

profile of v5, /device:TPU:1, one launch (start us, length us, event | category | flops | bytes accessed | tf_op | source)
XLA Modules:
  0.0 273.7 jit_solution(2136408265401272584)
XLA Ops:
  0.6 1.3 fusion.23
  1.9 7.3 %make_stripes.1 = bf16[32,2,64,384]{3,2,1,0:T(8,128)(2,1)} custom-call(bf16[2048,768]{1,0:T(8,128)(2,1)} %codes_ref.3, f32[16,128]{1,0:T(8,128)} %get-tuple-element.29.scales_ref), custom_call_target="tpu_custom_call" | custom-call | tf_op jit(solution)/shard_map/make_stripes/pallas_call | solution.py:55
  9.2 51.6 %all_to_all.31 = bf16[64,64,384]{2,1,0:T(8,128)(2,1)S(1)} all-to-all(bf16[64,64,384]{2,1,0:T(8,128)(2,1)} %bitcast.43), channel_id=1, replica_groups=mesh['z'=4,'core'=2,'x'=4,'y'=4] {'z','x','y'}, dimensions={0} | all-to-all | bytes 6291456 | tf_op jit(solution)/shard_map/all_to_all | solution.py:29
  60.9 2.5 collective-permute-start
  63.5 13.2 %all_to_all.32 = s32[128,1,64]{2,1,0:T(1,128)S(1)} all-to-all(s32[128,1,64]{2,1,0:T(1,128)S(1)} %bitcast.44), channel_id=1, replica_groups=mesh['z'=4,'core'=2,'x'=4,'y'=4] {'z','core','x','y'}, dimensions={0} | all-to-all | bytes 65536 | tf_op jit(solution)/shard_map/all_to_all | solution.py:29
  76.7 15.2 %gather_rows.1 = bf16[128,64,384]{2,1,0:T(8,128)(2,1)} custom-call(s32[128,64]{1,0:T(8,128)S(1)} %bitcast.39, bf16[4096,384]{1,0:T(8,128)(2,1)S(1)} %bitcast.36, bf16[4096,384]{1,0:T(8,128)(2,1)} %collective-permute-done.sister_ref), custom_call_target="tpu_custom_call" | custom-call | tf_op jit(solution)/shard_map/gather_rows/pallas_call | solution.py:107
  91.8 5.9 %all-to-all-start.2 = ((bf16[128,64,384]{2,1,0:T(8,128)(2,1)}), bf16[128,64,384]{2,1,0:T(8,128)(2,1)}, u32[]{:S(2)}, u32[]{:S(2)}) async-start(bf16[128,64,384]{2,1,0:T(8,128)(2,1)} %gather_rows.1), calls=%async_computation.2 | async-start | bytes 12582912 | tf_op jit(solution)/shard_map/all_to_all | solution.py:29
  99.8 2.5 fusion.4.column_ref
  103.3 1.4 copy-done.6
  104.8 42.7 %side.1 = (bf16[768,1024]{1,0:T(8,128)(2,1)S(1)}, f32[1024,1024]{1,0:T(8,128)S(1)}, bf16[1024,4096]{1,0:T(8,128)(2,1)S(1)}) custom-call(s32[1024,1]{1,0:T(8,128)S(1)} %copy-done.4, s32[1024,10]{1,0:T(8,128)S(1)} %fusion.4.column_ref, bf16[2048,768]{1,0:T(8,128)(2,1)S(1)} %copy-done, f32[1,2048]{1,0:T(1,128)S(1)} %bitcast.40, ...), custom_call_target="tpu_custom_call" | custom-call | tf_op jit(solution)/shard_map/side/pallas_call | solution.py:159
  147.4 3.2 %copy-done.1 = bf16[1024,4096]{1,0:T(8,128)(2,1)} copy-done((bf16[1024,4096]{1,0:T(8,128)(2,1)}, bf16[1024,4096]{1,0:T(8,128)(2,1)S(1)}, u32[]{:S(2)}) %copy-start.1) | copy-done | bytes 8388632
  150.7 2.0 copy-done.2
  153.8 19.6 %all-to-all-done.2.got_ref = bf16[128,64,384]{2,1,0:T(8,128)(2,1)} async-done(((bf16[128,64,384]{2,1,0:T(8,128)(2,1)}), bf16[128,64,384]{2,1,0:T(8,128)(2,1)}, u32[]{:S(2)}, u32[]{:S(2)}) %all-to-all-start.2) | async-done | bytes 6291488 | tf_op jit(solution)/shard_map/all_to_all | solution.py:29
  173.4 2.2 copy-done.3
  175.6 1.6 copy-done.5
  177.2 1.4 copy-done.7
  178.6 1.4 copy-done.9
  180.0 20.6 %layer.1 = (bf16[1024,1024]{1,0:T(8,128)(2,1)}, bf16[8,8,104,128]{3,2,1,0:T(8,128)(2,1)S(1)}, bf16[8,8,104,128]{3,2,1,0:T(8,128)(2,1)S(1)}) custom-call(s32[1]{0:T(128)} %bitcast.core_ref, bf16[128,64,384]{2,1,0:T(8,128)(2,1)} %all-to-all-done.2.got_ref, bf16[1024,4096]{1,0:T(8,128)(2,1)} %copy-done.1, f32[1024,1024]{1,0:T(8,128)S(1)} %copy-done.3, ...), custom_call_target="tpu_custom_call" | custom-call | tf_op jit(solution)/shard_map/layer/pallas_call | solution.py:256
  200.7 3.5 %collective-permute-done.1 = bf16[64,104,128]{2,1,0:T(8,128)(2,1)S(1)} collective-permute-done((bf16[64,104,128]{2,1,0:T(8,128)(2,1)S(1)}, bf16[64,104,128]{2,1,0:T(8,128)(2,1)S(1)}, u32[]{:S(2)}, u32[]{:S(2)}) %collective-permute-start.1) | collective-permute-done | bytes 1703968 | tf_op jit(solution)/shard_map/ppermute | solution.py:325
  204.7 30.1 %all_to_all.33 = bf16[64,104,128]{2,1,0:T(8,128)(2,1)S(1)} all-to-all(bf16[64,104,128]{2,1,0:T(8,128)(2,1)S(1)} %fusion), channel_id=1, replica_groups=mesh['z'=4,'core'=2,'x'=4,'y'=4] {'z','x','y'}, dimensions={0} | all-to-all | bytes 3407872 | tf_op jit(solution)/shard_map/all_to_all | solution.py:29
  235.3 28.5 %all_to_all.34 = bf16[64,104,128]{2,1,0:T(8,128)(2,1)S(1)} all-to-all(bf16[64,104,128]{2,1,0:T(8,128)(2,1)S(1)} %broadcast_in_dim.27), channel_id=1, replica_groups=mesh['z'=4,'core'=2,'x'=4,'y'=4] {'z','x','y'}, dimensions={0} | all-to-all | bytes 3407872 | tf_op jit(solution)/shard_map/all_to_all | solution.py:29
  263.8 3.6 %collective-permute-start.2 = (bf16[64,104,128]{2,1,0:T(8,128)(2,1)S(1)}, bf16[64,104,128]{2,1,0:T(8,128)(2,1)S(1)}, u32[]{:S(2)}, u32[]{:S(2)}) collective-permute-start(bf16[64,104,128]{2,1,0:T(8,128)(2,1)S(1)} %all_to_all.34), channel_id=1, source_target_pairs={{0,16},{16,0},{1,17},{17,1},{2,18},{18,2},{3,19},{19,3},{4,20},{20... | collective-permute-start | bytes 5111816 | tf_op jit(solution)/shard_map/ppermute | solution.py:330
  267.3 3.2 %collective-permute-done.2 = bf16[64,104,128]{2,1,0:T(8,128)(2,1)S(1)} collective-permute-done((bf16[64,104,128]{2,1,0:T(8,128)(2,1)S(1)}, bf16[64,104,128]{2,1,0:T(8,128)(2,1)S(1)}, u32[]{:S(2)}, u32[]{:S(2)}) %collective-permute-start.2) | collective-permute-done | bytes 1703968 | tf_op jit(solution)/shard_map/ppermute | solution.py:330
  270.6 3.1 %unpack.1 = (f32[768,1024]{1,0:T(8,128)}, f32[768,1024]{1,0:T(8,128)}, f32[1,1024]{1,0:T(1,128)}) custom-call(s32[1]{0:T(128)} %bitcast.core_ref, bf16[8,8,104,128]{3,2,1,0:T(8,128)(2,1)S(1)} %bitcast.37, bf16[8,8,104,128]{3,2,1,0:T(8,128)(2,1)S(1)} %bitcast.38), custom_call_target="tpu_custom_call" | custom-call | tf_op jit(solution)/shard_map/unpack/pallas_call | solution.py:301
  (33 shorter events, 5.5 us)
Async XLA Ops:
  9.2 54.1 %copy-start.13 = (s32[128]{0:T(128)S(1)}, s32[128]{0:T(128)}, u32[]{:S(2)}) copy-start(s32[128]{0:T(128)} %param.14) | copy-start | bytes 1540
  9.2 54.1 %copy-start.14 = (s32[128,1]{0,1:T(1,128)S(1)}, s32[128,1]{0,1:T(1,128)}, u32[]{:S(2)}) copy-start(s32[128,1]{0,1:T(1,128)} %param.13) | copy-start | bytes 1540
  60.9 15.8 %collective-permute-start = (bf16[4096,384]{1,0:T(8,128)(2,1)S(1)}, bf16[4096,384]{1,0:T(8,128)(2,1)}, u32[]{:S(2)}, u32[]{:S(2)}) collective-permute-start(bf16[4096,384]{1,0:T(8,128)(2,1)S(1)} %bitcast.35), channel_id=1, source_target_pairs={{0,16},{16,0},{1,17},{17,1},{2,18},{18,2},{3,19},{19,3},{4,20},{20... | collective-permute-start | bytes 9437192 | tf_op jit(solution)/shard_map/ppermute | solution.py:352
  91.8 5.9 %copy-start.12 = (s32[1024]{0:T(1024)S(1)}, s32[1024]{0:T(1024)}, u32[]{:S(2)}) copy-start(s32[1024]{0:T(1024)} %param.12) | copy-start | bytes 12292
  91.8 7.0 %copy-start.11 = (s32[1024,10]{0,1:T(8,128)S(1)}, s32[1024,10]{0,1:T(8,128)}, u32[]{:S(2)}) copy-start(s32[1024,10]{0,1:T(8,128)} %param.15) | copy-start | bytes 122884
  91.8 10.4 %copy-start = (bf16[2048,768]{1,0:T(8,128)(2,1)S(1)}, bf16[2048,768]{1,0:T(8,128)(2,1)}, u32[]{:S(2)}) copy-start(bf16[2048,768]{1,0:T(8,128)(2,1)} %codes_ref.3) | copy-start | bytes 9437188
  91.8 81.6 %all-to-all-start.2 = ((bf16[128,64,384]{2,1,0:T(8,128)(2,1)}), bf16[128,64,384]{2,1,0:T(8,128)(2,1)}, u32[]{:S(2)}, u32[]{:S(2)}) async-start(bf16[128,64,384]{2,1,0:T(8,128)(2,1)} %gather_rows.1), calls=%async_computation.2 | async-start | bytes 12582912 | tf_op jit(solution)/shard_map/all_to_all | solution.py:29
  97.7 4.6 %copy-start.10 = (f32[1024]{0:T(1024)S(1)}, f32[1024]{0:T(1024)}, u32[]{:S(2)}) copy-start(f32[1024]{0:T(1024)} %param.18) | copy-start | bytes 12292
  102.3 1.0 copy-start.4
  103.3 1.4 copy-start.6
  147.4 3.2 %copy-start.1 = (bf16[1024,4096]{1,0:T(8,128)(2,1)}, bf16[1024,4096]{1,0:T(8,128)(2,1)S(1)}, u32[]{:S(2)}) copy-start(bf16[1024,4096]{1,0:T(8,128)(2,1)S(1)} %get-tuple-element.19.tally_ref) | copy-start | bytes 25165828
  150.7 2.0 copy-start.2
  152.7 1.1 copy-start.8
  173.4 2.2 copy-start.3
  175.6 1.6 copy-start.5
  177.2 1.4 copy-start.7
  178.6 1.4 copy-start.9
  200.6 3.6 %collective-permute-start.1 = (bf16[64,104,128]{2,1,0:T(8,128)(2,1)S(1)}, bf16[64,104,128]{2,1,0:T(8,128)(2,1)S(1)}, u32[]{:S(2)}, u32[]{:S(2)}) collective-permute-start(bf16[64,104,128]{2,1,0:T(8,128)(2,1)S(1)} %bitcast.42), channel_id=1, source_target_pairs={{0,16},{16,0},{1,17},{17,1},{2,18},{18,2},{3,19},{19,3},{4,20},{20... | collective-permute-start | bytes 5111816 | tf_op jit(solution)/shard_map/ppermute | solution.py:325
  263.8 6.8 %collective-permute-start.2 = (bf16[64,104,128]{2,1,0:T(8,128)(2,1)S(1)}, bf16[64,104,128]{2,1,0:T(8,128)(2,1)S(1)}, u32[]{:S(2)}, u32[]{:S(2)}) collective-permute-start(bf16[64,104,128]{2,1,0:T(8,128)(2,1)S(1)} %all_to_all.34), channel_id=1, source_target_pairs={{0,16},{16,0},{1,17},{17,1},{2,18},{18,2},{3,19},{19,3},{4,20},{20... | collective-permute-start | bytes 5111816 | tf_op jit(solution)/shard_map/ppermute | solution.py:330

commit v6 on v5

--- a/solution.py
+++ b/solution.py
@@ -77,13 +77,26 @@
 SLOT = 4
 
 
-def gather_kernel(wanted_ref, own_ref, sister_ref, out_ref, table, picked):
+STAGES = 8
+STAGE = 2 * TABLE // STAGES
+
+
+def gather_kernel(wanted_ref, own_ref, sister_ref, out_ref, table, picked, narrow, sem):
     @pl.when(pl.program_id(0) == 0)
     def _():
-        for part, source in enumerate((own_ref, sister_ref)):
+        copies = []
+        for n in range(STAGES):
+            source = own_ref if n < STAGES // 2 else sister_ref
+            start = n % (STAGES // 2) * STAGE
+            copies.append(
+                pltpu.make_async_copy(source.at[pl.ds(start, STAGE)], narrow.at[n], sem.at[n])
+            )
+            copies[-1].start()
+        for n in range(STAGES):
+            copies[n].wait()
             for k in range(3):
-                table[pl.ds(part * TABLE * SLOT + k, TABLE, stride=SLOT), :] = source[
-                    :, k * 128 : (k + 1) * 128
+                table[pl.ds(n * STAGE * SLOT + k, STAGE, stride=SLOT), :] = narrow[
+                    n, :, k * 128 : (k + 1) * 128
                 ].astype(jnp.float32)
 
     first = pl.program_id(0) * GROUP
@@ -110,13 +123,15 @@
             num_scalar_prefetch=1,
             grid=(DEVICES // GROUP,),
             in_specs=[
-                pl.BlockSpec((TABLE, HALF), lambda i, w: (0, 0), pipeline_mode=pl.Buffered(1)),
-                pl.BlockSpec((TABLE, HALF), lambda i, w: (0, 0), pipeline_mode=pl.Buffered(1)),
+                pl.BlockSpec(memory_space=pl.ANY),
+                pl.BlockSpec(memory_space=pl.ANY),
             ],
             out_specs=pl.BlockSpec((GROUP, RQ, HALF), lambda i, w: (i, 0, 0)),
             scratch_shapes=[
                 pltpu.VMEM((2 * TABLE * SLOT, 128), jnp.float32),
                 pltpu.VMEM((2 * RQ * SLOT, 128), jnp.float32),
+                pltpu.VMEM((STAGES, STAGE, HALF), jnp.bfloat16),
+                pltpu.SemaphoreType.DMA((STAGES,)),
             ],
         ),
         out_shape=pltpu.HBM((DEVICES, RQ, HALF), jnp.bfloat16),
@@ -183,102 +198,132 @@
 
 
 MEAN_STEPS = 4
-COLS = 2 * BR * R_DEV // 2 // MEAN_STEPS
+COLS = R_DEV * BR // MEAN_STEPS
+PIECES = DEVICES // MEAN_STEPS
+LATE = H // HB
 
 
 def layer_kernel(
     core_ref, got_ref, tally_ref, pre_ref, x_t_ref, weight_ref, cot_ref,
-    hidden_ref, kept_ref, given_ref, acc, mean, mean_t,
+    hidden_ref, kept_ref, given_ref,
+    got, tally, pre_self, x_t, weight, cot, hidden, kept, given, acc, mean, mean_t, sem, out_sem,
 ):
-    step = pl.program_id(0)
-
-    @pl.when(step < MEAN_STEPS)
-    def _():
+    count = 0
+
+    def fetch(source, target):
+        nonlocal count
+        copy = pltpu.make_async_copy(source, target, sem.at[count])
+        count += 1
+        copy.start()
+        return copy
+
+    early = []
+    for n in range(MEAN_STEPS):
+        early.append(
+            (
+                fetch(got_ref.at[pl.ds(n * PIECES, PIECES)], got.at[n]),
+                fetch(tally_ref.at[:, pl.ds(n * COLS, COLS)], tally.at[n]),
+            )
+        )
+    late = [
+        fetch(source, target)
+        for source, target in (
+            (weight_ref, weight), (pre_ref, pre_self), (cot_ref, cot), (x_t_ref, x_t)
+        )
+    ]
+    for n in range(MEAN_STEPS):
+        for copy in early[n]:
+            copy.wait()
         rows = jnp.concatenate(
             [
-                jnp.concatenate([got_ref[2 * e + half] for e in range(COLS // RQ)], axis=0)
+                jnp.concatenate([got[n, 2 * e + half] for e in range(COLS // RQ)], axis=0)
                 for half in range(2)
             ],
             axis=1,
         )
-        part = jnp.dot(tally_ref[...], rows, preferred_element_type=jnp.float32)
-
-        @pl.when(step == 0)
-        def _():
+        part = jnp.dot(tally[n], rows, preferred_element_type=jnp.float32)
+        if n == 0:
             acc[...] = part
-
-        @pl.when(step > 0)
-        def _():
+        elif n < MEAN_STEPS - 1:
             acc[...] += part
-
-    @pl.when(step == MEAN_STEPS - 1)
-    def _():
-        value = (acc[...] / K).astype(jnp.bfloat16)
-        mean[...] = value
-        mean_t[...] = value.T
-
-    @pl.when(step >= MEAN_STEPS)
-    def _():
-        pre = pre_ref[...] + jnp.dot(
-            mean[...], weight_ref[...], preferred_element_type=jnp.float32
+        else:
+            value = ((acc[...] + part) / K).astype(jnp.bfloat16)
+            mean[...] = value
+            mean_t[...] = value.T
+    for copy in late:
+        copy.wait()
+    first = core_ref[0] == 0
+    leaving = []
+    for n in range(LATE):
+        block = slice(n * HB, (n + 1) * HB)
+        pre = pre_self[:, block] + jnp.dot(
+            mean[...], weight[:, block], preferred_element_type=jnp.float32
         )
         square = pre * pre
         tangent = jnp.tanh(0.7978845608 * (pre + 0.044715 * pre * square))
         rest = 1.0 + tangent
-        hidden_ref[...] = (0.5 * pre * rest).astype(jnp.bfloat16)
+        hidden[:, block] = (0.5 * pre * rest).astype(jnp.bfloat16)
         slope = 0.5 * rest + 0.5 * pre * (1.0 - tangent * tangent) * 0.7978845608 * (
             1.0 + 3.0 * 0.044715 * square
         )
-        wide = cot_ref[...].astype(jnp.float32) * slope
-        delta = wide.astype(jnp.bfloat16)
+        delta = (cot[:, block].astype(jnp.float32) * slope).astype(jnp.bfloat16)
         bias_term = jnp.sum(delta.astype(jnp.float32), axis=0, keepdims=True)
-        first = core_ref[0] == 0
-        grad_self = jnp.dot(x_t_ref[...], delta, preferred_element_type=jnp.float32)
+        grad_self = jnp.dot(x_t[...], delta, preferred_element_type=jnp.float32)
         grad_neigh = jnp.dot(mean_t[...], delta, preferred_element_type=jnp.float32)
         tail = jnp.broadcast_to(bias_term, (RBP - RB, HB))
         for ref, value in (
-            (kept_ref, jnp.where(first, grad_self, grad_neigh)),
-            (given_ref, jnp.where(first, grad_neigh, grad_self)),
+            (given, jnp.where(first, grad_neigh, grad_self)),
+            (kept, jnp.where(first, grad_self, grad_neigh)),
         ):
             for c in range(HB // 128):
                 lanes = slice(c * 128, (c + 1) * 128)
                 for r in range(8):
-                    ref[r, c] = jnp.concatenate(
+                    ref[n, r, c] = jnp.concatenate(
                         [value[r * RB : (r + 1) * RB, lanes], tail[:, lanes]], axis=0
                     ).astype(jnp.bfloat16)
+        chunk = pl.ds(n * (HB // 128), HB // 128)
+        for e, (source, target) in enumerate(
+            (
+                (given.at[n], given_ref.at[:, chunk]),
+                (kept.at[n], kept_ref.at[:, chunk]),
+                (hidden.at[:, pl.ds(n * HB, HB)], hidden_ref.at[:, pl.ds(n * HB, HB)]),
+            )
+        ):
+            copy = pltpu.make_async_copy(source, target, out_sem.at[3 * n + e])
+            copy.start()
+            leaving.append(copy)
+    for copy in leaving:
+        copy.wait()
 
 
 def layer(core, got, tally, pre_self, x_t, weight_neigh, cotangent):
-    last = MEAN_STEPS - 1
-    early = lambda i, w: jnp.minimum(i, last)
-    late = lambda i, w: jnp.maximum(i - MEAN_STEPS, 0)
-    term = pl.BlockSpec((8, HB // 128, RBP, 128), lambda i, w: (0, late(i, w), 0, 0))
+    whole = pl.BlockSpec(memory_space=pl.ANY)
     return pl.pallas_call(
         layer_kernel,
-        grid_spec=pltpu.PrefetchScalarGridSpec(
-            num_scalar_prefetch=1,
-            grid=(MEAN_STEPS + H // HB,),
-            in_specs=[
-                pl.BlockSpec((DEVICES // MEAN_STEPS, RQ, HALF), lambda i, w: (early(i, w), 0, 0)),
-                pl.BlockSpec((TGT, COLS), lambda i, w: (0, early(i, w))),
-                pl.BlockSpec((TGT, HB), lambda i, w: (0, late(i, w))),
-                pl.BlockSpec((F, TGT), lambda i, w: (0, 0)),
-                pl.BlockSpec((F, HB), lambda i, w: (0, late(i, w))),
-                pl.BlockSpec((TGT, HB), lambda i, w: (0, late(i, w))),
-            ],
-            out_specs=[pl.BlockSpec((TGT, HB), lambda i, w: (0, late(i, w))), term, term],
-            scratch_shapes=[
-                pltpu.VMEM((TGT, F), jnp.float32),
-                pltpu.VMEM((TGT, F), jnp.bfloat16),
-                pltpu.VMEM((F, TGT), jnp.bfloat16),
-            ],
-        ),
+        in_specs=[pl.BlockSpec(memory_space=pltpu.SMEM)] + [whole] * 6,
+        out_specs=[whole] * 3,
         out_shape=[
             jax.ShapeDtypeStruct((TGT, H), jnp.bfloat16),
             jax.ShapeDtypeStruct((8, 8, RBP, 128), jnp.bfloat16),
             jax.ShapeDtypeStruct((8, 8, RBP, 128), jnp.bfloat16),
         ],
-        compiler_params=pltpu.CompilerParams(vmem_limit_bytes=28 << 20),
+        scratch_shapes=[
+            pltpu.VMEM((MEAN_STEPS, PIECES, RQ, HALF), jnp.bfloat16),
+            pltpu.VMEM((MEAN_STEPS, TGT, COLS), jnp.bfloat16),
+            pltpu.VMEM((TGT, H), jnp.float32),
+            pltpu.VMEM((F, TGT), jnp.bfloat16),
+            pltpu.VMEM((F, H), jnp.bfloat16),
+            pltpu.VMEM((TGT, H), jnp.bfloat16),
+            pltpu.VMEM((TGT, H), jnp.bfloat16),
+            pltpu.VMEM((LATE, 8, HB // 128, RBP, 128), jnp.bfloat16),
+            pltpu.VMEM((LATE, 8, HB // 128, RBP, 128), jnp.bfloat16),
+            pltpu.VMEM((TGT, F), jnp.float32),
+            pltpu.VMEM((TGT, F), jnp.bfloat16),
+            pltpu.VMEM((F, TGT), jnp.bfloat16),
+            pltpu.SemaphoreType.DMA((2 * MEAN_STEPS + 4,)),
+            pltpu.SemaphoreType.DMA((3 * LATE,)),
+        ],
+        compiler_params=pltpu.CompilerParams(vmem_limit_bytes=58 << 20),
         name="layer",
     )(core, got, tally, pre_self, x_t, weight_neigh, cotangent)
 

time: 274 us -> 269 us (0.982)
  local copies, waits for them, and re-layouts: 17.8 us -> 11.3 us
    unnamed x30 -> x22, local copies, waits for them, and re-layouts: 15.4 us -> 8.89 us
where the time goes in v6:
time: 269 us
  blocking collectives  123 us (46%)
  Pallas kernels  88.9 us (33%)
  waiting for transfers between devices  26.3 us (10%)
  starting transfers between devices  12.1 us (4%)
  local copies, waits for them, and re-layouts  11.3 us (4%)
  other arithmetic  5.93 us (2%)
    all_to_all x4, blocking collectives, exchange(): return lax.all_to_all(array, axes, split_axis=0, concat_axis=0, tiled=True)  123 us
    pallas_call x1, Pallas kernels, side(): pl.pallas_call(side_kernel, grid=(TGT // SIDE,), in_specs=[pl.BlockSpec((...  42.9 us
    pallas_call x1, Pallas kernels, layer(): pl.pallas_call(layer_kernel, in_specs=[pl.BlockSpec(memory_space=pltpu.SM...  21.8 us
    all_to_all x1, waiting for transfers between devices, exchange(): return lax.all_to_all(array, axes, split_axis=0, concat_axis=0, tiled=True)  19.4 us
    pallas_call x1, Pallas kernels, gather(): pl.pallas_call(gather_kernel, grid_spec=pltpu.PrefetchScalarGridSpec(num_...  13.8 us
    unnamed x22, local copies, waits for them, and re-layouts  8.89 us
    pallas_call x1, Pallas kernels, make_stripes(): pl.pallas_call(stripe_kernel, grid=(6,), in_specs=[pl.BlockSpec(memory_sp...  7.3 us
    all_to_all x1, starting transfers between devices, exchange(): return lax.all_to_all(array, axes, split_axis=0, concat_axis=0, tiled=True)  5.85 us
  transfers between devices with their start and end apart: 4, of which 3 were waited for; matrix products, arithmetic and copies ran while one was open for 2% of the time, Pallas kernels for 16%

profile of v6, /device:TPU:1, one launch (start us, length us, event | category | flops | bytes accessed | tf_op | source)
XLA Modules:
  0.0 268.7 jit_solution(13210111135075047718)
XLA Ops:
  0.6 1.3 fusion.23
  1.9 7.3 %make_stripes.1 = bf16[32,2,64,384]{3,2,1,0:T(8,128)(2,1)} custom-call(bf16[2048,768]{1,0:T(8,128)(2,1)} %codes_ref.3, f32[16,128]{1,0:T(8,128)} %get-tuple-element.29.scales_ref), custom_call_target="tpu_custom_call" | custom-call | tf_op jit(solution)/shard_map/make_stripes/pallas_call | solution.py:55
  9.2 51.6 %all_to_all.31 = bf16[64,64,384]{2,1,0:T(8,128)(2,1)S(1)} all-to-all(bf16[64,64,384]{2,1,0:T(8,128)(2,1)} %bitcast.42), channel_id=1, replica_groups=mesh['z'=4,'core'=2,'x'=4,'y'=4] {'z','x','y'}, dimensions={0} | all-to-all | bytes 6291456 | tf_op jit(solution)/shard_map/all_to_all | solution.py:29
  60.9 2.5 collective-permute-start
  63.5 13.2 %all_to_all.32 = s32[128,1,64]{2,1,0:T(1,128)S(1)} all-to-all(s32[128,1,64]{2,1,0:T(1,128)S(1)} %bitcast.43), channel_id=1, replica_groups=mesh['z'=4,'core'=2,'x'=4,'y'=4] {'z','core','x','y'}, dimensions={0} | all-to-all | bytes 65536 | tf_op jit(solution)/shard_map/all_to_all | solution.py:29
  76.7 13.8 %gather_rows.1 = bf16[128,64,384]{2,1,0:T(8,128)(2,1)} custom-call(s32[128,64]{1,0:T(8,128)S(1)} %bitcast.39, bf16[4096,384]{1,0:T(8,128)(2,1)S(1)} %bitcast.36, bf16[4096,384]{1,0:T(8,128)(2,1)} %collective-permute-done.sister_ref), custom_call_target="tpu_custom_call" | custom-call | tf_op jit(solution)/shard_map/gather_rows/pallas_call | solution.py:120
  90.6 5.9 %all-to-all-start.2 = ((bf16[128,64,384]{2,1,0:T(8,128)(2,1)}), bf16[128,64,384]{2,1,0:T(8,128)(2,1)}, u32[]{:S(2)}, u32[]{:S(2)}) async-start(bf16[128,64,384]{2,1,0:T(8,128)(2,1)} %gather_rows.1), calls=%async_computation.2 | async-start | bytes 12582912 | tf_op jit(solution)/shard_map/all_to_all | solution.py:29
  96.5 1.0 copy.27.target_ref
  98.5 2.5 fusion.4.column_ref
  101.0 1.0 copy-done.3
  102.0 1.4 copy-done.4
  103.4 42.9 %side.1 = (bf16[768,1024]{1,0:T(8,128)(2,1)S(1)}, f32[1024,1024]{1,0:T(8,128)S(1)}, bf16[1024,4096]{1,0:T(8,128)(2,1)S(1)}) custom-call(s32[1024,1]{1,0:T(8,128)S(1)} %copy-done.3, s32[1024,10]{1,0:T(8,128)S(1)} %fusion.4.column_ref, bf16[2048,768]{1,0:T(8,128)(2,1)S(1)} %copy-done, f32[1,2048]{1,0:T(1,128)S(1)} %bitcast.40, ...), custom_call_target="tpu_custom_call" | custom-call | tf_op jit(solution)/shard_map/side/pallas_call | solution.py:174
  146.3 3.2 %copy-done.1 = bf16[1024,4096]{1,0:T(8,128)(2,1)} copy-done((bf16[1024,4096]{1,0:T(8,128)(2,1)}, bf16[1024,4096]{1,0:T(8,128)(2,1)S(1)}, u32[]{:S(2)}) %copy-start.1) | copy-done | bytes 8388632
  149.5 2.0 copy-done.2
  151.5 1.2 copy-done.5
  152.7 19.4 %all-to-all-done.2.got_ref = bf16[128,64,384]{2,1,0:T(8,128)(2,1)} async-done(((bf16[128,64,384]{2,1,0:T(8,128)(2,1)}), bf16[128,64,384]{2,1,0:T(8,128)(2,1)}, u32[]{:S(2)}, u32[]{:S(2)}) %all-to-all-start.2) | async-done | bytes 6291488 | tf_op jit(solution)/shard_map/all_to_all | solution.py:29
  172.1 21.8 %layer.1 = (bf16[1024,1024]{1,0:T(8,128)(2,1)}, bf16[8,8,104,128]{3,2,1,0:T(8,128)(2,1)}, bf16[8,8,104,128]{3,2,1,0:T(8,128)(2,1)}) custom-call(s32[1]{0:T(128)} %bitcast.core_ref, bf16[128,64,384]{2,1,0:T(8,128)(2,1)} %all-to-all-done.2.got_ref, bf16[1024,4096]{1,0:T(8,128)(2,1)} %copy-done.1, f32[1024,1024]{1,0:T(8,128)} %copy-done.2, ...), custom_call_target="tpu_custom_call" | custom-call | tf_op jit(solution)/shard_map/layer/pallas_call | solution.py:301
  194.0 3.7 %collective-permute-done.1 = bf16[64,104,128]{2,1,0:T(8,128)(2,1)S(1)} collective-permute-done((bf16[64,104,128]{2,1,0:T(8,128)(2,1)}, bf16[64,104,128]{2,1,0:T(8,128)(2,1)S(1)}, u32[]{:S(2)}, u32[]{:S(2)}) %collective-permute-start.1) | collective-permute-done | bytes 1703968 | tf_op jit(solution)/shard_map/ppermute | solution.py:370
  197.8 1.9 fusion
  199.7 30.1 %all_to_all.33 = bf16[64,104,128]{2,1,0:T(8,128)(2,1)S(1)} all-to-all(bf16[64,104,128]{2,1,0:T(8,128)(2,1)S(1)} %fusion), channel_id=1, replica_groups=mesh['z'=4,'core'=2,'x'=4,'y'=4] {'z','x','y'}, dimensions={0} | all-to-all | bytes 3407872 | tf_op jit(solution)/shard_map/all_to_all | solution.py:29
  230.2 28.5 %all_to_all.34 = bf16[64,104,128]{2,1,0:T(8,128)(2,1)S(1)} all-to-all(bf16[64,104,128]{2,1,0:T(8,128)(2,1)S(1)} %broadcast_in_dim.27), channel_id=1, replica_groups=mesh['z'=4,'core'=2,'x'=4,'y'=4] {'z','x','y'}, dimensions={0} | all-to-all | bytes 3407872 | tf_op jit(solution)/shard_map/all_to_all | solution.py:29
  258.7 3.6 %collective-permute-start.2 = (bf16[64,104,128]{2,1,0:T(8,128)(2,1)S(1)}, bf16[64,104,128]{2,1,0:T(8,128)(2,1)S(1)}, u32[]{:S(2)}, u32[]{:S(2)}) collective-permute-start(bf16[64,104,128]{2,1,0:T(8,128)(2,1)S(1)} %all_to_all.34), channel_id=1, source_target_pairs={{0,16},{16,0},{1,17},{17,1},{2,18},{18,2},{3,19},{19,3},{4,20},{20... | collective-permute-start | bytes 5111816 | tf_op jit(solution)/shard_map/ppermute | solution.py:375
  262.3 3.2 %collective-permute-done.2 = bf16[64,104,128]{2,1,0:T(8,128)(2,1)S(1)} collective-permute-done((bf16[64,104,128]{2,1,0:T(8,128)(2,1)S(1)}, bf16[64,104,128]{2,1,0:T(8,128)(2,1)S(1)}, u32[]{:S(2)}, u32[]{:S(2)}) %collective-permute-start.2) | collective-permute-done | bytes 1703968 | tf_op jit(solution)/shard_map/ppermute | solution.py:375
  265.5 3.1 %unpack.1 = (f32[768,1024]{1,0:T(8,128)}, f32[768,1024]{1,0:T(8,128)}, f32[1,1024]{1,0:T(1,128)}) custom-call(s32[1]{0:T(128)} %bitcast.core_ref, bf16[8,8,104,128]{3,2,1,0:T(8,128)(2,1)S(1)} %bitcast.37, bf16[8,8,104,128]{3,2,1,0:T(8,128)(2,1)S(1)} %bitcast.38), custom_call_target="tpu_custom_call" | custom-call | tf_op jit(solution)/shard_map/unpack/pallas_call | solution.py:346
  (25 shorter events, 1.8 us)
Async XLA Ops:
  9.2 54.1 %copy-start.9 = (s32[128]{0:T(128)S(1)}, s32[128]{0:T(128)}, u32[]{:S(2)}) copy-start(s32[128]{0:T(128)} %param.14) | copy-start | bytes 1540
  9.2 54.1 %copy-start.10 = (s32[128,1]{0,1:T(1,128)S(1)}, s32[128,1]{0,1:T(1,128)}, u32[]{:S(2)}) copy-start(s32[128,1]{0,1:T(1,128)} %param.13) | copy-start | bytes 1540
  60.9 15.8 %collective-permute-start = (bf16[4096,384]{1,0:T(8,128)(2,1)S(1)}, bf16[4096,384]{1,0:T(8,128)(2,1)}, u32[]{:S(2)}, u32[]{:S(2)}) collective-permute-start(bf16[4096,384]{1,0:T(8,128)(2,1)S(1)} %bitcast.35), channel_id=1, source_target_pairs={{0,16},{16,0},{1,17},{17,1},{2,18},{18,2},{3,19},{19,3},{4,20},{20... | collective-permute-start | bytes 9437192 | tf_op jit(solution)/shard_map/ppermute | solution.py:397
  90.5 5.9 %copy-start.8 = (s32[1024]{0:T(1024)S(1)}, s32[1024]{0:T(1024)}, u32[]{:S(2)}) copy-start(s32[1024]{0:T(1024)} %param.12) | copy-start | bytes 12292
  90.5 6.9 %copy-start.7 = (s32[1024,10]{0,1:T(8,128)S(1)}, s32[1024,10]{0,1:T(8,128)}, u32[]{:S(2)}) copy-start(s32[1024,10]{0,1:T(8,128)} %param.15) | copy-start | bytes 122884
  90.6 10.4 %copy-start = (bf16[2048,768]{1,0:T(8,128)(2,1)S(1)}, bf16[2048,768]{1,0:T(8,128)(2,1)}, u32[]{:S(2)}) copy-start(bf16[2048,768]{1,0:T(8,128)(2,1)} %codes_ref.3) | copy-start | bytes 9437188
  90.6 81.5 %all-to-all-start.2 = ((bf16[128,64,384]{2,1,0:T(8,128)(2,1)}), bf16[128,64,384]{2,1,0:T(8,128)(2,1)}, u32[]{:S(2)}, u32[]{:S(2)}) async-start(bf16[128,64,384]{2,1,0:T(8,128)(2,1)} %gather_rows.1), calls=%async_computation.2 | async-start | bytes 12582912 | tf_op jit(solution)/shard_map/all_to_all | solution.py:29
  96.4 4.6 %copy-start.6 = (f32[1024]{0:T(1024)S(1)}, f32[1024]{0:T(1024)}, u32[]{:S(2)}) copy-start(f32[1024]{0:T(1024)} %param.18) | copy-start | bytes 12292
  101.0 1.0 copy-start.3
  102.0 1.4 copy-start.4
  146.3 3.2 %copy-start.1 = (bf16[1024,4096]{1,0:T(8,128)(2,1)}, bf16[1024,4096]{1,0:T(8,128)(2,1)S(1)}, u32[]{:S(2)}) copy-start(bf16[1024,4096]{1,0:T(8,128)(2,1)S(1)} %get-tuple-element.19.tally_ref) | copy-start | bytes 25165828
  149.5 2.0 copy-start.2
  151.5 1.2 copy-start.5
  193.9 3.9 %collective-permute-start.1 = (bf16[64,104,128]{2,1,0:T(8,128)(2,1)}, bf16[64,104,128]{2,1,0:T(8,128)(2,1)S(1)}, u32[]{:S(2)}, u32[]{:S(2)}) collective-permute-start(bf16[64,104,128]{2,1,0:T(8,128)(2,1)} %bitcast.45), channel_id=1, source_target_pairs={{0,16},{16,0},{1,17},{17,1},{2,18},{18,2},{3,19},{19,3},{4,20},{20... | collective-permute-start | bytes 5111816 | tf_op jit(solution)/shard_map/ppermute | solution.py:370
  258.7 6.8 %collective-permute-start.2 = (bf16[64,104,128]{2,1,0:T(8,128)(2,1)S(1)}, bf16[64,104,128]{2,1,0:T(8,128)(2,1)S(1)}, u32[]{:S(2)}, u32[]{:S(2)}) collective-permute-start(bf16[64,104,128]{2,1,0:T(8,128)(2,1)S(1)} %all_to_all.34), channel_id=1, source_target_pairs={{0,16},{16,0},{1,17},{17,1},{2,18},{18,2},{3,19},{19,3},{4,20},{20... | collective-permute-start | bytes 5111816 | tf_op jit(solution)/shard_map/ppermute | solution.py:375

commit v7 on v6

--- a/solution.py
+++ b/solution.py
@@ -29,6 +29,9 @@
     return lax.all_to_all(array, axes, split_axis=0, concat_axis=0, tiled=True)
 
 
+PITCH = BR + 4
+
+
 def stripe_copy(codes_ref, codes, sem, k):
     lanes = pl.ds(pl.multiple_of(k * 128, 128), 128)
     return pltpu.make_async_copy(codes_ref.at[:, lanes], codes.at[k], sem.at[k])
@@ -46,9 +49,11 @@
             scales[c * 128 : (c + 1) * 128, :] = jnp.broadcast_to(columns[:, c : c + 1], (128, 128))
 
     stripe_copy(codes_ref, codes, sem, k).wait()
-    wide[...] = codes[k].astype(jnp.float32) * scales[...]
+    product = codes[k].astype(jnp.float32) * scales[...]
+    for b in range(NB_DEV):
+        wide[b * PITCH : b * PITCH + BR, :] = product[b * BR : (b + 1) * BR]
     for row in range(BR):
-        stripes_ref[row, 0] = wide[pl.ds(row, NB_DEV, stride=BR), :].astype(jnp.bfloat16)
+        stripes_ref[row, 0] = wide[pl.ds(row, NB_DEV, stride=PITCH), :].astype(jnp.bfloat16)
 
 
 def make_stripes(codes, scales):
@@ -64,7 +69,7 @@
         scratch_shapes=[
             pltpu.VMEM((6, NODE_DEV, 128), jnp.bfloat16),
             pltpu.VMEM((NODE_DEV, 128), jnp.float32),
-            pltpu.VMEM((NODE_DEV, 128), jnp.float32),
+            pltpu.VMEM((NB_DEV * PITCH, 128), jnp.float32),
             pltpu.SemaphoreType.DMA((6,)),
         ],
         compiler_params=pltpu.CompilerParams(vmem_limit_bytes=60 << 20),
@@ -304,8 +309,8 @@
         out_specs=[whole] * 3,
         out_shape=[
             jax.ShapeDtypeStruct((TGT, H), jnp.bfloat16),
-            jax.ShapeDtypeStruct((8, 8, RBP, 128), jnp.bfloat16),
-            jax.ShapeDtypeStruct((8, 8, RBP, 128), jnp.bfloat16),
+            pltpu.VMEM((8, 8, RBP, 128), jnp.bfloat16),
+            pltpu.VMEM((8, 8, RBP, 128), jnp.bfloat16),
         ],
         scratch_shapes=[
             pltpu.VMEM((MEAN_STEPS, PIECES, RQ, HALF), jnp.bfloat16),

time: 269 us -> 267 us (level)
  no operation moved by 1% of the time
where the time goes in v7:
time: 267 us
  blocking collectives  123 us (46%)
  Pallas kernels  88.4 us (33%)
  waiting for transfers between devices  26.4 us (10%)
  starting transfers between devices  12.1 us (5%)
  local copies, waits for them, and re-layouts  11.2 us (4%)
  other arithmetic  4.59 us (2%)
    all_to_all x4, blocking collectives, exchange(): return lax.all_to_all(array, axes, split_axis=0, concat_axis=0, tiled=True)  123 us
    pallas_call x1, Pallas kernels, side(): pl.pallas_call(side_kernel, grid=(TGT // SIDE,), in_specs=[pl.BlockSpec((...  42.7 us
    pallas_call x1, Pallas kernels, layer(): pl.pallas_call(layer_kernel, in_specs=[pl.BlockSpec(memory_space=pltpu.SM...  23.6 us
    all_to_all x1, waiting for transfers between devices, exchange(): return lax.all_to_all(array, axes, split_axis=0, concat_axis=0, tiled=True)  19.6 us
    pallas_call x1, Pallas kernels, gather(): pl.pallas_call(gather_kernel, grid_spec=pltpu.PrefetchScalarGridSpec(num_...  13.9 us
    unnamed x22, local copies, waits for them, and re-layouts  8.82 us
    all_to_all x1, starting transfers between devices, exchange(): return lax.all_to_all(array, axes, split_axis=0, concat_axis=0, tiled=True)  5.86 us
  transfers between devices with their start and end apart: 4, of which 3 were waited for; matrix products, arithmetic and copies ran while one was open for 2% of the time, Pallas kernels for 16%

profile of v7, /device:TPU:1, one launch (start us, length us, event | category | flops | bytes accessed | tf_op | source)
XLA Modules:
  0.0 266.7 jit_solution(7223613149117425215)
XLA Ops:
  0.6 1.3 fusion.23
  1.9 5.1 %make_stripes.1 = bf16[32,2,64,384]{3,2,1,0:T(8,128)(2,1)} custom-call(bf16[2048,768]{1,0:T(8,128)(2,1)} %codes_ref.3, f32[16,128]{1,0:T(8,128)} %get-tuple-element.29.scales_ref), custom_call_target="tpu_custom_call" | custom-call | tf_op jit(solution)/shard_map/make_stripes/pallas_call | solution.py:60
  7.1 51.6 %all_to_all.31 = bf16[64,64,384]{2,1,0:T(8,128)(2,1)S(1)} all-to-all(bf16[64,64,384]{2,1,0:T(8,128)(2,1)} %bitcast.43), channel_id=1, replica_groups=mesh['z'=4,'core'=2,'x'=4,'y'=4] {'z','x','y'}, dimensions={0} | all-to-all | bytes 6291456 | tf_op jit(solution)/shard_map/all_to_all | solution.py:29
  58.7 2.5 collective-permute-start
  61.3 13.2 %all_to_all.32 = s32[128,1,64]{2,1,0:T(1,128)S(1)} all-to-all(s32[128,1,64]{2,1,0:T(1,128)S(1)} %bitcast.44), channel_id=1, replica_groups=mesh['z'=4,'core'=2,'x'=4,'y'=4] {'z','core','x','y'}, dimensions={0} | all-to-all | bytes 65536 | tf_op jit(solution)/shard_map/all_to_all | solution.py:29
  74.5 13.9 %gather_rows.1 = bf16[128,64,384]{2,1,0:T(8,128)(2,1)} custom-call(s32[128,64]{1,0:T(8,128)S(1)} %bitcast.39, bf16[4096,384]{1,0:T(8,128)(2,1)S(1)} %bitcast.36, bf16[4096,384]{1,0:T(8,128)(2,1)} %collective-permute-done.sister_ref), custom_call_target="tpu_custom_call" | custom-call | tf_op jit(solution)/shard_map/gather_rows/pallas_call | solution.py:125
  88.4 5.9 %all-to-all-start.2 = ((bf16[128,64,384]{2,1,0:T(8,128)(2,1)}), bf16[128,64,384]{2,1,0:T(8,128)(2,1)}, u32[]{:S(2)}, u32[]{:S(2)}) async-start(bf16[128,64,384]{2,1,0:T(8,128)(2,1)} %gather_rows.1), calls=%async_computation.2 | async-start | bytes 12582912 | tf_op jit(solution)/shard_map/all_to_all | solution.py:29
  94.3 1.0 copy.27.target_ref
  95.3 1.0 copy.23
  96.3 2.5 fusion.4.column_ref
  98.8 1.0 copy-done.3
  99.9 1.4 copy-done.4
  101.3 42.7 %side.1 = (bf16[768,1024]{1,0:T(8,128)(2,1)S(1)}, f32[1024,1024]{1,0:T(8,128)S(1)}, bf16[1024,4096]{1,0:T(8,128)(2,1)S(1)}) custom-call(s32[1024,1]{1,0:T(8,128)S(1)} %copy-done.3, s32[1024,10]{1,0:T(8,128)S(1)} %fusion.4.column_ref, bf16[2048,768]{1,0:T(8,128)(2,1)S(1)} %copy-done, f32[1,2048]{1,0:T(1,128)S(1)} %bitcast.40, ...), custom_call_target="tpu_custom_call" | custom-call | tf_op jit(solution)/shard_map/side/pallas_call | solution.py:179
  144.0 3.2 %copy-done.1 = bf16[1024,4096]{1,0:T(8,128)(2,1)} copy-done((bf16[1024,4096]{1,0:T(8,128)(2,1)}, bf16[1024,4096]{1,0:T(8,128)(2,1)S(1)}, u32[]{:S(2)}) %copy-start.1) | copy-done | bytes 8388632
  147.2 2.0 copy-done.2
  149.2 1.1 copy-done.5
  150.3 19.6 %all-to-all-done.2.got_ref = bf16[128,64,384]{2,1,0:T(8,128)(2,1)} async-done(((bf16[128,64,384]{2,1,0:T(8,128)(2,1)}), bf16[128,64,384]{2,1,0:T(8,128)(2,1)}, u32[]{:S(2)}, u32[]{:S(2)}) %all-to-all-start.2) | async-done | bytes 6291488 | tf_op jit(solution)/shard_map/all_to_all | solution.py:29
  169.9 23.6 %layer.1 = (bf16[1024,1024]{1,0:T(8,128)(2,1)}, bf16[8,8,104,128]{3,2,1,0:T(8,128)(2,1)S(1)}, bf16[8,8,104,128]{3,2,1,0:T(8,128)(2,1)S(1)}) custom-call(s32[1]{0:T(128)} %bitcast.core_ref, bf16[128,64,384]{2,1,0:T(8,128)(2,1)} %all-to-all-done.2.got_ref, bf16[1024,4096]{1,0:T(8,128)(2,1)} %copy-done.1, f32[1024,1024]{1,0:T(8,128)} %copy-done.2, ...), custom_call_target="tpu_custom_call" | custom-call | tf_op jit(solution)/shard_map/layer/pallas_call | solution.py:306
  193.7 3.5 %collective-permute-done.1 = bf16[64,104,128]{2,1,0:T(8,128)(2,1)S(1)} collective-permute-done((bf16[64,104,128]{2,1,0:T(8,128)(2,1)S(1)}, bf16[64,104,128]{2,1,0:T(8,128)(2,1)S(1)}, u32[]{:S(2)}, u32[]{:S(2)}) %collective-permute-start.1) | collective-permute-done | bytes 1703968 | tf_op jit(solution)/shard_map/ppermute | solution.py:375
  197.7 30.1 %all_to_all.33 = bf16[64,104,128]{2,1,0:T(8,128)(2,1)S(1)} all-to-all(bf16[64,104,128]{2,1,0:T(8,128)(2,1)S(1)} %fusion), channel_id=1, replica_groups=mesh['z'=4,'core'=2,'x'=4,'y'=4] {'z','x','y'}, dimensions={0} | all-to-all | bytes 3407872 | tf_op jit(solution)/shard_map/all_to_all | solution.py:29
  228.3 28.5 %all_to_all.34 = bf16[64,104,128]{2,1,0:T(8,128)(2,1)S(1)} all-to-all(bf16[64,104,128]{2,1,0:T(8,128)(2,1)S(1)} %broadcast_in_dim.27), channel_id=1, replica_groups=mesh['z'=4,'core'=2,'x'=4,'y'=4] {'z','x','y'}, dimensions={0} | all-to-all | bytes 3407872 | tf_op jit(solution)/shard_map/all_to_all | solution.py:29
  256.8 3.6 %collective-permute-start.2 = (bf16[64,104,128]{2,1,0:T(8,128)(2,1)S(1)}, bf16[64,104,128]{2,1,0:T(8,128)(2,1)S(1)}, u32[]{:S(2)}, u32[]{:S(2)}) collective-permute-start(bf16[64,104,128]{2,1,0:T(8,128)(2,1)S(1)} %all_to_all.34), channel_id=1, source_target_pairs={{0,16},{16,0},{1,17},{17,1},{2,18},{18,2},{3,19},{19,3},{4,20},{20... | collective-permute-start | bytes 5111816 | tf_op jit(solution)/shard_map/ppermute | solution.py:380
  260.3 3.2 %collective-permute-done.2 = bf16[64,104,128]{2,1,0:T(8,128)(2,1)S(1)} collective-permute-done((bf16[64,104,128]{2,1,0:T(8,128)(2,1)S(1)}, bf16[64,104,128]{2,1,0:T(8,128)(2,1)S(1)}, u32[]{:S(2)}, u32[]{:S(2)}) %collective-permute-start.2) | collective-permute-done | bytes 1703968 | tf_op jit(solution)/shard_map/ppermute | solution.py:380
  263.6 3.1 %unpack.1 = (f32[768,1024]{1,0:T(8,128)}, f32[768,1024]{1,0:T(8,128)}, f32[1,1024]{1,0:T(1,128)}) custom-call(s32[1]{0:T(128)} %bitcast.core_ref, bf16[8,8,104,128]{3,2,1,0:T(8,128)(2,1)S(1)} %bitcast.37, bf16[8,8,104,128]{3,2,1,0:T(8,128)(2,1)S(1)} %bitcast.38), custom_call_target="tpu_custom_call" | custom-call | tf_op jit(solution)/shard_map/unpack/pallas_call | solution.py:351
  (25 shorter events, 1.3 us)
Async XLA Ops:
  7.0 54.1 %copy-start.9 = (s32[128]{0:T(128)S(1)}, s32[128]{0:T(128)}, u32[]{:S(2)}) copy-start(s32[128]{0:T(128)} %param.14) | copy-start | bytes 1540
  7.1 54.1 %copy-start.10 = (s32[128,1]{0,1:T(1,128)S(1)}, s32[128,1]{0,1:T(1,128)}, u32[]{:S(2)}) copy-start(s32[128,1]{0,1:T(1,128)} %param.13) | copy-start | bytes 1540
  58.7 15.8 %collective-permute-start = (bf16[4096,384]{1,0:T(8,128)(2,1)S(1)}, bf16[4096,384]{1,0:T(8,128)(2,1)}, u32[]{:S(2)}, u32[]{:S(2)}) collective-permute-start(bf16[4096,384]{1,0:T(8,128)(2,1)S(1)} %bitcast.35), channel_id=1, source_target_pairs={{0,16},{16,0},{1,17},{17,1},{2,18},{18,2},{3,19},{19,3},{4,20},{20... | collective-permute-start | bytes 9437192 | tf_op jit(solution)/shard_map/ppermute | solution.py:402
  88.4 5.9 %copy-start.8 = (s32[1024]{0:T(1024)S(1)}, s32[1024]{0:T(1024)}, u32[]{:S(2)}) copy-start(s32[1024]{0:T(1024)} %param.12) | copy-start | bytes 12292
  88.4 6.9 %copy-start.7 = (s32[1024,10]{0,1:T(8,128)S(1)}, s32[1024,10]{0,1:T(8,128)}, u32[]{:S(2)}) copy-start(s32[1024,10]{0,1:T(8,128)} %param.15) | copy-start | bytes 122884
  88.4 10.4 %copy-start = (bf16[2048,768]{1,0:T(8,128)(2,1)S(1)}, bf16[2048,768]{1,0:T(8,128)(2,1)}, u32[]{:S(2)}) copy-start(bf16[2048,768]{1,0:T(8,128)(2,1)} %codes_ref.3) | copy-start | bytes 9437188
  88.4 81.5 %all-to-all-start.2 = ((bf16[128,64,384]{2,1,0:T(8,128)(2,1)}), bf16[128,64,384]{2,1,0:T(8,128)(2,1)}, u32[]{:S(2)}, u32[]{:S(2)}) async-start(bf16[128,64,384]{2,1,0:T(8,128)(2,1)} %gather_rows.1), calls=%async_computation.2 | async-start | bytes 12582912 | tf_op jit(solution)/shard_map/all_to_all | solution.py:29
  94.3 4.6 %copy-start.6 = (f32[1024]{0:T(1024)S(1)}, f32[1024]{0:T(1024)}, u32[]{:S(2)}) copy-start(f32[1024]{0:T(1024)} %param.18) | copy-start | bytes 12292
  98.8 1.0 copy-start.3
  99.9 1.4 copy-start.4
  144.0 3.2 %copy-start.1 = (bf16[1024,4096]{1,0:T(8,128)(2,1)}, bf16[1024,4096]{1,0:T(8,128)(2,1)S(1)}, u32[]{:S(2)}) copy-start(bf16[1024,4096]{1,0:T(8,128)(2,1)S(1)} %get-tuple-element.19.tally_ref) | copy-start | bytes 25165828
  147.2 2.0 copy-start.2
  149.2 1.1 copy-start.5
  193.5 3.7 %collective-permute-start.1 = (bf16[64,104,128]{2,1,0:T(8,128)(2,1)S(1)}, bf16[64,104,128]{2,1,0:T(8,128)(2,1)S(1)}, u32[]{:S(2)}, u32[]{:S(2)}) collective-permute-start(bf16[64,104,128]{2,1,0:T(8,128)(2,1)S(1)} %bitcast.42), channel_id=1, source_target_pairs={{0,16},{16,0},{1,17},{17,1},{2,18},{18,2},{3,19},{19,3},{4,20},{20... | collective-permute-start | bytes 5111816 | tf_op jit(solution)/shard_map/ppermute | solution.py:375
  256.8 6.8 %collective-permute-start.2 = (bf16[64,104,128]{2,1,0:T(8,128)(2,1)S(1)}, bf16[64,104,128]{2,1,0:T(8,128)(2,1)S(1)}, u32[]{:S(2)}, u32[]{:S(2)}) collective-permute-start(bf16[64,104,128]{2,1,0:T(8,128)(2,1)S(1)} %all_to_all.34), channel_id=1, source_target_pairs={{0,16},{16,0},{1,17},{17,1},{2,18},{18,2},{3,19},{19,3},{4,20},{20... | collective-permute-start | bytes 5111816 | tf_op jit(solution)/shard_map/ppermute | solution.py:380

commit v8 on v7

--- a/solution.py
+++ b/solution.py
@@ -211,7 +211,7 @@
 def layer_kernel(
     core_ref, got_ref, tally_ref, pre_ref, x_t_ref, weight_ref, cot_ref,
     hidden_ref, kept_ref, given_ref,
-    got, tally, pre_self, x_t, weight, cot, hidden, kept, given, acc, mean, mean_t, sem, out_sem,
+    got, tally, pre_self, x_t, weight, cot, hidden, acc, mean, mean_t, sem, out_sem,
 ):
     count = 0
 
@@ -277,26 +277,19 @@
         grad_neigh = jnp.dot(mean_t[...], delta, preferred_element_type=jnp.float32)
         tail = jnp.broadcast_to(bias_term, (RBP - RB, HB))
         for ref, value in (
-            (given, jnp.where(first, grad_neigh, grad_self)),
-            (kept, jnp.where(first, grad_self, grad_neigh)),
+            (given_ref, jnp.where(first, grad_neigh, grad_self)),
+            (kept_ref, jnp.where(first, grad_self, grad_neigh)),
         ):
             for c in range(HB // 128):
                 lanes = slice(c * 128, (c + 1) * 128)
                 for r in range(8):
-                    ref[n, r, c] = jnp.concatenate(
+                    ref[r, n * (HB // 128) + c] = jnp.concatenate(
                         [value[r * RB : (r + 1) * RB, lanes], tail[:, lanes]], axis=0
                     ).astype(jnp.bfloat16)
-        chunk = pl.ds(n * (HB // 128), HB // 128)
-        for e, (source, target) in enumerate(
-            (
-                (given.at[n], given_ref.at[:, chunk]),
-                (kept.at[n], kept_ref.at[:, chunk]),
-                (hidden.at[:, pl.ds(n * HB, HB)], hidden_ref.at[:, pl.ds(n * HB, HB)]),
-            )
-        ):
-            copy = pltpu.make_async_copy(source, target, out_sem.at[3 * n + e])
-            copy.start()
-            leaving.append(copy)
+        lanes = pl.ds(n * HB, HB)
+        copy = pltpu.make_async_copy(hidden.at[:, lanes], hidden_ref.at[:, lanes], out_sem.at[n])
+        copy.start()
+        leaving.append(copy)
     for copy in leaving:
         copy.wait()
 
@@ -306,7 +299,7 @@
     return pl.pallas_call(
         layer_kernel,
         in_specs=[pl.BlockSpec(memory_space=pltpu.SMEM)] + [whole] * 6,
-        out_specs=[whole] * 3,
+        out_specs=[whole] + [pl.BlockSpec(memory_space=pltpu.VMEM)] * 2,
         out_shape=[
             jax.ShapeDtypeStruct((TGT, H), jnp.bfloat16),
             pltpu.VMEM((8, 8, RBP, 128), jnp.bfloat16),
@@ -320,13 +313,11 @@
             pltpu.VMEM((F, H), jnp.bfloat16),
             pltpu.VMEM((TGT, H), jnp.bfloat16),
             pltpu.VMEM((TGT, H), jnp.bfloat16),
-            pltpu.VMEM((LATE, 8, HB // 128, RBP, 128), jnp.bfloat16),
-            pltpu.VMEM((LATE, 8, HB // 128, RBP, 128), jnp.bfloat16),
             pltpu.VMEM((TGT, F), jnp.float32),
             pltpu.VMEM((TGT, F), jnp.bfloat16),
             pltpu.VMEM((F, TGT), jnp.bfloat16),
             pltpu.SemaphoreType.DMA((2 * MEAN_STEPS + 4,)),
-            pltpu.SemaphoreType.DMA((3 * LATE,)),
+            pltpu.SemaphoreType.DMA((LATE,)),
         ],
         compiler_params=pltpu.CompilerParams(vmem_limit_bytes=58 << 20),
         name="layer",

time: 267 us -> 264 us (0.989)
  Pallas kernels: 88.4 us -> 85.7 us
    pallas_call x1, Pallas kernels: 23.6 us -> 20.7 us  [layer(): pl.pallas_call(layer_kernel, in_specs=[pl.BlockSpec(memory_space=pltpu.SM...]
where the time goes in v8:
time: 264 us
  blocking collectives  123 us (47%)
  Pallas kernels  85.7 us (32%)
  waiting for transfers between devices  26.2 us (10%)
  starting transfers between devices  12.1 us (5%)
  local copies, waits for them, and re-layouts  11.2 us (4%)
  other arithmetic  4.59 us (2%)
    all_to_all x4, blocking collectives, exchange(): return lax.all_to_all(array, axes, split_axis=0, concat_axis=0, tiled=True)  123 us
    pallas_call x1, Pallas kernels, side(): pl.pallas_call(side_kernel, grid=(TGT // SIDE,), in_specs=[pl.BlockSpec((...  42.9 us
    pallas_call x1, Pallas kernels, layer(): pl.pallas_call(layer_kernel, in_specs=[pl.BlockSpec(memory_space=pltpu.SM...  20.7 us
    all_to_all x1, waiting for transfers between devices, exchange(): return lax.all_to_all(array, axes, split_axis=0, concat_axis=0, tiled=True)  19.5 us
    pallas_call x1, Pallas kernels, gather(): pl.pallas_call(gather_kernel, grid_spec=pltpu.PrefetchScalarGridSpec(num_...  13.8 us
    unnamed x22, local copies, waits for them, and re-layouts  8.82 us
    all_to_all x1, starting transfers between devices, exchange(): return lax.all_to_all(array, axes, split_axis=0, concat_axis=0, tiled=True)  5.85 us
  transfers between devices with their start and end apart: 4, of which 3 were waited for; matrix products, arithmetic and copies ran while one was open for 2% of the time, Pallas kernels for 16%

profile of v8, /device:TPU:1, one launch (start us, length us, event | category | flops | bytes accessed | tf_op | source)
XLA Modules:
  0.0 263.9 jit_solution(3235938750530507928)
XLA Ops:
  0.6 1.3 fusion.23
  1.9 5.1 %make_stripes.1 = bf16[32,2,64,384]{3,2,1,0:T(8,128)(2,1)} custom-call(bf16[2048,768]{1,0:T(8,128)(2,1)} %codes_ref.3, f32[16,128]{1,0:T(8,128)} %get-tuple-element.29.scales_ref), custom_call_target="tpu_custom_call" | custom-call | tf_op jit(solution)/shard_map/make_stripes/pallas_call | solution.py:60
  7.1 51.6 %all_to_all.31 = bf16[64,64,384]{2,1,0:T(8,128)(2,1)S(1)} all-to-all(bf16[64,64,384]{2,1,0:T(8,128)(2,1)} %bitcast.43), channel_id=1, replica_groups=mesh['z'=4,'core'=2,'x'=4,'y'=4] {'z','x','y'}, dimensions={0} | all-to-all | bytes 6291456 | tf_op jit(solution)/shard_map/all_to_all | solution.py:29
  58.7 2.5 collective-permute-start
  61.3 13.2 %all_to_all.32 = s32[128,1,64]{2,1,0:T(1,128)S(1)} all-to-all(s32[128,1,64]{2,1,0:T(1,128)S(1)} %bitcast.44), channel_id=1, replica_groups=mesh['z'=4,'core'=2,'x'=4,'y'=4] {'z','core','x','y'}, dimensions={0} | all-to-all | bytes 65536 | tf_op jit(solution)/shard_map/all_to_all | solution.py:29
  74.5 13.8 %gather_rows.1 = bf16[128,64,384]{2,1,0:T(8,128)(2,1)} custom-call(s32[128,64]{1,0:T(8,128)S(1)} %bitcast.39, bf16[4096,384]{1,0:T(8,128)(2,1)S(1)} %bitcast.36, bf16[4096,384]{1,0:T(8,128)(2,1)} %collective-permute-done.sister_ref), custom_call_target="tpu_custom_call" | custom-call | tf_op jit(solution)/shard_map/gather_rows/pallas_call | solution.py:125
  88.4 5.9 %all-to-all-start.2 = ((bf16[128,64,384]{2,1,0:T(8,128)(2,1)}), bf16[128,64,384]{2,1,0:T(8,128)(2,1)}, u32[]{:S(2)}, u32[]{:S(2)}) async-start(bf16[128,64,384]{2,1,0:T(8,128)(2,1)} %gather_rows.1), calls=%async_computation.2 | async-start | bytes 12582912 | tf_op jit(solution)/shard_map/all_to_all | solution.py:29
  94.3 1.0 copy.27.target_ref
  95.3 1.0 copy.23
  96.3 2.5 fusion.4.column_ref
  98.8 1.0 copy-done.3
  99.9 1.4 copy-done.4
  101.3 42.9 %side.1 = (bf16[768,1024]{1,0:T(8,128)(2,1)S(1)}, f32[1024,1024]{1,0:T(8,128)S(1)}, bf16[1024,4096]{1,0:T(8,128)(2,1)S(1)}) custom-call(s32[1024,1]{1,0:T(8,128)S(1)} %copy-done.3, s32[1024,10]{1,0:T(8,128)S(1)} %fusion.4.column_ref, bf16[2048,768]{1,0:T(8,128)(2,1)S(1)} %copy-done, f32[1,2048]{1,0:T(1,128)S(1)} %bitcast.40, ...), custom_call_target="tpu_custom_call" | custom-call | tf_op jit(solution)/shard_map/side/pallas_call | solution.py:179
  144.1 3.2 %copy-done.1 = bf16[1024,4096]{1,0:T(8,128)(2,1)} copy-done((bf16[1024,4096]{1,0:T(8,128)(2,1)}, bf16[1024,4096]{1,0:T(8,128)(2,1)S(1)}, u32[]{:S(2)}) %copy-start.1) | copy-done | bytes 8388632
  147.4 2.0 copy-done.2
  149.3 1.1 copy-done.5
  150.5 19.5 %all-to-all-done.2.got_ref = bf16[128,64,384]{2,1,0:T(8,128)(2,1)} async-done(((bf16[128,64,384]{2,1,0:T(8,128)(2,1)}), bf16[128,64,384]{2,1,0:T(8,128)(2,1)}, u32[]{:S(2)}, u32[]{:S(2)}) %all-to-all-start.2) | async-done | bytes 6291488 | tf_op jit(solution)/shard_map/all_to_all | solution.py:29
  169.9 20.7 %layer.1 = (bf16[1024,1024]{1,0:T(8,128)(2,1)}, bf16[8,8,104,128]{3,2,1,0:T(8,128)(2,1)S(1)}, bf16[8,8,104,128]{3,2,1,0:T(8,128)(2,1)S(1)}) custom-call(s32[1]{0:T(128)} %bitcast.core_ref, bf16[128,64,384]{2,1,0:T(8,128)(2,1)} %all-to-all-done.2.got_ref, bf16[1024,4096]{1,0:T(8,128)(2,1)} %copy-done.1, f32[1024,1024]{1,0:T(8,128)} %copy-done.2, ...), custom_call_target="tpu_custom_call" | custom-call | tf_op jit(solution)/shard_map/layer/pallas_call | solution.py:299
  190.8 3.5 %collective-permute-done.1 = bf16[64,104,128]{2,1,0:T(8,128)(2,1)S(1)} collective-permute-done((bf16[64,104,128]{2,1,0:T(8,128)(2,1)S(1)}, bf16[64,104,128]{2,1,0:T(8,128)(2,1)S(1)}, u32[]{:S(2)}, u32[]{:S(2)}) %collective-permute-start.1) | collective-permute-done | bytes 1703968 | tf_op jit(solution)/shard_map/ppermute | solution.py:366
  194.9 30.1 %all_to_all.33 = bf16[64,104,128]{2,1,0:T(8,128)(2,1)S(1)} all-to-all(bf16[64,104,128]{2,1,0:T(8,128)(2,1)S(1)} %fusion), channel_id=1, replica_groups=mesh['z'=4,'core'=2,'x'=4,'y'=4] {'z','x','y'}, dimensions={0} | all-to-all | bytes 3407872 | tf_op jit(solution)/shard_map/all_to_all | solution.py:29
  225.4 28.5 %all_to_all.34 = bf16[64,104,128]{2,1,0:T(8,128)(2,1)S(1)} all-to-all(bf16[64,104,128]{2,1,0:T(8,128)(2,1)S(1)} %broadcast_in_dim.27), channel_id=1, replica_groups=mesh['z'=4,'core'=2,'x'=4,'y'=4] {'z','x','y'}, dimensions={0} | all-to-all | bytes 3407872 | tf_op jit(solution)/shard_map/all_to_all | solution.py:29
  253.9 3.6 %collective-permute-start.2 = (bf16[64,104,128]{2,1,0:T(8,128)(2,1)S(1)}, bf16[64,104,128]{2,1,0:T(8,128)(2,1)S(1)}, u32[]{:S(2)}, u32[]{:S(2)}) collective-permute-start(bf16[64,104,128]{2,1,0:T(8,128)(2,1)S(1)} %all_to_all.34), channel_id=1, source_target_pairs={{0,16},{16,0},{1,17},{17,1},{2,18},{18,2},{3,19},{19,3},{4,20},{20... | collective-permute-start | bytes 5111816 | tf_op jit(solution)/shard_map/ppermute | solution.py:371
  257.5 3.2 %collective-permute-done.2 = bf16[64,104,128]{2,1,0:T(8,128)(2,1)S(1)} collective-permute-done((bf16[64,104,128]{2,1,0:T(8,128)(2,1)S(1)}, bf16[64,104,128]{2,1,0:T(8,128)(2,1)S(1)}, u32[]{:S(2)}, u32[]{:S(2)}) %collective-permute-start.2) | collective-permute-done | bytes 1703968 | tf_op jit(solution)/shard_map/ppermute | solution.py:371
  260.7 3.1 %unpack.1 = (f32[768,1024]{1,0:T(8,128)}, f32[768,1024]{1,0:T(8,128)}, f32[1,1024]{1,0:T(1,128)}) custom-call(s32[1]{0:T(128)} %bitcast.core_ref, bf16[8,8,104,128]{3,2,1,0:T(8,128)(2,1)S(1)} %bitcast.37, bf16[8,8,104,128]{3,2,1,0:T(8,128)(2,1)S(1)} %bitcast.38), custom_call_target="tpu_custom_call" | custom-call | tf_op jit(solution)/shard_map/unpack/pallas_call | solution.py:342
  (25 shorter events, 1.3 us)
Async XLA Ops:
  7.0 54.1 %copy-start.9 = (s32[128]{0:T(128)S(1)}, s32[128]{0:T(128)}, u32[]{:S(2)}) copy-start(s32[128]{0:T(128)} %param.14) | copy-start | bytes 1540
  7.1 54.1 %copy-start.10 = (s32[128,1]{0,1:T(1,128)S(1)}, s32[128,1]{0,1:T(1,128)}, u32[]{:S(2)}) copy-start(s32[128,1]{0,1:T(1,128)} %param.13) | copy-start | bytes 1540
  58.7 15.8 %collective-permute-start = (bf16[4096,384]{1,0:T(8,128)(2,1)S(1)}, bf16[4096,384]{1,0:T(8,128)(2,1)}, u32[]{:S(2)}, u32[]{:S(2)}) collective-permute-start(bf16[4096,384]{1,0:T(8,128)(2,1)S(1)} %bitcast.35), channel_id=1, source_target_pairs={{0,16},{16,0},{1,17},{17,1},{2,18},{18,2},{3,19},{19,3},{4,20},{20... | collective-permute-start | bytes 9437192 | tf_op jit(solution)/shard_map/ppermute | solution.py:393
  88.4 5.9 %copy-start.8 = (s32[1024]{0:T(1024)S(1)}, s32[1024]{0:T(1024)}, u32[]{:S(2)}) copy-start(s32[1024]{0:T(1024)} %param.12) | copy-start | bytes 12292
  88.4 6.9 %copy-start.7 = (s32[1024,10]{0,1:T(8,128)S(1)}, s32[1024,10]{0,1:T(8,128)}, u32[]{:S(2)}) copy-start(s32[1024,10]{0,1:T(8,128)} %param.15) | copy-start | bytes 122884
  88.4 10.4 %copy-start = (bf16[2048,768]{1,0:T(8,128)(2,1)S(1)}, bf16[2048,768]{1,0:T(8,128)(2,1)}, u32[]{:S(2)}) copy-start(bf16[2048,768]{1,0:T(8,128)(2,1)} %codes_ref.3) | copy-start | bytes 9437188
  88.4 81.5 %all-to-all-start.2 = ((bf16[128,64,384]{2,1,0:T(8,128)(2,1)}), bf16[128,64,384]{2,1,0:T(8,128)(2,1)}, u32[]{:S(2)}, u32[]{:S(2)}) async-start(bf16[128,64,384]{2,1,0:T(8,128)(2,1)} %gather_rows.1), calls=%async_computation.2 | async-start | bytes 12582912 | tf_op jit(solution)/shard_map/all_to_all | solution.py:29
  94.3 4.6 %copy-start.6 = (f32[1024]{0:T(1024)S(1)}, f32[1024]{0:T(1024)}, u32[]{:S(2)}) copy-start(f32[1024]{0:T(1024)} %param.18) | copy-start | bytes 12292
  98.8 1.0 copy-start.3
  99.9 1.4 copy-start.4
  144.1 3.2 %copy-start.1 = (bf16[1024,4096]{1,0:T(8,128)(2,1)}, bf16[1024,4096]{1,0:T(8,128)(2,1)S(1)}, u32[]{:S(2)}) copy-start(bf16[1024,4096]{1,0:T(8,128)(2,1)S(1)} %get-tuple-element.19.tally_ref) | copy-start | bytes 25165828
  147.4 2.0 copy-start.2
  149.3 1.1 copy-start.5
  190.6 3.7 %collective-permute-start.1 = (bf16[64,104,128]{2,1,0:T(8,128)(2,1)S(1)}, bf16[64,104,128]{2,1,0:T(8,128)(2,1)S(1)}, u32[]{:S(2)}, u32[]{:S(2)}) collective-permute-start(bf16[64,104,128]{2,1,0:T(8,128)(2,1)S(1)} %bitcast.42), channel_id=1, source_target_pairs={{0,16},{16,0},{1,17},{17,1},{2,18},{18,2},{3,19},{19,3},{4,20},{20... | collective-permute-start | bytes 5111816 | tf_op jit(solution)/shard_map/ppermute | solution.py:366
  253.9 6.8 %collective-permute-start.2 = (bf16[64,104,128]{2,1,0:T(8,128)(2,1)S(1)}, bf16[64,104,128]{2,1,0:T(8,128)(2,1)S(1)}, u32[]{:S(2)}, u32[]{:S(2)}) collective-permute-start(bf16[64,104,128]{2,1,0:T(8,128)(2,1)S(1)} %all_to_all.34), channel_id=1, source_target_pairs={{0,16},{16,0},{1,17},{17,1},{2,18},{18,2},{3,19},{19,3},{4,20},{20... | collective-permute-start | bytes 5111816 | tf_op jit(solution)/shard_map/ppermute | solution.py:371

commit v9 on v8

--- a/solution.py
+++ b/solution.py
@@ -112,6 +112,8 @@
             for j in range(RQ):
                 at = pl.multiple_of(wanted_ref[first + 2 * step + u, j], SLOT)
                 picked[pl.ds(base + j * SLOT, SLOT), :] = table[pl.ds(at, SLOT), :]
+        for u in range(2):
+            base = u * RQ * SLOT
             for k in range(3):
                 out_ref[2 * step + u, :, k * 128 : (k + 1) * 128] = picked[
                     pl.ds(base + k, RQ, stride=SLOT), :

time: 264 us -> 263 us (level)
  no operation moved by 1% of the time
where the time goes in v9:
time: 263 us
  blocking collectives  123 us (47%)
  Pallas kernels  84.5 us (32%)
  waiting for transfers between devices  26.2 us (10%)
  starting transfers between devices  12.1 us (5%)
  local copies, waits for them, and re-layouts  11.2 us (4%)
  other arithmetic  4.59 us (2%)
    all_to_all x4, blocking collectives, exchange(): return lax.all_to_all(array, axes, split_axis=0, concat_axis=0, tiled=True)  123 us
    pallas_call x1, Pallas kernels, side(): pl.pallas_call(side_kernel, grid=(TGT // SIDE,), in_specs=[pl.BlockSpec((...  42.9 us
    pallas_call x1, Pallas kernels, layer(): pl.pallas_call(layer_kernel, in_specs=[pl.BlockSpec(memory_space=pltpu.SM...  20.7 us
    all_to_all x1, waiting for transfers between devices, exchange(): return lax.all_to_all(array, axes, split_axis=0, concat_axis=0, tiled=True)  19.5 us
    pallas_call x1, Pallas kernels, gather(): pl.pallas_call(gather_kernel, grid_spec=pltpu.PrefetchScalarGridSpec(num_...  12.6 us
    unnamed x22, local copies, waits for them, and re-layouts  8.82 us
    all_to_all x1, starting transfers between devices, exchange(): return lax.all_to_all(array, axes, split_axis=0, concat_axis=0, tiled=True)  5.85 us
  transfers between devices with their start and end apart: 4, of which 3 were waited for; matrix products, arithmetic and copies ran while one was open for 2% of the time, Pallas kernels for 16%

profile of v9, /device:TPU:1, one launch (start us, length us, event | category | flops | bytes accessed | tf_op | source)
XLA Modules:
  0.0 262.6 jit_solution(18190992854958639150)
XLA Ops:
  0.6 1.3 fusion.23
  1.9 5.1 %make_stripes.1 = bf16[32,2,64,384]{3,2,1,0:T(8,128)(2,1)} custom-call(bf16[2048,768]{1,0:T(8,128)(2,1)} %codes_ref.3, f32[16,128]{1,0:T(8,128)} %get-tuple-element.29.scales_ref), custom_call_target="tpu_custom_call" | custom-call | tf_op jit(solution)/shard_map/make_stripes/pallas_call | solution.py:60
  7.1 51.6 %all_to_all.31 = bf16[64,64,384]{2,1,0:T(8,128)(2,1)S(1)} all-to-all(bf16[64,64,384]{2,1,0:T(8,128)(2,1)} %bitcast.43), channel_id=1, replica_groups=mesh['z'=4,'core'=2,'x'=4,'y'=4] {'z','x','y'}, dimensions={0} | all-to-all | bytes 6291456 | tf_op jit(solution)/shard_map/all_to_all | solution.py:29
  58.7 2.5 collective-permute-start
  61.3 13.2 %all_to_all.32 = s32[128,1,64]{2,1,0:T(1,128)S(1)} all-to-all(s32[128,1,64]{2,1,0:T(1,128)S(1)} %bitcast.44), channel_id=1, replica_groups=mesh['z'=4,'core'=2,'x'=4,'y'=4] {'z','core','x','y'}, dimensions={0} | all-to-all | bytes 65536 | tf_op jit(solution)/shard_map/all_to_all | solution.py:29
  74.5 12.6 %gather_rows.1 = bf16[128,64,384]{2,1,0:T(8,128)(2,1)} custom-call(s32[128,64]{1,0:T(8,128)S(1)} %bitcast.39, bf16[4096,384]{1,0:T(8,128)(2,1)S(1)} %bitcast.36, bf16[4096,384]{1,0:T(8,128)(2,1)} %collective-permute-done.sister_ref), custom_call_target="tpu_custom_call" | custom-call | tf_op jit(solution)/shard_map/gather_rows/pallas_call | solution.py:127
  87.2 5.8 %all-to-all-start.2 = ((bf16[128,64,384]{2,1,0:T(8,128)(2,1)}), bf16[128,64,384]{2,1,0:T(8,128)(2,1)}, u32[]{:S(2)}, u32[]{:S(2)}) async-start(bf16[128,64,384]{2,1,0:T(8,128)(2,1)} %gather_rows.1), calls=%async_computation.2 | async-start | bytes 12582912 | tf_op jit(solution)/shard_map/all_to_all | solution.py:29
  93.1 1.0 copy.27.target_ref
  94.1 1.0 copy.23
  95.1 2.5 fusion.4.column_ref
  97.6 1.0 copy-done.3
  98.6 1.4 copy-done.4
  100.1 42.9 %side.1 = (bf16[768,1024]{1,0:T(8,128)(2,1)S(1)}, f32[1024,1024]{1,0:T(8,128)S(1)}, bf16[1024,4096]{1,0:T(8,128)(2,1)S(1)}) custom-call(s32[1024,1]{1,0:T(8,128)S(1)} %copy-done.3, s32[1024,10]{1,0:T(8,128)S(1)} %fusion.4.column_ref, bf16[2048,768]{1,0:T(8,128)(2,1)S(1)} %copy-done, f32[1,2048]{1,0:T(1,128)S(1)} %bitcast.40, ...), custom_call_target="tpu_custom_call" | custom-call | tf_op jit(solution)/shard_map/side/pallas_call | solution.py:181
  142.9 3.2 %copy-done.1 = bf16[1024,4096]{1,0:T(8,128)(2,1)} copy-done((bf16[1024,4096]{1,0:T(8,128)(2,1)}, bf16[1024,4096]{1,0:T(8,128)(2,1)S(1)}, u32[]{:S(2)}) %copy-start.1) | copy-done | bytes 8388632
  146.2 2.0 copy-done.2
  148.1 1.1 copy-done.5
  149.3 19.5 %all-to-all-done.2.got_ref = bf16[128,64,384]{2,1,0:T(8,128)(2,1)} async-done(((bf16[128,64,384]{2,1,0:T(8,128)(2,1)}), bf16[128,64,384]{2,1,0:T(8,128)(2,1)}, u32[]{:S(2)}, u32[]{:S(2)}) %all-to-all-start.2) | async-done | bytes 6291488 | tf_op jit(solution)/shard_map/all_to_all | solution.py:29
  168.7 20.7 %layer.1 = (bf16[1024,1024]{1,0:T(8,128)(2,1)}, bf16[8,8,104,128]{3,2,1,0:T(8,128)(2,1)S(1)}, bf16[8,8,104,128]{3,2,1,0:T(8,128)(2,1)S(1)}) custom-call(s32[1]{0:T(128)} %bitcast.core_ref, bf16[128,64,384]{2,1,0:T(8,128)(2,1)} %all-to-all-done.2.got_ref, bf16[1024,4096]{1,0:T(8,128)(2,1)} %copy-done.1, f32[1024,1024]{1,0:T(8,128)} %copy-done.2, ...), custom_call_target="tpu_custom_call" | custom-call | tf_op jit(solution)/shard_map/layer/pallas_call | solution.py:301
  189.6 3.5 %collective-permute-done.1 = bf16[64,104,128]{2,1,0:T(8,128)(2,1)S(1)} collective-permute-done((bf16[64,104,128]{2,1,0:T(8,128)(2,1)S(1)}, bf16[64,104,128]{2,1,0:T(8,128)(2,1)S(1)}, u32[]{:S(2)}, u32[]{:S(2)}) %collective-permute-start.1) | collective-permute-done | bytes 1703968 | tf_op jit(solution)/shard_map/ppermute | solution.py:368
  193.7 30.1 %all_to_all.33 = bf16[64,104,128]{2,1,0:T(8,128)(2,1)S(1)} all-to-all(bf16[64,104,128]{2,1,0:T(8,128)(2,1)S(1)} %fusion), channel_id=1, replica_groups=mesh['z'=4,'core'=2,'x'=4,'y'=4] {'z','x','y'}, dimensions={0} | all-to-all | bytes 3407872 | tf_op jit(solution)/shard_map/all_to_all | solution.py:29
  224.2 28.5 %all_to_all.34 = bf16[64,104,128]{2,1,0:T(8,128)(2,1)S(1)} all-to-all(bf16[64,104,128]{2,1,0:T(8,128)(2,1)S(1)} %broadcast_in_dim.27), channel_id=1, replica_groups=mesh['z'=4,'core'=2,'x'=4,'y'=4] {'z','x','y'}, dimensions={0} | all-to-all | bytes 3407872 | tf_op jit(solution)/shard_map/all_to_all | solution.py:29
  252.7 3.6 %collective-permute-start.2 = (bf16[64,104,128]{2,1,0:T(8,128)(2,1)S(1)}, bf16[64,104,128]{2,1,0:T(8,128)(2,1)S(1)}, u32[]{:S(2)}, u32[]{:S(2)}) collective-permute-start(bf16[64,104,128]{2,1,0:T(8,128)(2,1)S(1)} %all_to_all.34), channel_id=1, source_target_pairs={{0,16},{16,0},{1,17},{17,1},{2,18},{18,2},{3,19},{19,3},{4,20},{20... | collective-permute-start | bytes 5111816 | tf_op jit(solution)/shard_map/ppermute | solution.py:373
  256.3 3.2 %collective-permute-done.2 = bf16[64,104,128]{2,1,0:T(8,128)(2,1)S(1)} collective-permute-done((bf16[64,104,128]{2,1,0:T(8,128)(2,1)S(1)}, bf16[64,104,128]{2,1,0:T(8,128)(2,1)S(1)}, u32[]{:S(2)}, u32[]{:S(2)}) %collective-permute-start.2) | collective-permute-done | bytes 1703968 | tf_op jit(solution)/shard_map/ppermute | solution.py:373
  259.5 3.1 %unpack.1 = (f32[768,1024]{1,0:T(8,128)}, f32[768,1024]{1,0:T(8,128)}, f32[1,1024]{1,0:T(1,128)}) custom-call(s32[1]{0:T(128)} %bitcast.core_ref, bf16[8,8,104,128]{3,2,1,0:T(8,128)(2,1)S(1)} %bitcast.37, bf16[8,8,104,128]{3,2,1,0:T(8,128)(2,1)S(1)} %bitcast.38), custom_call_target="tpu_custom_call" | custom-call | tf_op jit(solution)/shard_map/unpack/pallas_call | solution.py:344
  (25 shorter events, 1.3 us)
Async XLA Ops:
  7.0 54.1 %copy-start.9 = (s32[128]{0:T(128)S(1)}, s32[128]{0:T(128)}, u32[]{:S(2)}) copy-start(s32[128]{0:T(128)} %param.14) | copy-start | bytes 1540
  7.1 54.1 %copy-start.10 = (s32[128,1]{0,1:T(1,128)S(1)}, s32[128,1]{0,1:T(1,128)}, u32[]{:S(2)}) copy-start(s32[128,1]{0,1:T(1,128)} %param.13) | copy-start | bytes 1540
  58.7 15.8 %collective-permute-start = (bf16[4096,384]{1,0:T(8,128)(2,1)S(1)}, bf16[4096,384]{1,0:T(8,128)(2,1)}, u32[]{:S(2)}, u32[]{:S(2)}) collective-permute-start(bf16[4096,384]{1,0:T(8,128)(2,1)S(1)} %bitcast.35), channel_id=1, source_target_pairs={{0,16},{16,0},{1,17},{17,1},{2,18},{18,2},{3,19},{19,3},{4,20},{20... | collective-permute-start | bytes 9437192 | tf_op jit(solution)/shard_map/ppermute | solution.py:395
  87.1 5.9 %copy-start.8 = (s32[1024]{0:T(1024)S(1)}, s32[1024]{0:T(1024)}, u32[]{:S(2)}) copy-start(s32[1024]{0:T(1024)} %param.12) | copy-start | bytes 12292
  87.2 6.9 %copy-start.7 = (s32[1024,10]{0,1:T(8,128)S(1)}, s32[1024,10]{0,1:T(8,128)}, u32[]{:S(2)}) copy-start(s32[1024,10]{0,1:T(8,128)} %param.15) | copy-start | bytes 122884
  87.2 10.4 %copy-start = (bf16[2048,768]{1,0:T(8,128)(2,1)S(1)}, bf16[2048,768]{1,0:T(8,128)(2,1)}, u32[]{:S(2)}) copy-start(bf16[2048,768]{1,0:T(8,128)(2,1)} %codes_ref.3) | copy-start | bytes 9437188
  87.2 81.5 %all-to-all-start.2 = ((bf16[128,64,384]{2,1,0:T(8,128)(2,1)}), bf16[128,64,384]{2,1,0:T(8,128)(2,1)}, u32[]{:S(2)}, u32[]{:S(2)}) async-start(bf16[128,64,384]{2,1,0:T(8,128)(2,1)} %gather_rows.1), calls=%async_computation.2 | async-start | bytes 12582912 | tf_op jit(solution)/shard_map/all_to_all | solution.py:29
  93.0 4.6 %copy-start.6 = (f32[1024]{0:T(1024)S(1)}, f32[1024]{0:T(1024)}, u32[]{:S(2)}) copy-start(f32[1024]{0:T(1024)} %param.18) | copy-start | bytes 12292
  97.6 1.0 copy-start.3
  98.6 1.4 copy-start.4
  142.9 3.2 %copy-start.1 = (bf16[1024,4096]{1,0:T(8,128)(2,1)}, bf16[1024,4096]{1,0:T(8,128)(2,1)S(1)}, u32[]{:S(2)}) copy-start(bf16[1024,4096]{1,0:T(8,128)(2,1)S(1)} %get-tuple-element.19.tally_ref) | copy-start | bytes 25165828
  146.1 2.0 copy-start.2
  148.1 1.1 copy-start.5
  189.4 3.7 %collective-permute-start.1 = (bf16[64,104,128]{2,1,0:T(8,128)(2,1)S(1)}, bf16[64,104,128]{2,1,0:T(8,128)(2,1)S(1)}, u32[]{:S(2)}, u32[]{:S(2)}) collective-permute-start(bf16[64,104,128]{2,1,0:T(8,128)(2,1)S(1)} %bitcast.42), channel_id=1, source_target_pairs={{0,16},{16,0},{1,17},{17,1},{2,18},{18,2},{3,19},{19,3},{4,20},{20... | collective-permute-start | bytes 5111816 | tf_op jit(solution)/shard_map/ppermute | solution.py:368
  252.7 6.8 %collective-permute-start.2 = (bf16[64,104,128]{2,1,0:T(8,128)(2,1)S(1)}, bf16[64,104,128]{2,1,0:T(8,128)(2,1)S(1)}, u32[]{:S(2)}, u32[]{:S(2)}) collective-permute-start(bf16[64,104,128]{2,1,0:T(8,128)(2,1)S(1)} %all_to_all.34), channel_id=1, source_target_pairs={{0,16},{16,0},{1,17},{17,1},{2,18},{18,2},{3,19},{19,3},{4,20},{20... | collective-permute-start | bytes 5111816 | tf_op jit(solution)/shard_map/ppermute | solution.py:373

commit v10 on v9

--- a/solution.py
+++ b/solution.py
@@ -254,7 +254,7 @@
         elif n < MEAN_STEPS - 1:
             acc[...] += part
         else:
-            value = ((acc[...] + part) / K).astype(jnp.bfloat16)
+            value = ((acc[...] + part) * (1.0 / K)).astype(jnp.bfloat16)
             mean[...] = value
             mean_t[...] = value.T
     for copy in late:
@@ -267,11 +267,11 @@
             mean[...], weight[:, block], preferred_element_type=jnp.float32
         )
         square = pre * pre
-        tangent = jnp.tanh(0.7978845608 * (pre + 0.044715 * pre * square))
-        rest = 1.0 + tangent
-        hidden[:, block] = (0.5 * pre * rest).astype(jnp.bfloat16)
-        slope = 0.5 * rest + 0.5 * pre * (1.0 - tangent * tangent) * 0.7978845608 * (
-            1.0 + 3.0 * 0.044715 * square
+        tangent = jnp.tanh(pre * (0.7978845608 + (0.7978845608 * 0.044715) * square))
+        rest = 0.5 + 0.5 * tangent
+        hidden[:, block] = (pre * rest).astype(jnp.bfloat16)
+        slope = rest + pre * (1.0 - tangent * tangent) * (
+            0.5 * 0.7978845608 + (1.5 * 0.7978845608 * 0.044715) * square
         )
         delta = (cot[:, block].astype(jnp.float32) * slope).astype(jnp.bfloat16)
         bias_term = jnp.sum(delta.astype(jnp.float32), axis=0, keepdims=True)

time: 263 us -> 263 us (level)
  no operation moved by 1% of the time
where the time goes in v10:
time: 263 us; the launch traced here: 262 us
  blocking collectives  123 us (47%)
  Pallas kernels  84 us (32%)
  waiting for transfers between devices  26.2 us (10%)
  starting transfers between devices  12.1 us (5%)
  local copies, waits for them, and re-layouts  11.2 us (4%)
  other arithmetic  4.59 us (2%)
    all_to_all x4, blocking collectives, exchange(): return lax.all_to_all(array, axes, split_axis=0, concat_axis=0, tiled=True)  123 us
    pallas_call x1, Pallas kernels, side(): pl.pallas_call(side_kernel, grid=(TGT // SIDE,), in_specs=[pl.BlockSpec((...  42.9 us
    pallas_call x1, Pallas kernels, layer(): pl.pallas_call(layer_kernel, in_specs=[pl.BlockSpec(memory_space=pltpu.SM...  20.3 us
    all_to_all x1, waiting for transfers between devices, exchange(): return lax.all_to_all(array, axes, split_axis=0, concat_axis=0, tiled=True)  19.5 us
    pallas_call x1, Pallas kernels, gather(): pl.pallas_call(gather_kernel, grid_spec=pltpu.PrefetchScalarGridSpec(num_...  12.6 us
    unnamed x22, local copies, waits for them, and re-layouts  8.82 us
    all_to_all x1, starting transfers between devices, exchange(): return lax.all_to_all(array, axes, split_axis=0, concat_axis=0, tiled=True)  5.85 us
  transfers between devices with their start and end apart: 4, of which 3 were waited for; matrix products, arithmetic and copies ran while one was open for 2% of the time, Pallas kernels for 16%

profile of v10, /device:TPU:1, one launch (start us, length us, event | category | flops | bytes accessed | tf_op | source)
XLA Modules:
  0.0 262.2 jit_solution(8955396981058005440)
XLA Ops:
  0.6 1.3 fusion.23
  1.9 5.1 %make_stripes.1 = bf16[32,2,64,384]{3,2,1,0:T(8,128)(2,1)} custom-call(bf16[2048,768]{1,0:T(8,128)(2,1)} %codes_ref.3, f32[16,128]{1,0:T(8,128)} %get-tuple-element.29.scales_ref), custom_call_target="tpu_custom_call" | custom-call | tf_op jit(solution)/shard_map/make_stripes/pallas_call | solution.py:60
  7.1 51.6 %all_to_all.31 = bf16[64,64,384]{2,1,0:T(8,128)(2,1)S(1)} all-to-all(bf16[64,64,384]{2,1,0:T(8,128)(2,1)} %bitcast.43), channel_id=1, replica_groups=mesh['z'=4,'core'=2,'x'=4,'y'=4] {'z','x','y'}, dimensions={0} | all-to-all | bytes 6291456 | tf_op jit(solution)/shard_map/all_to_all | solution.py:29
  58.7 2.5 collective-permute-start
  61.3 13.2 %all_to_all.32 = s32[128,1,64]{2,1,0:T(1,128)S(1)} all-to-all(s32[128,1,64]{2,1,0:T(1,128)S(1)} %bitcast.44), channel_id=1, replica_groups=mesh['z'=4,'core'=2,'x'=4,'y'=4] {'z','core','x','y'}, dimensions={0} | all-to-all | bytes 65536 | tf_op jit(solution)/shard_map/all_to_all | solution.py:29
  74.5 12.6 %gather_rows.1 = bf16[128,64,384]{2,1,0:T(8,128)(2,1)} custom-call(s32[128,64]{1,0:T(8,128)S(1)} %bitcast.39, bf16[4096,384]{1,0:T(8,128)(2,1)S(1)} %bitcast.36, bf16[4096,384]{1,0:T(8,128)(2,1)} %collective-permute-done.sister_ref), custom_call_target="tpu_custom_call" | custom-call | tf_op jit(solution)/shard_map/gather_rows/pallas_call | solution.py:127
  87.2 5.8 %all-to-all-start.2 = ((bf16[128,64,384]{2,1,0:T(8,128)(2,1)}), bf16[128,64,384]{2,1,0:T(8,128)(2,1)}, u32[]{:S(2)}, u32[]{:S(2)}) async-start(bf16[128,64,384]{2,1,0:T(8,128)(2,1)} %gather_rows.1), calls=%async_computation.2 | async-start | bytes 12582912 | tf_op jit(solution)/shard_map/all_to_all | solution.py:29
  93.1 1.0 copy.27.target_ref
  94.1 1.0 copy.23
  95.1 2.5 fusion.4.column_ref
  97.6 1.0 copy-done.3
  98.6 1.4 copy-done.4
  100.1 42.9 %side.1 = (bf16[768,1024]{1,0:T(8,128)(2,1)S(1)}, f32[1024,1024]{1,0:T(8,128)S(1)}, bf16[1024,4096]{1,0:T(8,128)(2,1)S(1)}) custom-call(s32[1024,1]{1,0:T(8,128)S(1)} %copy-done.3, s32[1024,10]{1,0:T(8,128)S(1)} %fusion.4.column_ref, bf16[2048,768]{1,0:T(8,128)(2,1)S(1)} %copy-done, f32[1,2048]{1,0:T(1,128)S(1)} %bitcast.40, ...), custom_call_target="tpu_custom_call" | custom-call | tf_op jit(solution)/shard_map/side/pallas_call | solution.py:181
  142.9 3.2 %copy-done.1 = bf16[1024,4096]{1,0:T(8,128)(2,1)} copy-done((bf16[1024,4096]{1,0:T(8,128)(2,1)}, bf16[1024,4096]{1,0:T(8,128)(2,1)S(1)}, u32[]{:S(2)}) %copy-start.1) | copy-done | bytes 8388632
  146.2 2.0 copy-done.2
  148.1 1.1 copy-done.5
  149.3 19.5 %all-to-all-done.2.got_ref = bf16[128,64,384]{2,1,0:T(8,128)(2,1)} async-done(((bf16[128,64,384]{2,1,0:T(8,128)(2,1)}), bf16[128,64,384]{2,1,0:T(8,128)(2,1)}, u32[]{:S(2)}, u32[]{:S(2)}) %all-to-all-start.2) | async-done | bytes 6291488 | tf_op jit(solution)/shard_map/all_to_all | solution.py:29
  168.7 20.3 %layer.1 = (bf16[1024,1024]{1,0:T(8,128)(2,1)}, bf16[8,8,104,128]{3,2,1,0:T(8,128)(2,1)S(1)}, bf16[8,8,104,128]{3,2,1,0:T(8,128)(2,1)S(1)}) custom-call(s32[1]{0:T(128)} %bitcast.core_ref, bf16[128,64,384]{2,1,0:T(8,128)(2,1)} %all-to-all-done.2.got_ref, bf16[1024,4096]{1,0:T(8,128)(2,1)} %copy-done.1, f32[1024,1024]{1,0:T(8,128)} %copy-done.2, ...), custom_call_target="tpu_custom_call" | custom-call | tf_op jit(solution)/shard_map/layer/pallas_call | solution.py:301
  189.2 3.5 %collective-permute-done.1 = bf16[64,104,128]{2,1,0:T(8,128)(2,1)S(1)} collective-permute-done((bf16[64,104,128]{2,1,0:T(8,128)(2,1)S(1)}, bf16[64,104,128]{2,1,0:T(8,128)(2,1)S(1)}, u32[]{:S(2)}, u32[]{:S(2)}) %collective-permute-start.1) | collective-permute-done | bytes 1703968 | tf_op jit(solution)/shard_map/ppermute | solution.py:368
  193.2 30.1 %all_to_all.33 = bf16[64,104,128]{2,1,0:T(8,128)(2,1)S(1)} all-to-all(bf16[64,104,128]{2,1,0:T(8,128)(2,1)S(1)} %fusion), channel_id=1, replica_groups=mesh['z'=4,'core'=2,'x'=4,'y'=4] {'z','x','y'}, dimensions={0} | all-to-all | bytes 3407872 | tf_op jit(solution)/shard_map/all_to_all | solution.py:29
  223.8 28.5 %all_to_all.34 = bf16[64,104,128]{2,1,0:T(8,128)(2,1)S(1)} all-to-all(bf16[64,104,128]{2,1,0:T(8,128)(2,1)S(1)} %broadcast_in_dim.27), channel_id=1, replica_groups=mesh['z'=4,'core'=2,'x'=4,'y'=4] {'z','x','y'}, dimensions={0} | all-to-all | bytes 3407872 | tf_op jit(solution)/shard_map/all_to_all | solution.py:29
  252.3 3.6 %collective-permute-start.2 = (bf16[64,104,128]{2,1,0:T(8,128)(2,1)S(1)}, bf16[64,104,128]{2,1,0:T(8,128)(2,1)S(1)}, u32[]{:S(2)}, u32[]{:S(2)}) collective-permute-start(bf16[64,104,128]{2,1,0:T(8,128)(2,1)S(1)} %all_to_all.34), channel_id=1, source_target_pairs={{0,16},{16,0},{1,17},{17,1},{2,18},{18,2},{3,19},{19,3},{4,20},{20... | collective-permute-start | bytes 5111816 | tf_op jit(solution)/shard_map/ppermute | solution.py:373
  255.8 3.2 %collective-permute-done.2 = bf16[64,104,128]{2,1,0:T(8,128)(2,1)S(1)} collective-permute-done((bf16[64,104,128]{2,1,0:T(8,128)(2,1)S(1)}, bf16[64,104,128]{2,1,0:T(8,128)(2,1)S(1)}, u32[]{:S(2)}, u32[]{:S(2)}) %collective-permute-start.2) | collective-permute-done | bytes 1703968 | tf_op jit(solution)/shard_map/ppermute | solution.py:373
  259.1 3.1 %unpack.1 = (f32[768,1024]{1,0:T(8,128)}, f32[768,1024]{1,0:T(8,128)}, f32[1,1024]{1,0:T(1,128)}) custom-call(s32[1]{0:T(128)} %bitcast.core_ref, bf16[8,8,104,128]{3,2,1,0:T(8,128)(2,1)S(1)} %bitcast.37, bf16[8,8,104,128]{3,2,1,0:T(8,128)(2,1)S(1)} %bitcast.38), custom_call_target="tpu_custom_call" | custom-call | tf_op jit(solution)/shard_map/unpack/pallas_call | solution.py:344
  (25 shorter events, 1.3 us)
Async XLA Ops:
  7.0 54.1 %copy-start.9 = (s32[128]{0:T(128)S(1)}, s32[128]{0:T(128)}, u32[]{:S(2)}) copy-start(s32[128]{0:T(128)} %param.14) | copy-start | bytes 1540
  7.1 54.1 %copy-start.10 = (s32[128,1]{0,1:T(1,128)S(1)}, s32[128,1]{0,1:T(1,128)}, u32[]{:S(2)}) copy-start(s32[128,1]{0,1:T(1,128)} %param.13) | copy-start | bytes 1540
  58.7 15.8 %collective-permute-start = (bf16[4096,384]{1,0:T(8,128)(2,1)S(1)}, bf16[4096,384]{1,0:T(8,128)(2,1)}, u32[]{:S(2)}, u32[]{:S(2)}) collective-permute-start(bf16[4096,384]{1,0:T(8,128)(2,1)S(1)} %bitcast.35), channel_id=1, source_target_pairs={{0,16},{16,0},{1,17},{17,1},{2,18},{18,2},{3,19},{19,3},{4,20},{20... | collective-permute-start | bytes 9437192 | tf_op jit(solution)/shard_map/ppermute | solution.py:395
  87.1 5.9 %copy-start.8 = (s32[1024]{0:T(1024)S(1)}, s32[1024]{0:T(1024)}, u32[]{:S(2)}) copy-start(s32[1024]{0:T(1024)} %param.12) | copy-start | bytes 12292
  87.2 6.9 %copy-start.7 = (s32[1024,10]{0,1:T(8,128)S(1)}, s32[1024,10]{0,1:T(8,128)}, u32[]{:S(2)}) copy-start(s32[1024,10]{0,1:T(8,128)} %param.15) | copy-start | bytes 122884
  87.2 10.4 %copy-start = (bf16[2048,768]{1,0:T(8,128)(2,1)S(1)}, bf16[2048,768]{1,0:T(8,128)(2,1)}, u32[]{:S(2)}) copy-start(bf16[2048,768]{1,0:T(8,128)(2,1)} %codes_ref.3) | copy-start | bytes 9437188
  87.2 81.5 %all-to-all-start.2 = ((bf16[128,64,384]{2,1,0:T(8,128)(2,1)}), bf16[128,64,384]{2,1,0:T(8,128)(2,1)}, u32[]{:S(2)}, u32[]{:S(2)}) async-start(bf16[128,64,384]{2,1,0:T(8,128)(2,1)} %gather_rows.1), calls=%async_computation.2 | async-start | bytes 12582912 | tf_op jit(solution)/shard_map/all_to_all | solution.py:29
  93.0 4.6 %copy-start.6 = (f32[1024]{0:T(1024)S(1)}, f32[1024]{0:T(1024)}, u32[]{:S(2)}) copy-start(f32[1024]{0:T(1024)} %param.18) | copy-start | bytes 12292
  97.6 1.0 copy-start.3
  98.6 1.4 copy-start.4
  142.9 3.2 %copy-start.1 = (bf16[1024,4096]{1,0:T(8,128)(2,1)}, bf16[1024,4096]{1,0:T(8,128)(2,1)S(1)}, u32[]{:S(2)}) copy-start(bf16[1024,4096]{1,0:T(8,128)(2,1)S(1)} %get-tuple-element.19.tally_ref) | copy-start | bytes 25165828
  146.1 2.0 copy-start.2
  148.1 1.1 copy-start.5
  189.0 3.7 %collective-permute-start.1 = (bf16[64,104,128]{2,1,0:T(8,128)(2,1)S(1)}, bf16[64,104,128]{2,1,0:T(8,128)(2,1)S(1)}, u32[]{:S(2)}, u32[]{:S(2)}) collective-permute-start(bf16[64,104,128]{2,1,0:T(8,128)(2,1)S(1)} %bitcast.42), channel_id=1, source_target_pairs={{0,16},{16,0},{1,17},{17,1},{2,18},{18,2},{3,19},{19,3},{4,20},{20... | collective-permute-start | bytes 5111816 | tf_op jit(solution)/shard_map/ppermute | solution.py:368
  252.3 6.8 %collective-permute-start.2 = (bf16[64,104,128]{2,1,0:T(8,128)(2,1)S(1)}, bf16[64,104,128]{2,1,0:T(8,128)(2,1)S(1)}, u32[]{:S(2)}, u32[]{:S(2)}) collective-permute-start(bf16[64,104,128]{2,1,0:T(8,128)(2,1)S(1)} %all_to_all.34), channel_id=1, source_target_pairs={{0,16},{16,0},{1,17},{17,1},{2,18},{18,2},{3,19},{19,3},{4,20},{20... | collective-permute-start | bytes 5111816 | tf_op jit(solution)/shard_map/ppermute | solution.py:373
